TPU v7x, 128 devices: a whole 4x4x4 slice. The times are simulated.
128 devices in a mesh: tm: 8 (over x, core), space: 16 (over z, y).
Axes of the slice: x: 4, y: 4, z: 4, core: 2. Of those that a mesh axis runs over, the one named last changes fastest.
Arguments:
- thermal_reading: bfloat16 [32, 1440, 2048], P(None, 'space', 'tm'), may hold values from -140 to 140
- moisture_content: bfloat16 [32, 1440, 2048], P(None, 'space', 'tm'), may hold values from -160 to 160
- gram_eigenvector_columns: float32 [2048, 64], replicated, may hold values from -0.125 to 0.125
- marine_indicator: int32 [32, 1440], P('tm', 'space'), may hold values 0 or 1
Outputs:
- correlation: float32 [32, 1440, 64], P('tm', 'space')
All inputs are finite; a program needn't handle non-finite values. No bound on the sum of `marine_indicator` on one device may be relied on, other than what follows from the above.
Results may differ from a plain program's by a relative error of at most 0.0007.
Values may be sent and summed in bfloat16 or wider, within the bound.
No kernel may reach another device: no remote copies, remote signals or barrier semaphores. Data moves between devices by JAX's collectives and lax.ppermute only.
A program may use at most 64 MiB of HBM per device.

v0:
```python
import math

import jax
import jax.numpy as jnp
from jax import lax
from jax.sharding import PartitionSpec as P


def zscore(values):
    values = values.astype(jnp.float32)
    average = jnp.mean(values, axis=-1, keepdims=True)
    centered = values - average
    return centered * lax.rsqrt(jnp.mean(centered * centered, axis=-1, keepdims=True) + 1e-05)


def standardize(fields):
    return (zscore(fields[0]), zscore(fields[1]).astype(jnp.bfloat16))


def area_root(first_row, row_count, total_lat):
    rows = (first_row + jnp.arange(row_count, dtype=jnp.int32)).astype(jnp.float32)
    latitude = ((rows + 0.5) / total_lat * 120.0 - 60.0) * (math.pi / 180.0)
    return jnp.sqrt(jnp.cos(latitude))


def standardize_pcs(pcs, pc_mean, pc_var):
    return ((pcs - pc_mean) * lax.rsqrt(pc_var + 1e-05)).astype(jnp.bfloat16)


def per_device(thermal_reading, moisture_content, gram_eigenvector_columns, marine_indicator):
    mask_float = marine_indicator.astype(jnp.float32)
    zt_float, zhum = standardize(
        (
            lax.all_to_all(thermal_reading, "tm", split_axis=0, concat_axis=2, tiled=True),
            lax.all_to_all(moisture_content, "tm", split_axis=0, concat_axis=2, tiled=True),
        )
    )
    lat_count = zt_float.shape[0]
    lon_count = zt_float.shape[1]
    hour_count = zt_float.shape[2]
    total_lat = lat_count * lax.axis_size("tm")
    radical_value = area_root(lax.axis_index("tm") * lat_count, lat_count, total_lat)
    scaling = radical_value[:, None] * mask_float
    ztemp = (zt_float * scaling[:, :, None]).astype(jnp.bfloat16)
    flat_temp = ztemp.reshape(lat_count * lon_count, hour_count)
    loadings = jnp.dot(
        flat_temp,
        gram_eigenvector_columns,
        precision=lax.Precision.HIGHEST,
        preferred_element_type=jnp.float32,
    )
    partial_value = lax.dot_general(
        flat_temp,
        loadings,
        (((0,), (0,)), ((), ())),
        precision=lax.Precision.HIGHEST,
        preferred_element_type=jnp.float32,
    )
    pcs = lax.psum(partial_value, ("tm", "space"))
    pc_mean = jnp.mean(pcs, axis=0, keepdims=True)
    pc_centered = pcs - pc_mean
    pcz = standardize_pcs(pcs, pc_mean, jnp.mean(pc_centered * pc_centered, axis=0, keepdims=True))
    flat_hum = zhum.reshape(lat_count * lon_count, hour_count)
    summed = jnp.dot(flat_hum, pcz, preferred_element_type=jnp.float32).reshape(
        lat_count, lon_count, pcz.shape[1]
    )
    factor = mask_float / hour_count
    return summed * factor[:, :, None]


def solution(mesh):
    in_specs = (P(None, "space", "tm"), P(None, "space", "tm"), P(), P("tm", "space"))
    out_specs = P("tm", "space", None)
    return jax.shard_map(
        per_device, mesh=mesh, in_specs=in_specs, out_specs=out_specs, check_vma=False
    )
```

profile of v0, /device:TPU:1, one launch (start us, length us, event | category | flops | bytes accessed | tf_op | source)
XLA Modules:
  0.0 211.8 jit_solution(1335140150090077958)
XLA Ops:
  6.5 0.0 copy-start
  6.5 0.0 copy-start.3
  6.5 3.4 %copy.55 = bf16[32,90,256]{2,1,0:T(8,128)(2,1)} copy(bf16[32,90,256]{2,0,1:T(8,128)(2,1)} %param.4) | data formatting | bytes 2949120 | tf_op args[0]
  10.0 5.8 %all-to-all-start.1 = ((bf16[32,90,256]{2,1,0:T(8,128)(2,1)}), bf16[32,90,256]{2,1,0:T(8,128)(2,1)S(1)}, u32[]{:S(2)}, u32[]{:S(2)}) async-start(bf16[32,90,256]{2,1,0:T(8,128)(2,1)} %copy.55), calls=%async_computation.1 | async-start | bytes 3145728 | tf_op jit(solution)/shard_map/all_to_all | solution.py:34
  15.8 0.0 copy-done.3
  15.8 0.1 convert_multiply_fusion
  15.9 0.1 mul.96
  16.0 3.4 %copy.48 = bf16[32,90,256]{2,1,0:T(8,128)(2,1)} copy(bf16[32,90,256]{2,0,1:T(8,128)(2,1)} %param.5) | data formatting | bytes 2949120 | tf_op args[1]
  19.3 17.1 %all-to-all-done.1 = bf16[32,90,256]{2,1,0:T(8,128)(2,1)S(1)} async-done(((bf16[32,90,256]{2,1,0:T(8,128)(2,1)}), bf16[32,90,256]{2,1,0:T(8,128)(2,1)S(1)}, u32[]{:S(2)}, u32[]{:S(2)}) %all-to-all-start.1) | async-done | bytes 1474592 | tf_op jit(solution)/shard_map/all_to_all | solution.py:34
  36.5 0.0 copy-start.2
  36.5 5.0 %all-to-all-start = ((bf16[32,90,256]{2,1,0:T(8,128)(2,1)}), bf16[32,90,256]{2,1,0:T(8,128)(2,1)}, u32[]{:S(2)}, u32[]{:S(2)}) async-start(bf16[32,90,256]{2,1,0:T(8,128)(2,1)} %copy.48), calls=%async_computation | async-start | bytes 3145728 | tf_op jit(solution)/shard_map/all_to_all | solution.py:35
  41.5 0.0 all-reduce.2.cloned.1.call-start
  41.5 0.0 copy-done.2
  41.5 2.7 %bitcast_reduce_fusion = (f32[4,90]{1,0:T(4,128)S(1)}, f32[8,4,90,256]{3,0,2,1:T(8,128)S(1)}) fusion(bf16[8,4,90,256]{3,2,1,0:T(8,128)(2,1)} %bitcast.31), kind=kLoop, calls=%fused_computation | loop fusion | flops 736920 | bytes 4425120 | tf_op jit(solution)/shard_map/reduce_sum | solution.py:11
  44.2 0.1 div.28
  44.3 2.0 fusion.1
  46.3 0.1 rsqrt.29
  46.4 1.3 copy.58
  47.7 0.6 multiply_convert_fusion
  48.3 0.0 copy-done
  48.3 1.3 fusion.12
  49.7 1.7 fusion.13
  51.4 0.0 all-reduce.2.cloned.1.call-update
  51.4 10.9 %all-to-all-done = bf16[32,90,256]{2,1,0:T(8,128)(2,1)} async-done(((bf16[32,90,256]{2,1,0:T(8,128)(2,1)}), bf16[32,90,256]{2,1,0:T(8,128)(2,1)}, u32[]{:S(2)}, u32[]{:S(2)}) %all-to-all-start) | async-done | bytes 1474592 | tf_op jit(solution)/shard_map/all_to_all | solution.py:35
  62.4 1.8 bitcast_convert_fusion
  64.2 2.1 %fusion.11 = (f32[4,90]{0,1:T(8,128)S(1)}, f32[4,90,8,256]{3,2,0,1:T(8,128)S(1)}) fusion(f32[8,4,90,256]{3,2,1,0:T(8,128)S(1)} %bitcast_convert_fusion), kind=kLoop, calls=%fused_computation.25 | loop fusion | flops 736920 | bytes 5899680 | tf_op jit(solution)/shard_map/reduce_sum | solution.py:11
  66.3 2.7 %reshape.97 = f32[4,90,2048]{2,0,1:T(4,128)} reshape(f32[4,90,8,256]{3,2,0,1:T(8,128)S(1)} %get-tuple-element.8) | data formatting | bytes 5898240 | tf_op jit(solution)/shard_map/convert_element_type | solution.py:10
  69.0 0.0 copy-start.1
  69.0 1.0 multiply_reduce_fusion
  70.1 0.8 copy-done.1
  70.9 0.8 multiply_convert_fusion.1
  71.7 127.4 %all-reduce.2.cloned.1.call-done = f32[2048,64]{0,1:T(8,128)} async-done(((f32[2048,64]{0,1:T(8,128)}), f32[2048,64]{0,1:T(8,128)}) %all-reduce.2.cloned.1.call-update) | async-done | bytes 524304 | tf_op jit(solution)/shard_map/psum | solution.py:59
  199.1 1.2 reduce_sum.58
  200.3 1.3 multiply_reduce_fusion.1
  201.6 3.4 %fusion.4 = f32[4,90,64]{1,2,0:T(8,128)} fusion(bf16[4,90,2048]{2,0,1:T(4,128)(2,1)S(1)} %multiply_convert_fusion.1, f32[2048,64]{0,1:T(8,128)} %all-reduce.2.cloned.1.call-done, f32[64]{0:T(128)S(1)} %add_rsqrt_fusion.2, f32[64]{0:T(128)S(1)} %broadcast_multiply_fusion.2, f32[4,90]{1,0:T(4,128)S(1)} %get-tuple-element.9), kind=kOutput, calls=%fused_computation.10 | convolution fusion | flops 94788096 | bytes 2092960 | tf_op jit(solution)/shard_map/dot_general | solution.py:64
  (7 shorter events, 0.1 us)
Async XLA Ops:
  6.5 41.8 %copy-start = (f32[2048,64]{0,1:T(8,128)S(1)}, f32[2048,64]{0,1:T(8,128)}, u32[]{:S(2)}) copy-start(f32[2048,64]{0,1:T(8,128)} %param.6) | copy-start | bytes 1572868
  6.5 9.3 %copy-start.3 = (s32[4,90]{1,0:T(4,128)S(1)}, s32[4,90]{1,0:T(4,128)}, u32[]{:S(2)}) copy-start(s32[4,90]{1,0:T(4,128)} %param.7) | copy-start | bytes 4324
  10.0 26.5 %all-to-all-start.1 = ((bf16[32,90,256]{2,1,0:T(8,128)(2,1)}), bf16[32,90,256]{2,1,0:T(8,128)(2,1)S(1)}, u32[]{:S(2)}, u32[]{:S(2)}) async-start(bf16[32,90,256]{2,1,0:T(8,128)(2,1)} %copy.55), calls=%async_computation.1 | async-start | bytes 3145728 | tf_op jit(solution)/shard_map/all_to_all | solution.py:34
  36.5 5.0 %copy-start.2 = (bf16[32,90,256]{2,1,0:T(8,128)(2,1)}, bf16[32,90,256]{2,1,0:T(8,128)(2,1)S(1)}, u32[]{:S(2)}) copy-start(bf16[32,90,256]{2,1,0:T(8,128)(2,1)S(1)} %all-to-all-done.1) | copy-start | bytes 4423684
  36.5 25.9 %all-to-all-start = ((bf16[32,90,256]{2,1,0:T(8,128)(2,1)}), bf16[32,90,256]{2,1,0:T(8,128)(2,1)}, u32[]{:S(2)}, u32[]{:S(2)}) async-start(bf16[32,90,256]{2,1,0:T(8,128)(2,1)} %copy.48), calls=%async_computation | async-start | bytes 3145728 | tf_op jit(solution)/shard_map/all_to_all | solution.py:35
  41.5 157.6 %all-reduce.2.cloned.1.call-start = ((), (), s32[]{:S(2)}) async-start(), calls=%async_computation.2 | async-start | bytes 1048576 | tf_op jit(solution)/shard_map/psum | solution.py:59
  69.0 1.9 copy-start.1
Sparse Core Ops, SparseCore 0:
  51.5 147.4 all-reduce.1
where the time goes:
time: 212 us
  waiting for transfers between devices  156 us (74%)
  other arithmetic  13.6 us (6%)
  between operations  13.5 us (6%)
  local copies, waits for them, and re-layouts  11.9 us (6%)
  starting transfers between devices  10.8 us (5%)
  matrix products  6.49 us (3%)
    psum x1, waiting for transfers between devices, per_device(): pcs = lax.psum(partial_value, ('tm', 'space'))  127 us
    all_to_all x1, waiting for transfers between devices, per_device(): lax.all_to_all(thermal_reading, 'tm', split_axis=0, concat_axis=2, tiled=...  17.1 us
    all_to_all x1, waiting for transfers between devices, per_device(): lax.all_to_all(moisture_content, 'tm', split_axis=0, concat_axis=2, tiled...  10.9 us
    unnamed x11, local copies, waits for them, and re-layouts  8.93 us
    all_to_all x1, starting transfers between devices, per_device(): lax.all_to_all(thermal_reading, 'tm', split_axis=0, concat_axis=2, tiled=...  5.8 us
    all_to_all x1, starting transfers between devices, per_device(): lax.all_to_all(moisture_content, 'tm', split_axis=0, concat_axis=2, tiled...  5.03 us
    reduce_sum x2, other arithmetic, zscore(): average = jnp.mean(values, axis=-1, keepdims=True)  4.8 us
  transfers between devices with their start and end apart: 3, of which 3 were waited for; matrix products, arithmetic and copies ran while one was open for 10% of the time, Pallas kernels for 0%

commit v1 on v0

v1 whole, which is shorter than its diff:
```python
import math

import jax
import jax.numpy as jnp
from jax import lax
from jax.sharding import PartitionSpec as P


def zscore(values):
    values = values.astype(jnp.float32)
    average = jnp.mean(values, axis=-1, keepdims=True)
    centered = values - average
    return centered * lax.rsqrt(jnp.mean(centered * centered, axis=-1, keepdims=True) + 1e-05)


def area_root(first_row, row_count, total_lat):
    rows = (first_row + jnp.arange(row_count, dtype=jnp.int32)).astype(jnp.float32)
    latitude = ((rows + 0.5) / total_lat * 120.0 - 60.0) * (math.pi / 180.0)
    return jnp.sqrt(jnp.cos(latitude))


BOTH = ("tm", "space")


def sum_over_devices(partial_t):
    modes, hours = partial_t.shape
    blocks = partial_t.reshape(modes // 8, 8, hours // 128, 128)
    blocks = blocks.transpose(0, 2, 1, 3).reshape(-1, 8, 128)
    got = lax.all_to_all(blocks, BOTH, 0, 0)
    mine = jnp.sum(got, axis=0, keepdims=True)
    every = lax.all_to_all(jnp.broadcast_to(mine, blocks.shape), BOTH, 0, 0)
    every = every.reshape(modes // 8, hours // 128, 8, 128).transpose(0, 2, 1, 3)
    return every.reshape(modes, hours)


def per_device(thermal_reading, moisture_content, gram_eigenvector_columns, marine_indicator):
    mask_float = marine_indicator.astype(jnp.float32)
    temp = lax.all_to_all(thermal_reading, "tm", split_axis=0, concat_axis=2, tiled=True)
    hum = lax.all_to_all(moisture_content, "tm", split_axis=0, concat_axis=2, tiled=True)
    zt_float = zscore(temp)
    zhum = zscore(hum).astype(jnp.bfloat16)
    lat_count, lon_count, hour_count = zt_float.shape
    total_lat = lat_count * lax.axis_size("tm")
    root = area_root(lax.axis_index("tm") * lat_count, lat_count, total_lat)
    scaling = root[:, None] * mask_float
    ztemp = (zt_float * scaling[:, :, None]).astype(jnp.bfloat16)
    flat_temp = ztemp.reshape(lat_count * lon_count, hour_count)
    loadings = jnp.dot(
        flat_temp,
        gram_eigenvector_columns,
        precision=lax.Precision.HIGHEST,
        preferred_element_type=jnp.float32,
    )
    partial_t = lax.dot_general(
        loadings,
        flat_temp,
        (((0,), (0,)), ((), ())),
        precision=lax.Precision.HIGHEST,
        preferred_element_type=jnp.float32,
    )
    pcs = sum_over_devices(partial_t)
    pc_centered = pcs - jnp.mean(pcs, axis=1, keepdims=True)
    pc_var = jnp.mean(pc_centered * pc_centered, axis=1, keepdims=True)
    pcz = (pc_centered * lax.rsqrt(pc_var + 1e-05)).astype(jnp.bfloat16)
    flat_hum = zhum.reshape(lat_count * lon_count, hour_count)
    summed = lax.dot_general(
        flat_hum, pcz, (((1,), (1,)), ((), ())), preferred_element_type=jnp.float32
    ).reshape(lat_count, lon_count, pcz.shape[0])
    factor = mask_float / hour_count
    return summed * factor[:, :, None]


def solution(mesh):
    in_specs = (P(None, "space", "tm"), P(None, "space", "tm"), P(), P("tm", "space"))
    out_specs = P("tm", "space", None)
    return jax.shard_map(
        per_device, mesh=mesh, in_specs=in_specs, out_specs=out_specs, check_vma=False
    )
```

time: 212 us -> 103 us (0.49)
  waiting for transfers between devices: 156 us -> 44.4 us
  between operations: 13.5 us -> 0.12 us
  starting transfers between devices: 10.8 us -> 23.8 us
    psum x1 -> x0, waiting for transfers between devices: 127 us -> none  [per_device(): pcs = lax.psum(partial_value, ('tm', 'space'))]
    all_to_all x0 -> x2, waiting for transfers between devices: none -> 16.2 us  [the longest x1 8.31 us: sum_over_devices(): every = lax.all_to_all(jnp.broadcast_to(mine, blocks.shape), BOTH, 0, 0)]
    all_to_all x0 -> x2, starting transfers between devices: none -> 13 us  [the longest x1 9 us: sum_over_devices(): got = lax.all_to_all(blocks, BOTH, 0, 0)]
    convert_element_type x2 -> x1, other arithmetic: 1.4 us -> 3.85 us  [per_device(): zhum = zscore(hum).astype(jnp.bfloat16)]
  transfers between devices with their start and end apart: 3 -> 4, of which waited for: 3 -> 4; matrix products, arithmetic and copies ran while one was open for 10% -> 25% of each run, Pallas kernels for 0% -> 0%
where the time goes in v1:
time: 103 us; the launch traced here: 102 us
  waiting for transfers between devices  44.4 us (43%)
  starting transfers between devices  23.8 us (23%)
  other arithmetic  15.3 us (15%)
  local copies, waits for them, and re-layouts  11.2 us (11%)
  matrix products  7.34 us (7%)
    all_to_all x1, waiting for transfers between devices, per_device(): lax.all_to_all(thermal_reading, 'tm', split_axis=0, concat_axis=2, tiled=...  17.1 us
    all_to_all x1, waiting for transfers between devices, per_device(): lax.all_to_all(moisture_content, 'tm', split_axis=0, concat_axis=2, tiled...  11.1 us
    all_to_all x1, starting transfers between devices, sum_over_devices(): got = lax.all_to_all(blocks, BOTH, 0, 0)  9 us
    all_to_all x1, waiting for transfers between devices, sum_over_devices(): every = lax.all_to_all(jnp.broadcast_to(mine, blocks.shape), BOTH, 0, 0)  8.31 us
    unnamed x11, local copies, waits for them, and re-layouts  8.11 us
    all_to_all x1, waiting for transfers between devices, sum_over_devices(): got = lax.all_to_all(blocks, BOTH, 0, 0)  7.87 us
    all_to_all x1, starting transfers between devices, per_device(): lax.all_to_all(thermal_reading, 'tm', split_axis=0, concat_axis=2, tiled=...  5.8 us
    all_to_all x1, starting transfers between devices, per_device(): lax.all_to_all(moisture_content, 'tm', split_axis=0, concat_axis=2, tiled...  5.03 us
  transfers between devices with their start and end apart: 4, of which 4 were waited for; matrix products, arithmetic and copies ran while one was open for 25% of the time, Pallas kernels for 0%

profile of v1, /device:TPU:1, one launch (start us, length us, event | category | flops | bytes accessed | tf_op | source)
XLA Modules:
  0.0 102.2 jit_solution(18046777964718367636)
XLA Ops:
  0.0 0.0 copy-start
  0.0 0.0 copy-start.3
  0.0 3.4 %copy.58 = bf16[32,90,256]{2,1,0:T(8,128)(2,1)} copy(bf16[32,90,256]{2,0,1:T(8,128)(2,1)} %param.4) | data formatting | bytes 2949120 | tf_op args[0]
  3.4 5.8 %all-to-all-start.1 = ((bf16[32,90,256]{2,1,0:T(8,128)(2,1)}), bf16[32,90,256]{2,1,0:T(8,128)(2,1)S(1)}, u32[]{:S(2)}, u32[]{:S(2)}) async-start(bf16[32,90,256]{2,1,0:T(8,128)(2,1)} %copy.58), calls=%async_computation.1 | async-start | bytes 3145728 | tf_op jit(solution)/shard_map/all_to_all | solution.py:38
  9.3 0.0 copy-done.3
  9.3 0.1 convert_multiply_fusion
  9.4 0.1 mul.103
  9.4 3.4 %copy.52 = bf16[32,90,256]{2,1,0:T(8,128)(2,1)} copy(bf16[32,90,256]{2,0,1:T(8,128)(2,1)} %param.5) | data formatting | bytes 2949120 | tf_op args[1]
  12.8 17.1 %all-to-all-done.1 = bf16[32,90,256]{2,1,0:T(8,128)(2,1)S(1)} async-done(((bf16[32,90,256]{2,1,0:T(8,128)(2,1)}), bf16[32,90,256]{2,1,0:T(8,128)(2,1)S(1)}, u32[]{:S(2)}, u32[]{:S(2)}) %all-to-all-start.1) | async-done | bytes 1474592 | tf_op jit(solution)/shard_map/all_to_all | solution.py:38
  29.9 0.0 copy-start.2
  29.9 5.0 %all-to-all-start = ((bf16[32,90,256]{2,1,0:T(8,128)(2,1)}), bf16[32,90,256]{2,1,0:T(8,128)(2,1)}, u32[]{:S(2)}, u32[]{:S(2)}) async-start(bf16[32,90,256]{2,1,0:T(8,128)(2,1)} %copy.52), calls=%async_computation | async-start | bytes 3145728 | tf_op jit(solution)/shard_map/all_to_all | solution.py:39
  35.0 0.0 copy-done.2
  35.0 2.7 %bitcast_reduce_fusion = (f32[4,90]{1,0:T(4,128)S(1)}, f32[8,4,90,256]{3,0,2,1:T(8,128)S(1)}) fusion(bf16[8,4,90,256]{3,2,1,0:T(8,128)(2,1)} %bitcast.62), kind=kLoop, calls=%fused_computation | loop fusion | flops 736920 | bytes 4425120 | tf_op jit(solution)/shard_map/reduce_sum | solution.py:11
  37.6 0.1 div.28
  37.7 2.0 %fusion.1 = f32[4,90]{1,0:T(4,128)S(1)} fusion(f32[8,4,90,256]{3,0,2,1:T(8,128)S(1)} %get-tuple-element.6, f32[4,90]{1,0:T(4,128)S(1)} %broadcast_multiply_fusion.2), kind=kLoop, calls=%fused_computation.3 | loop fusion | flops 2211480 | bytes 2952000 | tf_op jit(solution)/shard_map/reduce_sum | solution.py:13
  39.7 0.1 rsqrt.29
  39.8 1.3 %copy.64 = f32[45,8,8,256]{3,1,2,0:T(8,128)S(1)} copy(f32[45,8,8,256]{3,2,1,0:T(8,128)S(1)} %bitcast.59) | data formatting | bytes 5898240
  41.1 0.0 copy-done
  41.2 1.6 %convolution_bitcast_fusion = f32[8,8,360,1]{2,1,3,0:T(8,128)S(1)} fusion(f32[2048,64]{0,1:T(8,128)S(1)} %copy-done, f32[360,2048]{1,0:T(8,128)S(1)} %bitcast.60, f32[360]{0:T(512)S(1)} %mul.103, f32[360]{0:T(512)S(1)} %rsqrt.29, f32[360]{0:T(512)S(1)} %div.28), kind=kOutput, calls=%fused_computation.15 | convolution fusion | flops 569180160 | bytes 3569888 | tf_op jit(solution)/shard_map/dot_general | solution.py:48
  42.8 2.0 %fusion.4 = f32[8,8,16,128]{3,1,2,0:T(8,128)} fusion(f32[8,8,360,1]{2,1,3,0:T(8,128)S(1)} %convolution_bitcast_fusion, f32[360]{0:T(512)S(1)} %mul.103, f32[360]{0:T(512)S(1)} %rsqrt.29, f32[360,2048]{1,0:T(8,128)S(1)} %bitcast.61, f32[360]{0:T(512)S(1)} %div.28), kind=kOutput, calls=%fused_computation.12 | convolution fusion | flops 569180160 | bytes 3569888 | tf_op jit(solution)/shard_map/dot_general | solution.py:54
  44.7 11.1 %all-to-all-done = bf16[32,90,256]{2,1,0:T(8,128)(2,1)} async-done(((bf16[32,90,256]{2,1,0:T(8,128)(2,1)}), bf16[32,90,256]{2,1,0:T(8,128)(2,1)}, u32[]{:S(2)}, u32[]{:S(2)}) %all-to-all-start) | async-done | bytes 1474592 | tf_op jit(solution)/shard_map/all_to_all | solution.py:39
  55.8 9.0 %all-to-all-start.2 = ((f32[128,8,128]{2,1,0:T(8,128)}), f32[128,8,128]{2,1,0:T(8,128)S(1)}, u32[]{:S(2)}, u32[]{:S(2)}) async-start(f32[128,8,128]{2,1,0:T(8,128)} %bitcast.11), calls=%async_computation.2 | async-start | bytes 1048576 | tf_op jit(solution)/shard_map/all_to_all | solution.py:29
  64.8 1.8 %bitcast_convert_fusion = f32[8,4,90,256]{3,2,1,0:T(8,128)S(1)} fusion(bf16[32,90,256]{2,1,0:T(8,128)(2,1)} %all-to-all-done), kind=kLoop, calls=%fused_computation.30 | loop fusion | flops 737280 | bytes 4423680 | tf_op jit(solution)/shard_map/convert_element_type | solution.py:10
  66.6 0.0 copy-start.1
  66.6 2.0 %bitcast_reduce_fusion.1 = f32[4,90]{0,1:T(8,128)S(1)} fusion(f32[8,4,90,256]{3,2,1,0:T(8,128)S(1)} %bitcast_convert_fusion), kind=kLoop, calls=%fused_computation.5 | loop fusion | flops 736920 | bytes 2950560 | tf_op jit(solution)/shard_map/reduce_sum | solution.py:11
  68.7 0.0 copy-done.1
  68.7 2.3 %multiply_reduce_fusion = f32[4,90]{0,1:T(8,128)S(1)} fusion(f32[8,4,90,256]{3,2,1,0:T(8,128)S(1)} %bitcast_convert_fusion, f32[4,90]{0,1:T(8,128)S(1)} %broadcast_multiply_fusion), kind=kLoop, calls=%fused_computation.8 | loop fusion | flops 2211480 | bytes 2952000 | tf_op jit(solution)/shard_map/reduce_sum | solution.py:13
  71.0 7.9 %all-to-all-done.2 = f32[128,8,128]{2,1,0:T(8,128)S(1)} async-done(((f32[128,8,128]{2,1,0:T(8,128)}), f32[128,8,128]{2,1,0:T(8,128)S(1)}, u32[]{:S(2)}, u32[]{:S(2)}) %all-to-all-start.2) | async-done | bytes 524320 | tf_op jit(solution)/shard_map/all_to_all | solution.py:29
  78.9 0.1 reduce_sum.67
  79.0 0.8 broadcast_in_dim.2
  79.9 4.0 %all-to-all-start.3 = ((f32[128,8,128]{2,1,0:T(8,128)}), f32[128,8,128]{2,1,0:T(8,128)S(1)}, u32[]{:S(2)}, u32[]{:S(2)}) async-start(f32[128,8,128]{2,1,0:T(8,128)} %broadcast_in_dim.2), calls=%async_computation.3 | async-start | bytes 1048576 | tf_op jit(solution)/shard_map/all_to_all | solution.py:31
  83.9 3.9 %multiply_convert_fusion.1 = bf16[4,90,8,256]{3,2,0,1:T(8,128)(2,1)S(1)} fusion(f32[8,4,90,256]{3,2,1,0:T(8,128)} %copy-done.1, f32[4,90]{0,1:T(8,128)S(1)} %add_rsqrt_fusion, f32[4,90]{0,1:T(8,128)S(1)} %broadcast_multiply_fusion), kind=kLoop, calls=%fused_computation.7 | loop fusion | flops 2211840 | bytes 4426560 | tf_op jit(solution)/shard_map/convert_element_type | solution.py:41
  87.8 2.0 %convert_element_type.73 = bf16[4,90,2048]{2,0,1:T(4,128)(2,1)} reshape(bf16[4,90,8,256]{3,2,0,1:T(8,128)(2,1)S(1)} %multiply_convert_fusion.1) | data formatting | bytes 2949120 | tf_op jit(solution)/shard_map/convert_element_type | solution.py:41
  89.8 8.3 %all-to-all-done.3 = f32[128,8,128]{2,1,0:T(8,128)S(1)} async-done(((f32[128,8,128]{2,1,0:T(8,128)}), f32[128,8,128]{2,1,0:T(8,128)S(1)}, u32[]{:S(2)}, u32[]{:S(2)}) %all-to-all-start.3) | async-done | bytes 524320 | tf_op jit(solution)/shard_map/all_to_all | solution.py:31
  98.1 0.1 reduce_sum.68
  98.2 0.2 multiply_reduce_fusion.1
  98.4 3.8 %fusion.6 = f32[4,90,64]{1,2,0:T(8,128)} fusion(bf16[4,90,2048]{2,0,1:T(4,128)(2,1)} %convert_element_type.73, f32[8,8,16,128]{3,1,2,0:T(8,128)S(1)} %bitcast.65, f32[8,8]{1,0:T(8,128)S(1)} %add_rsqrt_fusion.1, f32[8,8]{1,0:T(8,128)S(1)} %broadcast_multiply_fusion.1, f32[4,90]{1,0:T(4,128)S(1)} %get-tuple-element.7), kind=kOutput, calls=%fused_computation.14 | convolution fusion | flops 94788096 | bytes 2092960 | tf_op jit(solution)/shard_map/dot_general | solution.py:66
  (7 shorter events, 0.1 us)
Async XLA Ops:
  0.0 41.1 %copy-start = (f32[2048,64]{0,1:T(8,128)S(1)}, f32[2048,64]{0,1:T(8,128)}, u32[]{:S(2)}) copy-start(f32[2048,64]{0,1:T(8,128)} %param.6) | copy-start | bytes 1572868
  0.0 9.3 %copy-start.3 = (s32[4,90]{1,0:T(4,128)S(1)}, s32[4,90]{1,0:T(4,128)}, u32[]{:S(2)}) copy-start(s32[4,90]{1,0:T(4,128)} %param.7) | copy-start | bytes 4324
  3.4 26.5 %all-to-all-start.1 = ((bf16[32,90,256]{2,1,0:T(8,128)(2,1)}), bf16[32,90,256]{2,1,0:T(8,128)(2,1)S(1)}, u32[]{:S(2)}, u32[]{:S(2)}) async-start(bf16[32,90,256]{2,1,0:T(8,128)(2,1)} %copy.58), calls=%async_computation.1 | async-start | bytes 3145728 | tf_op jit(solution)/shard_map/all_to_all | solution.py:38
  29.9 5.0 %copy-start.2 = (bf16[32,90,256]{2,1,0:T(8,128)(2,1)}, bf16[32,90,256]{2,1,0:T(8,128)(2,1)S(1)}, u32[]{:S(2)}) copy-start(bf16[32,90,256]{2,1,0:T(8,128)(2,1)S(1)} %all-to-all-done.1) | copy-start | bytes 4423684
  29.9 25.9 %all-to-all-start = ((bf16[32,90,256]{2,1,0:T(8,128)(2,1)}), bf16[32,90,256]{2,1,0:T(8,128)(2,1)}, u32[]{:S(2)}, u32[]{:S(2)}) async-start(bf16[32,90,256]{2,1,0:T(8,128)(2,1)} %copy.52), calls=%async_computation | async-start | bytes 3145728 | tf_op jit(solution)/shard_map/all_to_all | solution.py:39
  55.8 23.1 %all-to-all-start.2 = ((f32[128,8,128]{2,1,0:T(8,128)}), f32[128,8,128]{2,1,0:T(8,128)S(1)}, u32[]{:S(2)}, u32[]{:S(2)}) async-start(f32[128,8,128]{2,1,0:T(8,128)} %bitcast.11), calls=%async_computation.2 | async-start | bytes 1048576 | tf_op jit(solution)/shard_map/all_to_all | solution.py:29
  66.6 2.1 %copy-start.1 = (f32[8,4,90,256]{3,2,1,0:T(8,128)}, f32[8,4,90,256]{3,2,1,0:T(8,128)S(1)}, u32[]{:S(2)}) copy-start(f32[8,4,90,256]{3,2,1,0:T(8,128)S(1)} %bitcast_convert_fusion) | copy-start | bytes 8847364
  79.9 18.2 %all-to-all-start.3 = ((f32[128,8,128]{2,1,0:T(8,128)}), f32[128,8,128]{2,1,0:T(8,128)S(1)}, u32[]{:S(2)}, u32[]{:S(2)}) async-start(f32[128,8,128]{2,1,0:T(8,128)} %broadcast_in_dim.2), calls=%async_computation.3 | async-start | bytes 1048576 | tf_op jit(solution)/shard_map/all_to_all | solution.py:31

commit v2 on v1

v2 whole, which is shorter than its diff:
```python
import math

import jax
import jax.numpy as jnp
from jax import lax
from jax.experimental import pallas as pl
from jax.experimental.pallas import tpu as pltpu
from jax.sharding import PartitionSpec as P

BOTH = ("tm", "space")
F32 = jnp.float32
BF16 = jnp.bfloat16
EPS = 1e-05
NT = (((1,), (1,)), ((), ()))
NN = (((1,), (0,)), ((), ()))


def params():
    return pltpu.CompilerParams(vmem_limit_bytes=40 * 1024 * 1024)


def row_chunks(rows, step):
    return [(start, min(step, rows - start)) for start in range(0, rows, step)]


def three_terms(x):
    high = x.astype(BF16)
    rest = x - high.astype(F32)
    middle = rest.astype(BF16)
    low = (rest - middle.astype(F32)).astype(BF16)
    return high, middle, low


def split_kernel(modes, e_ref, out_ref):
    for n, term in enumerate(three_terms(e_ref[...])):
        out_ref[n * modes : (n + 1) * modes, :] = term


def split_columns(columns_t):
    modes, hours = columns_t.shape
    return pl.pallas_call(
        lambda e_ref, out_ref: split_kernel(modes, e_ref, out_ref),
        out_shape=jax.ShapeDtypeStruct((3 * modes, hours), BF16),
        compiler_params=params(),
        cost_estimate=pl.CostEstimate(flops=0, bytes_accessed=5 * modes * hours * 2, transcendentals=0),
    )(columns_t)


def temp_kernel(t_ref, e_ref, w_ref, out_ref, z_ref):
    blocks, cells, width = t_ref.shape
    modes = out_ref.shape[0]
    hours = blocks * width
    for start, size in row_chunks(cells, 48):
        rows = slice(start, start + size)
        total = jnp.zeros((size, width), F32)
        for b in range(blocks):
            total = total + t_ref[b, rows, :].astype(F32)
        average = jnp.sum(total, axis=1, keepdims=True) / hours
        square = jnp.zeros((size, width), F32)
        for b in range(blocks):
            centered = t_ref[b, rows, :].astype(F32) - average
            square = square + centered * centered
        scale = lax.rsqrt(jnp.sum(square, axis=1, keepdims=True) / hours + EPS)
        weight = w_ref[rows, :]
        for b in range(blocks):
            centered = t_ref[b, rows, :].astype(F32) - average
            z_ref[b, rows, :] = ((centered * scale) * weight).astype(BF16)
    loadings = jnp.zeros((cells, 3 * modes), F32)
    for b in range(blocks):
        loadings = loadings + lax.dot_general(
            z_ref[b], e_ref[:, b * width : (b + 1) * width], NT, preferred_element_type=F32
        )
    turned = loadings.T
    turned = turned[:modes] + (turned[modes : 2 * modes] + turned[2 * modes :])
    stacked = jnp.concatenate(three_terms(turned), axis=0)
    for b in range(blocks):
        sums = lax.dot_general(stacked, z_ref[b], NN, preferred_element_type=F32)
        out_ref[:, b * width : (b + 1) * width] = sums[:modes] + (
            sums[modes : 2 * modes] + sums[2 * modes :]
        )


def temp_sums(temp, split, weight):
    blocks, cells, width = temp.shape
    modes = split.shape[0] // 3
    return pl.pallas_call(
        temp_kernel,
        out_shape=jax.ShapeDtypeStruct((modes, blocks * width), F32),
        scratch_shapes=[pltpu.VMEM((blocks, cells, width), BF16)],
        compiler_params=params(),
        cost_estimate=pl.CostEstimate(
            flops=12 * cells * modes * blocks * width,
            bytes_accessed=2 * temp.size + 2 * split.size,
            transcendentals=cells,
        ),
    )(temp, split, weight)


def hum_kernel(place_ref, *refs):
    pieces, out_ref = refs[:-1], refs[-1]
    _, lats, lons, width = pieces[0].shape
    count = 2 * len(pieces)
    for i in range(lats):
        total = jnp.zeros((lons, width), F32)
        for piece in pieces:
            for n in range(2):
                total = total + piece[n, i].astype(F32)
        average = jnp.sum(total, axis=1, keepdims=True) / (count * width)
        square = jnp.zeros((lons, width), F32)
        for piece in pieces:
            for n in range(2):
                centered = piece[n, i].astype(F32) - average
                square = square + centered * centered
        scale = lax.rsqrt(jnp.sum(square, axis=1, keepdims=True) / (count * width) + EPS)
        for p, piece in enumerate(pieces):
            for n in range(2):
                centered = piece[n, i].astype(F32) - average
                out_ref[place_ref[2 * p + n], i, :lons, :] = (centered * scale).astype(BF16)


def hum_scores(places, pieces):
    _, lats, lons, width = pieces[0].shape
    padded = -(-lons // 16) * 16
    return pl.pallas_call(
        hum_kernel,
        in_specs=[pl.BlockSpec(memory_space=pltpu.SMEM)]
        + [pl.BlockSpec(memory_space=pltpu.VMEM)] * len(pieces),
        out_shape=jax.ShapeDtypeStruct((2 * len(pieces), lats, padded, width), BF16),
        compiler_params=params(),
        cost_estimate=pl.CostEstimate(
            flops=0, bytes_accessed=16 * pieces[0].size * len(pieces), transcendentals=0
        ),
    )(places, *pieces)


def final_kernel(pcs_ref, z_ref, factor_ref, out_ref):
    octets, runs, _, _ = pcs_ref.shape
    blocks, lats, padded, width = z_ref.shape
    lons = out_ref.shape[2]
    hours = runs * 128
    rows = []
    for r in range(octets):
        pcs = jnp.concatenate([pcs_ref[r, c] for c in range(runs)], axis=1)
        centered = pcs - jnp.sum(pcs, axis=1, keepdims=True) / hours
        variance = jnp.sum(centered * centered, axis=1, keepdims=True) / hours
        rows.append(centered * lax.rsqrt(variance + EPS))
    pcz = jnp.concatenate(rows, axis=0).astype(BF16)
    for i in range(lats):
        total = jnp.zeros((padded, 8 * octets), F32)
        for b in range(blocks):
            total = total + lax.dot_general(
                z_ref[b, i], pcz[:, b * width : (b + 1) * width], NT, preferred_element_type=F32
            )
        out_ref[i] = total.T[:, :lons] * factor_ref[i : i + 1, :]


def correlate(pcs, scores, factor):
    lats, lons = factor.shape
    modes = pcs.shape[0] * pcs.shape[2]
    return pl.pallas_call(
        final_kernel,
        out_shape=jax.ShapeDtypeStruct((lats, modes, lons), F32),
        compiler_params=params(),
        cost_estimate=pl.CostEstimate(
            flops=2 * scores.size * modes, bytes_accessed=4 * pcs.size + 2 * scores.size, transcendentals=0
        ),
    )(pcs, scores, factor)


def area_root(rows, total_lat):
    latitude = ((rows.astype(F32) + 0.5) / total_lat * 120.0 - 60.0) * (math.pi / 180.0)
    return jnp.sqrt(jnp.cos(latitude))


def per_device(thermal_reading, moisture_content, gram_eigenvector_columns, marine_indicator):
    total_lat, lons, width = thermal_reading.shape
    lats = marine_indicator.shape[0]
    hours, modes = gram_eigenvector_columns.shape
    members = lax.axis_size("tm")
    chips = members // 2
    me = lax.axis_index("tm")
    chip, core = lax.div(me, 2), lax.rem(me, 2)
    to_core = [(n, n ^ 1) for n in range(members)]
    to_chip = [[(n, (n + 2 * d) % members) for n in range(members)] for d in range(chips)]
    mask_float = marine_indicator.astype(F32)

    cells = total_lat * lons // members
    temp = thermal_reading.transpose(1, 0, 2).reshape(members, cells, width)
    temp = lax.all_to_all(temp, "tm", 0, 0)

    other = lax.ppermute(mask_float, "tm", to_core)
    pair = jnp.where(core == 0, jnp.stack([mask_float, other]), jnp.stack([other, mask_float]))
    whole = jnp.zeros((chips, 2, lats, lons), F32)
    for d in range(chips):
        got = pair if d == 0 else lax.ppermute(pair, "tm", to_chip[d])
        whole = lax.dynamic_update_slice(whole, got[None], (lax.rem(chip + chips - d, chips), 0, 0, 0))
    sea = lax.dynamic_slice(whole.reshape(total_lat, lons).T.reshape(-1), (me * cells,), (cells,))
    lat_of_cell = lax.rem(me * cells + jnp.arange(cells, dtype=jnp.int32), total_lat)
    weight = (area_root(lat_of_cell, total_lat) * sea)[:, None]

    hum = moisture_content.reshape(chips, 2, lats, lons, width)
    kept = lax.dynamic_index_in_dim(hum, core, 1, keepdims=False)
    sent = lax.dynamic_index_in_dim(hum, 1 - core, 1, keepdims=False)
    traded = lax.ppermute(sent, "tm", to_core)
    pieces = []
    for d in range(chips):
        target = lax.rem(chip + d, chips)
        pieces.append(
            jnp.stack(
                [
                    lax.dynamic_index_in_dim(kept, target, 0, keepdims=False),
                    lax.dynamic_index_in_dim(traded, target, 0, keepdims=False),
                ]
            )
        )

    split = split_columns(gram_eigenvector_columns.T)
    partial_t = temp_sums(temp, split, weight)

    partial_t, *pieces = lax.optimization_barrier((partial_t, *pieces))
    blocks = partial_t.reshape(modes // 8, 8, hours // 128, 128)
    blocks = blocks.transpose(0, 2, 1, 3).reshape(-1, 8, 128)
    got = lax.all_to_all(blocks, BOTH, 0, 0)
    pieces = [pieces[0]] + [lax.ppermute(pieces[d], "tm", to_chip[d]) for d in range(1, chips)]
    mine = jnp.sum(got, axis=0, keepdims=True)
    pcs = lax.all_to_all(jnp.broadcast_to(mine, blocks.shape), BOTH, 0, 0)
    pcs = pcs.reshape(modes // 8, hours // 128, 8, 128)

    places = []
    for d in range(chips):
        source = lax.rem(chip + chips - d, chips)
        places += [2 * source + core, 2 * source + 1 - core]
    scores = hum_scores(jnp.stack(places).astype(jnp.int32), pieces)
    return correlate(pcs, scores, mask_float / hours).transpose(0, 2, 1)


def solution(mesh):
    in_specs = (P(None, "space", "tm"), P(None, "space", "tm"), P(), P("tm", "space"))
    out_specs = P("tm", "space", None)
    return jax.shard_map(
        per_device, mesh=mesh, in_specs=in_specs, out_specs=out_specs, check_vma=False
    )
```

time: 103 us -> 91.8 us (0.89)
  blocking collectives: 0 us -> 23 us
  waiting for transfers between devices: 44.4 us -> 29 us
  other arithmetic: 15.3 us -> 2.68 us
  matrix products: 7.34 us -> 0 us
  Pallas kernels: 0 us -> 6.1 us
  starting transfers between devices: 23.8 us -> 19.4 us
    all_to_all x4 -> x2, waiting for transfers between devices: 44.4 us -> 0.01 us  [the longest x1 0.01 us: per_device(): pcs = lax.all_to_all(jnp.broadcast_to(mine, blocks.shape), BOTH, 0, 0)]
    ppermute x0 -> x8, waiting for transfers between devices: none -> 29 us  [the longest x3 20.3 us: per_device(): lax.ppermute(pieces[d], 'tm', to_chip[d])]
    all_to_all x0 -> x1, blocking collectives: none -> 23 us  [per_device(): got = lax.all_to_all(blocks, BOTH, 0, 0)]
    all_to_all x4 -> x2, starting transfers between devices: 23.8 us -> 9.93 us  [the longest x1 5.93 us: per_device(): temp = lax.all_to_all(temp, 'tm', 0, 0)]
    ppermute x0 -> x8, starting transfers between devices: none -> 9.45 us  [the longest x3 5.05 us: per_device(): lax.ppermute(pieces[d], 'tm', to_chip[d])]
    reduce_sum x7 -> x1, other arithmetic: 9.47 us -> 0.14 us  [per_device(): mine = jnp.sum(got, axis=0, keepdims=True)]
    dot_general x3 -> x0, matrix products: 7.34 us -> none  [the longest x1 3.76 us: per_device(): lax.dot_general(flat_hum, pcz, (((1,), (1,)), ((), ())), preferred_elemen...]
    unnamed x11 -> x20, local copies, waits for them, and re-layouts: 8.11 us -> 1.88 us
  transfers between devices with their start and end apart: 4 -> 10, of which waited for: 4 -> 4; matrix products, arithmetic and copies ran while one was open for 25% -> 12% of each run, Pallas kernels for 0% -> 2%
where the time goes in v2:
time: 91.8 us; the launch traced here: 91.4 us
  waiting for transfers between devices  29 us (32%)
  blocking collectives  23 us (25%)
  starting transfers between devices  19.4 us (21%)
  local copies, waits for them, and re-layouts  11.1 us (12%)
  Pallas kernels  6.1 us (7%)
  other arithmetic  2.68 us (3%)
    all_to_all x1, blocking collectives, per_device(): got = lax.all_to_all(blocks, BOTH, 0, 0)  23 us
    ppermute x3, waiting for transfers between devices, per_device(): lax.ppermute(pieces[d], 'tm', to_chip[d])  20.3 us
    ppermute x3, waiting for transfers between devices, per_device(): got = pair if d == 0 else lax.ppermute(pair, 'tm', to_chip[d])  8.62 us
    all_to_all x1, starting transfers between devices, per_device(): temp = lax.all_to_all(temp, 'tm', 0, 0)  5.93 us
    ppermute x3, starting transfers between devices, per_device(): lax.ppermute(pieces[d], 'tm', to_chip[d])  5.05 us
    all_to_all x1, starting transfers between devices, per_device(): pcs = lax.all_to_all(jnp.broadcast_to(mine, blocks.shape), BOTH, 0, 0)  4 us
    ppermute x3, starting transfers between devices, per_device(): got = pair if d == 0 else lax.ppermute(pair, 'tm', to_chip[d])  3.82 us
    reshape x1, local copies, waits for them, and re-layouts, per_device(): hum = moisture_content.reshape(chips, 2, lats, lons, width)  2.8 us
  transfers between devices with their start and end apart: 10, of which 4 were waited for; matrix products, arithmetic and copies ran while one was open for 12% of the time, Pallas kernels for 2%

profile of v2, /device:TPU:1, one launch (start us, length us, event | category | flops | bytes accessed | tf_op | source)
XLA Modules:
  0.0 91.4 jit_solution(2262295453191843589)
XLA Ops:
  0.0 0.0 copy-start.7
  0.0 5.9 %all-to-all-start = ((bf16[8,360,256]{2,1,0:T(8,128)(2,1)}), bf16[8,360,256]{2,1,0:T(8,128)(2,1)S(1)}, u32[]{:S(2)}, u32[]{:S(2)}) async-start(bf16[8,360,256]{2,1,0:T(8,128)(2,1)} %bitcast.49), calls=%async_computation | async-start | bytes 2949120 | tf_op jit(solution)/shard_map/all_to_all | solution.py:189
  5.9 0.0 copy-done.7
  5.9 0.1 collective-permute-start
  6.0 2.8 %reshape.88 = bf16[4,2,4,90,256]{4,2,1,0,3:T(4,128)(2,1)S(1)} reshape(bf16[32,90,256]{2,0,1:T(8,128)(2,1)} %param.5) | data formatting | bytes 2949120 | tf_op jit(solution)/shard_map/reshape | solution.py:201
  8.8 0.0 copy-start.3
  8.9 1.4 %copy_bitcast_fusion = bf16[4,4,90,256]{3,1,2,0:T(4,128)(2,1)} fusion(bf16[4,2,4,90,256]{4,2,1,0,3:T(4,128)(2,1)S(1)} %reshape.88, s32[]{:T(128)S(6)} %select_n.75), kind=kLoop, calls=%fused_computation | loop fusion | bytes 1474564 | tf_op jit(solution)/shard_map/jit(dynamic_index_in_dim)/squeeze | solution.py:203
  10.2 0.5 collective-permute-start.4
  10.7 0.0 copy-done.3
  10.7 0.0 copy-start
  10.7 1.5 %constant_dynamic-slice_fusion.1 = (bf16[1,1,4,90,256]{4,2,1,0,3:T(4,128)(2,1)S(1)}, bf16[1,1,4,90,256]{4,2,1,0,3:T(4,128)(2,1)S(1)}, bf16[1,1,4,90,256]{4,2,1,0,3:T(4,128)(2,1)S(1)}, bf16[1,1,4,90,256]{4,2,1,0,3:T(4,128)(2,1)S(1)}) fusion(bf16[4,2,4,90,256]{4,2,1,0,3:T(4,128)(2,1)} %copy-done.3, s32[]{:T(128)S(6)} %select_n.78, s32[]{:T(128)S(6)} %select_n.74, ...), kind=kLoop, calls=%fused_computation.16 | loop fusion | bytes 1474580 | tf_op jit(solution)/shard_map/jit(dynamic_index_in_dim)/dynamic_slice | solution.py:211
  12.2 0.7 copy_bitcast_fusion.1
  13.0 0.0 copy-done
  13.0 0.2 shard_map.46.e_ref
  13.2 0.0 collective-permute-done
  13.2 2.7 %collective-permute-start.3 = (f32[2,4,90]{2,1,0:T(4,128)S(1)}, f32[2,4,90]{2,1,0:T(4,128)S(1)}, u32[]{:S(2)}, u32[]{:S(2)}) collective-permute-start(f32[2,4,90]{2,1,0:T(4,128)S(1)} %maximum_select_fusion.1), channel_id=1, source_target_pairs={{0,96},{16,112},{32,0},{48,16},{64,32},{80,48},{96,64},{112,80},{1... | collective-permute-start | bytes 8648 | tf_op jit(solution)/shard_map/ppermute | solution.py:195
  15.9 0.6 collective-permute-start.2
  16.5 0.6 collective-permute-start.1
  17.1 5.4 %collective-permute-done.1 = f32[2,4,90]{2,1,0:T(4,128)S(1)} collective-permute-done((f32[2,4,90]{2,1,0:T(4,128)S(1)}, f32[2,4,90]{2,1,0:T(4,128)S(1)}, u32[]{:S(2)}, u32[]{:S(2)}) %collective-permute-start.1) | collective-permute-done | bytes 2912 | tf_op jit(solution)/shard_map/ppermute | solution.py:195
  22.5 3.2 %collective-permute-done.2 = f32[2,4,90]{2,1,0:T(4,128)S(1)} collective-permute-done((f32[2,4,90]{2,1,0:T(4,128)S(1)}, f32[2,4,90]{2,1,0:T(4,128)S(1)}, u32[]{:S(2)}, u32[]{:S(2)}) %collective-permute-start.2) | collective-permute-done | bytes 2912 | tf_op jit(solution)/shard_map/ppermute | solution.py:195
  25.7 0.0 collective-permute-done.3
  25.7 0.1 copy.25
  25.8 0.1 reshape.87
  25.9 0.1 fusion.9
  26.0 0.1 broadcast_in_dim.28.w_ref
  26.1 0.0 copy-start.4
  26.1 0.0 collective-permute-done.4
  26.1 1.5 %constant_dynamic-slice_fusion = (bf16[1,4,90,256]{3,1,2,0:T(4,128)(2,1)S(1)}, bf16[1,4,90,256]{3,1,2,0:T(4,128)(2,1)S(1)}, bf16[1,4,90,256]{3,1,2,0:T(4,128)(2,1)S(1)}, bf16[1,4,90,256]{3,1,2,0:T(4,128)(2,1)S(1)}) fusion(bf16[4,4,90,256]{3,1,2,0:T(4,128)(2,1)} %collective-permute-done.4, s32[]{:T(128)S(6)} %select_n.67, s32[]{:T(128)S(6)} %select_n.68, ...), kind=kLoop, calls=%fused_computation.15 | loop fusion | bytes 1474576 | tf_op jit(solution)/shard_map/jit(dynamic_index_in_dim)/dynamic_slice | solution.py:212
  27.7 0.0 copy-done.4
  27.7 0.8 pad_maximum_fusion.3
  28.5 0.8 pad_maximum_fusion.2
  29.3 0.8 pad_maximum_fusion.1
  30.2 0.0 all-to-all-done.t_ref
  30.2 2.6 %shard_map.47 = f32[64,2048]{1,0:T(8,128)S(1)} custom-call(bf16[8,360,256]{2,1,0:T(8,128)(2,1)S(1)} %all-to-all-done.t_ref, bf16[192,2048]{1,0:T(8,128)(2,1)S(1)} %shard_map.46.e_ref, f32[360,1]{1,0:T(8,128)S(1)} %broadcast_in_dim.28.w_ref), custom_call_target="tpu_custom_call" | custom-call | flops 566231040 | bytes 2260992 | tf_op jit(solution)/shard_map/pallas_call | solution.py:86
  32.8 0.0 copy-start.6
  32.8 0.0 copy-start.5
  32.8 23.0 %all_to_all.15 = f32[128,8,128]{2,1,0:T(8,128)S(1)} all-to-all(f32[128,8,128]{2,1,0:T(8,128)S(1)} %bitcast.47), channel_id=1, replica_groups=mesh['tm'=8,'space'=16] {'tm','space'}, dimensions={0} | all-to-all | bytes 1048576 | tf_op jit(solution)/shard_map/all_to_all | solution.py:223
  55.8 0.1 reduce_sum.9
  55.9 0.8 broadcast_in_dim.27
  56.8 4.0 %all-to-all-start.2 = ((f32[128,8,128]{2,1,0:T(8,128)}), f32[128,8,128]{2,1,0:T(8,128)S(1)}, u32[]{:S(2)}, u32[]{:S(2)}) async-start(f32[128,8,128]{2,1,0:T(8,128)} %broadcast_in_dim.27), calls=%async_computation.2 | async-start | bytes 1048576 | tf_op jit(solution)/shard_map/all_to_all | solution.py:226
  60.8 1.5 %collective-permute-start.5 = (bf16[2,4,90,256]{3,2,1,0:T(8,128)(2,1)}, bf16[2,4,90,256]{3,2,1,0:T(8,128)(2,1)S(1)}, u32[]{:S(2)}, u32[]{:S(2)}) collective-permute-start(bf16[2,4,90,256]{3,2,1,0:T(8,128)(2,1)} %pad_maximum_fusion.1), channel_id=1, source_target_pairs={{0,32},{16,48},{32,64},{48,80},{64,96},{80,112},{96,0},{112,16},{1... | collective-permute-start | bytes 1105928 | tf_op jit(solution)/shard_map/ppermute | solution.py:224
  62.3 0.0 copy-done.6
  62.3 2.4 %collective-permute-start.6 = (bf16[2,4,90,256]{3,2,1,0:T(8,128)(2,1)S(1)}, bf16[2,4,90,256]{3,2,1,0:T(8,128)(2,1)S(1)}, u32[]{:S(2)}, u32[]{:S(2)}) collective-permute-start(bf16[2,4,90,256]{3,2,1,0:T(8,128)(2,1)S(1)} %copy-done.6), channel_id=1, source_target_pairs={{0,64},{16,80},{32,96},{48,112},{64,0},{80,16},{96,32},{112,48},{1... | collective-permute-start | bytes 1105928 | tf_op jit(solution)/shard_map/ppermute | solution.py:224
  64.7 0.0 copy-done.5
  64.7 1.2 %collective-permute-start.7 = (bf16[2,4,90,256]{3,2,1,0:T(8,128)(2,1)S(1)}, bf16[2,4,90,256]{3,2,1,0:T(8,128)(2,1)S(1)}, u32[]{:S(2)}, u32[]{:S(2)}) collective-permute-start(bf16[2,4,90,256]{3,2,1,0:T(8,128)(2,1)S(1)} %copy-done.5), channel_id=1, source_target_pairs={{0,96},{16,112},{32,0},{48,16},{64,32},{80,48},{96,64},{112,80},{1... | collective-permute-start | bytes 1105928 | tf_op jit(solution)/shard_map/ppermute | solution.py:224
  65.9 0.1 stack.89.place_ref
  65.9 11.8 %collective-permute-done.5.refs_1_ = bf16[2,4,90,256]{3,2,1,0:T(8,128)(2,1)S(1)} collective-permute-done((bf16[2,4,90,256]{3,2,1,0:T(8,128)(2,1)}, bf16[2,4,90,256]{3,2,1,0:T(8,128)(2,1)S(1)}, u32[]{:S(2)}, u32[]{:S(2)}) %collective-permute-start.5) | collective-permute-done | bytes 368672 | tf_op jit(solution)/shard_map/ppermute | solution.py:224
  77.7 8.6 %collective-permute-done.6.refs_2_ = bf16[2,4,90,256]{3,2,1,0:T(8,128)(2,1)S(1)} collective-permute-done((bf16[2,4,90,256]{3,2,1,0:T(8,128)(2,1)S(1)}, bf16[2,4,90,256]{3,2,1,0:T(8,128)(2,1)S(1)}, u32[]{:S(2)}, u32[]{:S(2)}) %collective-permute-start.6) | collective-permute-done | bytes 368672 | tf_op jit(solution)/shard_map/ppermute | solution.py:224
  86.3 0.0 collective-permute-done.7.refs_3_
  86.3 0.0 copy-start.1
  86.3 0.8 copy-done.1
  87.1 0.0 copy-start.2
  87.1 1.0 %copy-done.2 = bf16[2,4,90,256]{3,2,1,0:T(8,128)(2,1)S(1)} copy-done((bf16[2,4,90,256]{3,2,1,0:T(8,128)(2,1)S(1)}, bf16[2,4,90,256]{3,2,1,0:T(8,128)(2,1)}, u32[]{:S(2)}) %copy-start.2) | copy-done | bytes 368664
  88.1 1.8 %shard_map.48.z_ref = bf16[8,4,96,256]{3,2,1,0:T(8,128)(2,1)S(1)} custom-call(s32[8]{0:T(128)S(1)} %stack.89.place_ref, bf16[2,4,90,256]{3,2,1,0:T(8,128)(2,1)S(1)} %pad_maximum_fusion.refs_0_, bf16[2,4,90,256]{3,2,1,0:T(8,128)(2,1)S(1)} %collective-permute-done.5.refs_1_, bf16[2,4,90,256]{3,2,1,0:T(8,128)(2,1)S(1)} %collective-permute-done.6.refs_2_, ...), custom_call_target="tpu_custom_call" | custom-call | bytes 11796480 | tf_op jit(solution)/shard_map/pallas_call | solution.py:124
  89.9 0.0 all-to-all-done.2
  89.9 1.5 %shard_map.49 = f32[4,64,90]{2,1,0:T(8,128)} custom-call(f32[8,16,8,128]{3,2,1,0:T(8,128)S(1)} %bitcast.46, bf16[8,4,96,256]{3,2,1,0:T(8,128)(2,1)S(1)} %shard_map.48.z_ref, f32[4,90]{1,0:T(4,128)S(1)} %broadcast_multiply_fusion.factor_ref), custom_call_target="tpu_custom_call" | custom-call | flops 100663296 | bytes 2097152 | tf_op jit(solution)/shard_map/pallas_call | solution.py:160
  (14 shorter events, 0.2 us)
Async XLA Ops:
  0.0 5.9 %copy-start.7 = (s32[4,90]{1,0:T(4,128)S(1)}, s32[4,90]{1,0:T(4,128)}, u32[]{:S(2)}) copy-start(s32[4,90]{1,0:T(4,128)} %param.7) | copy-start | bytes 4324
  0.0 30.2 %all-to-all-start = ((bf16[8,360,256]{2,1,0:T(8,128)(2,1)}), bf16[8,360,256]{2,1,0:T(8,128)(2,1)S(1)}, u32[]{:S(2)}, u32[]{:S(2)}) async-start(bf16[8,360,256]{2,1,0:T(8,128)(2,1)} %bitcast.49), calls=%async_computation | async-start | bytes 2949120 | tf_op jit(solution)/shard_map/all_to_all | solution.py:189
  5.9 7.3 %collective-permute-start = (f32[4,90]{1,0:T(4,128)S(1)}, f32[4,90]{1,0:T(4,128)S(1)}, u32[]{:S(2)}, u32[]{:S(2)}) collective-permute-start(f32[4,90]{1,0:T(4,128)S(1)} %get-tuple-element.25), channel_id=1, source_target_pairs={{0,16},{16,0},{32,48},{48,32},{64,80},{80,64},{96,112},{112,96},{1... | collective-permute-start | bytes 4328 | tf_op jit(solution)/shard_map/ppermute | solution.py:191
  8.8 1.9 %copy-start.3 = (bf16[4,2,4,90,256]{4,2,1,0,3:T(4,128)(2,1)}, bf16[4,2,4,90,256]{4,2,1,0,3:T(4,128)(2,1)S(1)}, u32[]{:S(2)}) copy-start(bf16[4,2,4,90,256]{4,2,1,0,3:T(4,128)(2,1)S(1)} %reshape.88) | copy-start | bytes 4423684
  10.2 15.9 %collective-permute-start.4 = (bf16[4,4,90,256]{3,1,2,0:T(4,128)(2,1)}, bf16[4,4,90,256]{3,1,2,0:T(4,128)(2,1)}, u32[]{:S(2)}, u32[]{:S(2)}) collective-permute-start(bf16[4,4,90,256]{3,1,2,0:T(4,128)(2,1)} %copy_bitcast_fusion), channel_id=1, source_target_pairs={{0,16},{16,0},{32,48},{48,32},{64,80},{80,64},{96,112},{112,96},{1... | collective-permute-start | bytes 2211848 | tf_op jit(solution)/shard_map/ppermute | solution.py:204
  10.7 2.3 %copy-start = (f32[2048,64]{0,1:T(8,128)S(1)}, f32[2048,64]{0,1:T(8,128)}, u32[]{:S(2)}) copy-start(f32[2048,64]{0,1:T(8,128)} %param.6) | copy-start | bytes 1572868
  13.2 12.5 %collective-permute-start.3 = (f32[2,4,90]{2,1,0:T(4,128)S(1)}, f32[2,4,90]{2,1,0:T(4,128)S(1)}, u32[]{:S(2)}, u32[]{:S(2)}) collective-permute-start(f32[2,4,90]{2,1,0:T(4,128)S(1)} %maximum_select_fusion.1), channel_id=1, source_target_pairs={{0,96},{16,112},{32,0},{48,16},{64,32},{80,48},{96,64},{112,80},{1... | collective-permute-start | bytes 8648 | tf_op jit(solution)/shard_map/ppermute | solution.py:195
  15.9 9.8 %collective-permute-start.2 = (f32[2,4,90]{2,1,0:T(4,128)S(1)}, f32[2,4,90]{2,1,0:T(4,128)S(1)}, u32[]{:S(2)}, u32[]{:S(2)}) collective-permute-start(f32[2,4,90]{2,1,0:T(4,128)S(1)} %maximum_select_fusion.1), channel_id=1, source_target_pairs={{0,64},{16,80},{32,96},{48,112},{64,0},{80,16},{96,32},{112,48},{1... | collective-permute-start | bytes 8648 | tf_op jit(solution)/shard_map/ppermute | solution.py:195
  16.5 6.0 %collective-permute-start.1 = (f32[2,4,90]{2,1,0:T(4,128)S(1)}, f32[2,4,90]{2,1,0:T(4,128)S(1)}, u32[]{:S(2)}, u32[]{:S(2)}) collective-permute-start(f32[2,4,90]{2,1,0:T(4,128)S(1)} %maximum_select_fusion.1), channel_id=1, source_target_pairs={{0,32},{16,48},{32,64},{48,80},{64,96},{80,112},{96,0},{112,16},{1... | collective-permute-start | bytes 8648 | tf_op jit(solution)/shard_map/ppermute | solution.py:195
  26.1 1.6 %copy-start.4 = (bf16[1,4,90,256]{3,2,1,0:T(8,128)(2,1)S(1)}, bf16[1,4,90,256]{3,2,1,0:T(8,128)(2,1)}, u32[]{:S(2)}) copy-start(bf16[1,4,90,256]{3,2,1,0:T(8,128)(2,1)} %get-tuple-element.26) | copy-start | bytes 552964
  32.8 29.5 %copy-start.6 = (bf16[2,4,90,256]{3,2,1,0:T(8,128)(2,1)S(1)}, bf16[2,4,90,256]{3,2,1,0:T(8,128)(2,1)}, u32[]{:S(2)}) copy-start(bf16[2,4,90,256]{3,2,1,0:T(8,128)(2,1)} %pad_maximum_fusion.2) | copy-start | bytes 1105924
  32.8 31.9 %copy-start.5 = (bf16[2,4,90,256]{3,2,1,0:T(8,128)(2,1)S(1)}, bf16[2,4,90,256]{3,2,1,0:T(8,128)(2,1)}, u32[]{:S(2)}) copy-start(bf16[2,4,90,256]{3,2,1,0:T(8,128)(2,1)} %pad_maximum_fusion.3) | copy-start | bytes 1105924
  56.8 33.1 %all-to-all-start.2 = ((f32[128,8,128]{2,1,0:T(8,128)}), f32[128,8,128]{2,1,0:T(8,128)S(1)}, u32[]{:S(2)}, u32[]{:S(2)}) async-start(f32[128,8,128]{2,1,0:T(8,128)} %broadcast_in_dim.27), calls=%async_computation.2 | async-start | bytes 1048576 | tf_op jit(solution)/shard_map/all_to_all | solution.py:226
  60.8 16.9 %collective-permute-start.5 = (bf16[2,4,90,256]{3,2,1,0:T(8,128)(2,1)}, bf16[2,4,90,256]{3,2,1,0:T(8,128)(2,1)S(1)}, u32[]{:S(2)}, u32[]{:S(2)}) collective-permute-start(bf16[2,4,90,256]{3,2,1,0:T(8,128)(2,1)} %pad_maximum_fusion.1), channel_id=1, source_target_pairs={{0,32},{16,48},{32,64},{48,80},{64,96},{80,112},{96,0},{112,16},{1... | collective-permute-start | bytes 1105928 | tf_op jit(solution)/shard_map/ppermute | solution.py:224
  62.3 24.0 %collective-permute-start.6 = (bf16[2,4,90,256]{3,2,1,0:T(8,128)(2,1)S(1)}, bf16[2,4,90,256]{3,2,1,0:T(8,128)(2,1)S(1)}, u32[]{:S(2)}, u32[]{:S(2)}) collective-permute-start(bf16[2,4,90,256]{3,2,1,0:T(8,128)(2,1)S(1)} %copy-done.6), channel_id=1, source_target_pairs={{0,64},{16,80},{32,96},{48,112},{64,0},{80,16},{96,32},{112,48},{1... | collective-permute-start | bytes 1105928 | tf_op jit(solution)/shard_map/ppermute | solution.py:224
  64.7 21.6 %collective-permute-start.7 = (bf16[2,4,90,256]{3,2,1,0:T(8,128)(2,1)S(1)}, bf16[2,4,90,256]{3,2,1,0:T(8,128)(2,1)S(1)}, u32[]{:S(2)}, u32[]{:S(2)}) collective-permute-start(bf16[2,4,90,256]{3,2,1,0:T(8,128)(2,1)S(1)} %copy-done.5), channel_id=1, source_target_pairs={{0,96},{16,112},{32,0},{48,16},{64,32},{80,48},{96,64},{112,80},{1... | collective-permute-start | bytes 1105928 | tf_op jit(solution)/shard_map/ppermute | solution.py:224
  86.3 0.8 copy-start.1
  87.1 1.0 %copy-start.2 = (bf16[2,4,90,256]{3,2,1,0:T(8,128)(2,1)S(1)}, bf16[2,4,90,256]{3,2,1,0:T(8,128)(2,1)}, u32[]{:S(2)}) copy-start(bf16[2,4,90,256]{3,2,1,0:T(8,128)(2,1)} %copy-done.1) | copy-start | bytes 1105924

commit v3 on v2

--- a/solution.py
+++ b/solution.py
@@ -96,47 +96,74 @@
     )(temp, split, weight)
 
 
+def band_kernel(place_ref, h_ref, out_ref):
+    lons, lats, width = h_ref.shape
+    low = lax.broadcasted_iota(jnp.int32, (1, 8, width), 1) < 4
+    for start, size in row_chunks(lons, 16):
+        for top in range(0, lats, 16):
+            tiles = h_ref[start : start + size, top : top + 16, :].astype(F32)
+            for q in range(2):
+                pairs = tiles[:, 8 * q : 8 * q + 8, :].reshape(size // 2, 2, 8, width)
+                even, odd = pairs[:, 0], pairs[:, 1]
+                first = jnp.where(low, even, jnp.roll(odd, 4, axis=1))
+                second = jnp.where(low, jnp.roll(even, 4, axis=1), odd)
+                rows = slice(4 * start, 4 * (start + size))
+                band = top // 4 + 2 * q
+                out_ref[place_ref[band], rows, :] = first.reshape(4 * size, width).astype(BF16)
+                out_ref[place_ref[band + 1], rows, :] = second.reshape(4 * size, width).astype(BF16)
+
+
+def lay_out_bands(places, hum):
+    lons, lats, width = hum.shape
+    return pl.pallas_call(
+        band_kernel,
+        in_specs=[pl.BlockSpec(memory_space=pltpu.SMEM), pl.BlockSpec(memory_space=pltpu.VMEM)],
+        out_shape=jax.ShapeDtypeStruct((lats // 4, 4 * lons, width), BF16),
+        compiler_params=params(),
+        cost_estimate=pl.CostEstimate(flops=0, bytes_accessed=4 * hum.size, transcendentals=0),
+    )(places, hum)
+
+
 def hum_kernel(place_ref, *refs):
     pieces, out_ref = refs[:-1], refs[-1]
-    _, lats, lons, width = pieces[0].shape
-    count = 2 * len(pieces)
-    for i in range(lats):
-        total = jnp.zeros((lons, width), F32)
+    count = len(pieces)
+    _, cells, width = pieces[0].shape
+    hours = count * width
+    for start, size in row_chunks(cells, 48):
+        rows = slice(start, start + size)
+        total = jnp.zeros((size, width), F32)
         for piece in pieces:
-            for n in range(2):
-                total = total + piece[n, i].astype(F32)
-        average = jnp.sum(total, axis=1, keepdims=True) / (count * width)
-        square = jnp.zeros((lons, width), F32)
+            total = total + piece[0, rows, :].astype(F32)
+        average = jnp.sum(total, axis=1, keepdims=True) / hours
+        square = jnp.zeros((size, width), F32)
         for piece in pieces:
-            for n in range(2):
-                centered = piece[n, i].astype(F32) - average
-                square = square + centered * centered
-        scale = lax.rsqrt(jnp.sum(square, axis=1, keepdims=True) / (count * width) + EPS)
-        for p, piece in enumerate(pieces):
-            for n in range(2):
-                centered = piece[n, i].astype(F32) - average
-                out_ref[place_ref[2 * p + n], i, :lons, :] = (centered * scale).astype(BF16)
+            centered = piece[0, rows, :].astype(F32) - average
+            square = square + centered * centered
+        scale = lax.rsqrt(jnp.sum(square, axis=1, keepdims=True) / hours + EPS)
+        for n, piece in enumerate(pieces):
+            centered = piece[0, rows, :].astype(F32) - average
+            out_ref[place_ref[n], rows, :] = (centered * scale).astype(BF16)
 
 
 def hum_scores(places, pieces):
-    _, lats, lons, width = pieces[0].shape
-    padded = -(-lons // 16) * 16
+    count = len(pieces)
+    _, cells, width = pieces[0].shape
     return pl.pallas_call(
         hum_kernel,
         in_specs=[pl.BlockSpec(memory_space=pltpu.SMEM)]
-        + [pl.BlockSpec(memory_space=pltpu.VMEM)] * len(pieces),
-        out_shape=jax.ShapeDtypeStruct((2 * len(pieces), lats, padded, width), BF16),
+        + [pl.BlockSpec(memory_space=pltpu.VMEM)] * count,
+        out_shape=jax.ShapeDtypeStruct((count, cells, width), BF16),
         compiler_params=params(),
         cost_estimate=pl.CostEstimate(
-            flops=0, bytes_accessed=16 * pieces[0].size * len(pieces), transcendentals=0
+            flops=0, bytes_accessed=16 * cells * width * count, transcendentals=0
         ),
     )(places, *pieces)
 
 
-def final_kernel(pcs_ref, z_ref, factor_ref, out_ref):
+def final_kernel(pcs_ref, z_ref, factor_ref, out_ref, rows_ref):
     octets, runs, _, _ = pcs_ref.shape
-    blocks, lats, padded, width = z_ref.shape
-    lons = out_ref.shape[2]
+    blocks, cells, width = z_ref.shape
+    lats, modes, lons = out_ref.shape
     hours = runs * 128
     rows = []
     for r in range(octets):
@@ -145,13 +172,15 @@
         variance = jnp.sum(centered * centered, axis=1, keepdims=True) / hours
         rows.append(centered * lax.rsqrt(variance + EPS))
     pcz = jnp.concatenate(rows, axis=0).astype(BF16)
+    total = jnp.zeros((cells, modes), F32)
+    for b in range(blocks):
+        total = total + lax.dot_general(
+            z_ref[b], pcz[:, b * width : (b + 1) * width], NT, preferred_element_type=F32
+        )
+    rows_ref[:, :modes] = total
     for i in range(lats):
-        total = jnp.zeros((padded, 8 * octets), F32)
-        for b in range(blocks):
-            total = total + lax.dot_general(
-                z_ref[b, i], pcz[:, b * width : (b + 1) * width], NT, preferred_element_type=F32
-            )
-        out_ref[i] = total.T[:, :lons] * factor_ref[i : i + 1, :]
+        picked = rows_ref[pl.ds(i, lons, stride=lats), :]
+        out_ref[i] = picked.T[:modes] * factor_ref[i : i + 1, :]
 
 
 def correlate(pcs, scores, factor):
@@ -160,6 +189,7 @@
     return pl.pallas_call(
         final_kernel,
         out_shape=jax.ShapeDtypeStruct((lats, modes, lons), F32),
+        scratch_shapes=[pltpu.VMEM((lats * lons, 128), F32)],
         compiler_params=params(),
         cost_estimate=pl.CostEstimate(
             flops=2 * scores.size * modes, bytes_accessed=4 * pcs.size + 2 * scores.size, transcendentals=0
@@ -198,39 +228,38 @@
     lat_of_cell = lax.rem(me * cells + jnp.arange(cells, dtype=jnp.int32), total_lat)
     weight = (area_root(lat_of_cell, total_lat) * sea)[:, None]
 
-    hum = moisture_content.reshape(chips, 2, lats, lons, width)
-    kept = lax.dynamic_index_in_dim(hum, core, 1, keepdims=False)
-    sent = lax.dynamic_index_in_dim(hum, 1 - core, 1, keepdims=False)
-    traded = lax.ppermute(sent, "tm", to_core)
-    pieces = []
-    for d in range(chips):
-        target = lax.rem(chip + d, chips)
-        pieces.append(
-            jnp.stack(
-                [
-                    lax.dynamic_index_in_dim(kept, target, 0, keepdims=False),
-                    lax.dynamic_index_in_dim(traded, target, 0, keepdims=False),
-                ]
-            )
-        )
+    band = jnp.arange(members, dtype=jnp.int32)
+    far = lax.rem(lax.div(band, 2) + chips - chip, chips)
+    slot = lax.rem(band + core, 2)
+    order = jnp.where(far == 0, 6 + slot, jnp.where(far == 1, slot, jnp.where(far == 2, 2 + 3 * slot, 3 + slot)))
+    laid = lay_out_bands(order, moisture_content.transpose(1, 0, 2))
+    ahead, behind, own = laid[0:3], laid[3:6], laid[6:8]
+    own_traded = lax.ppermute(own[1:2], "tm", to_core)
 
     split = split_columns(gram_eigenvector_columns.T)
     partial_t = temp_sums(temp, split, weight)
 
-    partial_t, *pieces = lax.optimization_barrier((partial_t, *pieces))
+    partial_t, ahead, behind = lax.optimization_barrier((partial_t, ahead, behind))
     blocks = partial_t.reshape(modes // 8, 8, hours // 128, 128)
     blocks = blocks.transpose(0, 2, 1, 3).reshape(-1, 8, 128)
     got = lax.all_to_all(blocks, BOTH, 0, 0)
-    pieces = [pieces[0]] + [lax.ppermute(pieces[d], "tm", to_chip[d]) for d in range(1, chips)]
+    from_back = lax.ppermute(ahead, "tm", to_chip[1])
+    from_front = lax.ppermute(behind, "tm", to_chip[chips - 1])
     mine = jnp.sum(got, axis=0, keepdims=True)
+    mine, from_back, from_front = lax.optimization_barrier((mine, from_back, from_front))
     pcs = lax.all_to_all(jnp.broadcast_to(mine, blocks.shape), BOTH, 0, 0)
     pcs = pcs.reshape(modes // 8, hours // 128, 8, 128)
-
-    places = []
-    for d in range(chips):
-        source = lax.rem(chip + chips - d, chips)
-        places += [2 * source + core, 2 * source + 1 - core]
-    scores = hum_scores(jnp.stack(places).astype(jnp.int32), pieces)
+    far_first = lax.ppermute(from_back[2:3], "tm", to_chip[1])
+    far_second = lax.ppermute(from_front[2:3], "tm", to_chip[chips - 1])
+    back_traded = lax.ppermute(from_back[1:2], "tm", to_core)
+    front_traded = lax.ppermute(from_front[1:2], "tm", to_core)
+    far_traded = lax.ppermute(far_second, "tm", to_core)
+
+    pieces = [own, own_traded, from_back, back_traded, from_front, front_traded, far_first, far_traded]
+    step = lax.div(band, 2)
+    distance = jnp.where(step == 0, 0, jnp.where(step == 1, chips - 1, step - 1))
+    places = 2 * lax.rem(chip + distance, chips) + lax.rem(band + core, 2)
+    scores = hum_scores(places, pieces)
     return correlate(pcs, scores, mask_float / hours).transpose(0, 2, 1)
 
 

time: 91.8 us -> 82.9 us (0.903)
  blocking collectives: 23 us -> 0 us
  starting transfers between devices: 19.4 us -> 34.6 us
  local copies, waits for them, and re-layouts: 11.1 us -> 6.48 us
  waiting for transfers between devices: 29 us -> 32.1 us
  Pallas kernels: 6.1 us -> 8.07 us
  other arithmetic: 2.68 us -> 0.94 us
    all_to_all x1 -> x0, blocking collectives: 23 us -> none  [per_device(): got = lax.all_to_all(blocks, BOTH, 0, 0)]
    all_to_all x0 -> x1, waiting for transfers between devices: none -> 13.3 us  [per_device(): got = lax.all_to_all(blocks, BOTH, 0, 0)]
    ppermute x4 -> x8, waiting for transfers between devices: 20.3 us -> 8.54 us  [the longest x1 7.51 us: per_device(): far_second = lax.ppermute(from_front[2:3], 'tm', to_chip[chips - 1])]
    all_to_all x0 -> x1, starting transfers between devices: none -> 8.96 us  [per_device(): got = lax.all_to_all(blocks, BOTH, 0, 0)]
    dynamic_slice x4 -> x0, local copies, waits for them, and re-layouts: 3.77 us -> none  [the longest x3 2.28 us: per_device(): lax.dynamic_index_in_dim(kept, target, 0, keepdims=False)]
    reshape x1 -> x0, local copies, waits for them, and re-layouts: 2.8 us -> none  [per_device(): hum = moisture_content.reshape(chips, 2, lats, lons, width)]
    all_to_all x1, starting transfers between devices: 4 us -> 6.64 us  [per_device(): pcs = lax.all_to_all(jnp.broadcast_to(mine, blocks.shape), BOTH, 0, 0)]
    ppermute x4 -> x8, starting transfers between devices: 5.54 us -> 8.1 us  [the longest x1 2.67 us: per_device(): far_second = lax.ppermute(from_front[2:3], 'tm', to_chip[chips - 1])]
  transfers between devices with their start and end apart: 10 -> 15, of which waited for: 4 -> 6; matrix products, arithmetic and copies ran while one was open for 12% -> 4% of each run, Pallas kernels for 2% -> 4%
where the time goes in v3:
time: 82.9 us; the launch traced here: 82.4 us
  starting transfers between devices  34.6 us (42%)
  waiting for transfers between devices  32.1 us (39%)
  Pallas kernels  8.07 us (10%)
  local copies, waits for them, and re-layouts  6.48 us (8%)
  other arithmetic  0.94 us (1%)
    all_to_all x1, waiting for transfers between devices, per_device(): got = lax.all_to_all(blocks, BOTH, 0, 0)  13.3 us
    ppermute x3, waiting for transfers between devices, per_device(): got = pair if d == 0 else lax.ppermute(pair, 'tm', to_chip[d])  10.2 us
    all_to_all x1, starting transfers between devices, per_device(): got = lax.all_to_all(blocks, BOTH, 0, 0)  8.96 us
    ppermute x1, waiting for transfers between devices, per_device(): far_second = lax.ppermute(from_front[2:3], 'tm', to_chip[chips - 1])  7.51 us
    all_to_all x1, starting transfers between devices, per_device(): pcs = lax.all_to_all(jnp.broadcast_to(mine, blocks.shape), BOTH, 0, 0)  6.64 us
    ppermute x3, starting transfers between devices, per_device(): got = pair if d == 0 else lax.ppermute(pair, 'tm', to_chip[d])  5.03 us
    all_to_all x1, starting transfers between devices, per_device(): temp = lax.all_to_all(temp, 'tm', 0, 0)  4.49 us
    unnamed x10, local copies, waits for them, and re-layouts  3.46 us
  transfers between devices with their start and end apart: 15, of which 6 were waited for; matrix products, arithmetic and copies ran while one was open for 4% of the time, Pallas kernels for 4%

profile of v3, /device:TPU:1, one launch (start us, length us, event | category | flops | bytes accessed | tf_op | source)
XLA Modules:
  0.0 82.4 jit_solution(7783080775841749797)
XLA Ops:
  0.0 0.7 convert_bitcast_fusion
  0.7 1.4 %collective-permute-start = (f32[4,90]{1,0:T(4,128)S(1)}, f32[4,90]{1,0:T(4,128)S(1)}, u32[]{:S(2)}, u32[]{:S(2)}) collective-permute-start(f32[4,90]{1,0:T(4,128)S(1)} %get-tuple-element.25), channel_id=1, source_target_pairs={{0,16},{16,0},{32,48},{48,32},{64,80},{80,64},{96,112},{112,96},{1... | collective-permute-start | bytes 4328 | tf_op jit(solution)/shard_map/ppermute | solution.py:221
  2.1 4.5 %all-to-all-start = ((bf16[8,360,256]{2,1,0:T(8,128)(2,1)}), bf16[8,360,256]{2,1,0:T(8,128)(2,1)S(1)}, u32[]{:S(2)}, u32[]{:S(2)}) async-start(bf16[8,360,256]{2,1,0:T(8,128)(2,1)} %bitcast.32), calls=%async_computation | async-start | bytes 2949120 | tf_op jit(solution)/shard_map/all_to_all | solution.py:219
  6.6 0.0 copy-start.2
  6.7 1.4 %copy-done.2 = bf16[32,90,256]{2,0,1:T(8,128)(2,1)S(1)} copy-done((bf16[32,90,256]{2,0,1:T(8,128)(2,1)S(1)}, bf16[32,90,256]{2,0,1:T(8,128)(2,1)}, u32[]{:S(2)}) %copy-start.2) | copy-done | bytes 1474584
  8.0 0.9 %shard_map.48 = bf16[8,360,256]{2,1,0:T(8,128)(2,1)S(1)} custom-call(s32[8]{0:T(128)S(1)} %compare_select_fusion.10.place_ref, bf16[90,32,256]{2,1,0:T(8,128)(2,1)S(1)} %bitcast.30), custom_call_target="tpu_custom_call" | custom-call | bytes 2949120 | tf_op jit(solution)/shard_map/pallas_call | solution.py:118
  8.9 0.0 copy-start.3
  8.9 1.1 %fusion.16 = (bf16[3,360,256]{2,1,0:T(8,128)(2,1)}, bf16[3,360,256]{2,1,0:T(8,128)(2,1)}) fusion(bf16[8,360,256]{2,1,0:T(8,128)(2,1)S(1)} %shard_map.48), kind=kLoop, calls=%fused_computation.38 | loop fusion | bytes 2211840 | tf_op jit(solution)/shard_map/slice | solution.py:236
  10.0 0.1 copy-done.3
  10.1 0.2 shard_map.46.e_ref
  10.3 0.0 copy-start
  10.3 0.9 %copy-done = bf16[192,2048]{1,0:T(8,128)(2,1)} copy-done((bf16[192,2048]{1,0:T(8,128)(2,1)}, bf16[192,2048]{1,0:T(8,128)(2,1)S(1)}, u32[]{:S(2)}) %copy-start) | copy-done | bytes 786456
  11.1 0.0 collective-permute-done
  11.2 1.5 %collective-permute-start.1 = (f32[2,4,90]{2,1,0:T(4,128)S(1)}, f32[2,4,90]{2,1,0:T(4,128)S(1)}, u32[]{:S(2)}, u32[]{:S(2)}) collective-permute-start(f32[2,4,90]{2,1,0:T(4,128)S(1)} %maximum_select_fusion.1), channel_id=1, source_target_pairs={{0,32},{16,48},{32,64},{48,80},{64,96},{80,112},{96,0},{112,16},{1... | collective-permute-start | bytes 8648 | tf_op jit(solution)/shard_map/ppermute | solution.py:225
  12.6 2.4 %collective-permute-start.2 = (f32[2,4,90]{2,1,0:T(4,128)S(1)}, f32[2,4,90]{2,1,0:T(4,128)S(1)}, u32[]{:S(2)}, u32[]{:S(2)}) collective-permute-start(f32[2,4,90]{2,1,0:T(4,128)S(1)} %maximum_select_fusion.1), channel_id=1, source_target_pairs={{0,64},{16,80},{32,96},{48,112},{64,0},{80,16},{96,32},{112,48},{1... | collective-permute-start | bytes 8648 | tf_op jit(solution)/shard_map/ppermute | solution.py:225
  15.0 1.2 %collective-permute-start.3 = (f32[2,4,90]{2,1,0:T(4,128)S(1)}, f32[2,4,90]{2,1,0:T(4,128)S(1)}, u32[]{:S(2)}, u32[]{:S(2)}) collective-permute-start(f32[2,4,90]{2,1,0:T(4,128)S(1)} %maximum_select_fusion.1), channel_id=1, source_target_pairs={{0,96},{16,112},{32,0},{48,16},{64,32},{80,48},{96,64},{112,80},{1... | collective-permute-start | bytes 8648 | tf_op jit(solution)/shard_map/ppermute | solution.py:225
  16.2 6.9 %collective-permute-done.1 = f32[2,4,90]{2,1,0:T(4,128)S(1)} collective-permute-done((f32[2,4,90]{2,1,0:T(4,128)S(1)}, f32[2,4,90]{2,1,0:T(4,128)S(1)}, u32[]{:S(2)}, u32[]{:S(2)}) %collective-permute-start.1) | collective-permute-done | bytes 2912 | tf_op jit(solution)/shard_map/ppermute | solution.py:225
  23.1 3.4 %collective-permute-done.2 = f32[2,4,90]{2,1,0:T(4,128)S(1)} collective-permute-done((f32[2,4,90]{2,1,0:T(4,128)S(1)}, f32[2,4,90]{2,1,0:T(4,128)S(1)}, u32[]{:S(2)}, u32[]{:S(2)}) %collective-permute-start.2) | collective-permute-done | bytes 2912 | tf_op jit(solution)/shard_map/ppermute | solution.py:225
  26.4 0.0 collective-permute-done.3
  26.5 0.1 copy.8
  26.6 0.1 reshape.79
  26.6 0.1 fusion.9
  26.7 0.1 broadcast_in_dim.37.w_ref
  26.8 0.0 all-to-all-done.t_ref
  26.9 0.0 copy-start.1
  26.9 1.1 %copy-done.1 = bf16[192,2048]{1,0:T(8,128)(2,1)S(1)} copy-done((bf16[192,2048]{1,0:T(8,128)(2,1)S(1)}, bf16[192,2048]{1,0:T(8,128)(2,1)}, u32[]{:S(2)}) %copy-start.1) | copy-done | bytes 786456
  28.0 3.4 %shard_map.47 = f32[64,2048]{1,0:T(8,128)} custom-call(bf16[8,360,256]{2,1,0:T(8,128)(2,1)S(1)} %all-to-all-done.t_ref, bf16[192,2048]{1,0:T(8,128)(2,1)S(1)} %copy-done.1, f32[360,1]{1,0:T(8,128)S(1)} %broadcast_in_dim.37.w_ref), custom_call_target="tpu_custom_call" | custom-call | flops 566231040 | bytes 2260992 | tf_op jit(solution)/shard_map/pallas_call | solution.py:86
  31.4 0.2 collective-permute-start.4
  31.6 2.5 %collective-permute-start.5 = (bf16[3,360,256]{2,1,0:T(8,128)(2,1)}, bf16[3,360,256]{2,1,0:T(8,128)(2,1)S(1)}, u32[]{:S(2)}, u32[]{:S(2)}) collective-permute-start(bf16[3,360,256]{2,1,0:T(8,128)(2,1)} %get-tuple-element.13), channel_id=1, source_target_pairs={{0,96},{16,112},{32,0},{48,16},{64,32},{80,48},{96,64},{112,80},{1... | collective-permute-start | bytes 1658888 | tf_op jit(solution)/shard_map/ppermute | solution.py:247
  34.1 9.0 %all-to-all-start.1 = ((f32[128,8,128]{2,1,0:T(8,128)}), f32[128,8,128]{2,1,0:T(8,128)S(1)}, u32[]{:S(2)}, u32[]{:S(2)}) async-start(f32[128,8,128]{2,1,0:T(8,128)} %bitcast.15), calls=%async_computation.1 | async-start | bytes 1048576 | tf_op jit(solution)/shard_map/all_to_all | solution.py:245
  43.1 0.7 slice.36
  43.8 1.1 %collective-permute-start.6 = (bf16[1,360,256]{2,1,0:T(8,128)(2,1)}, bf16[1,360,256]{2,1,0:T(8,128)(2,1)}, u32[]{:S(2)}, u32[]{:S(2)}) collective-permute-start(bf16[1,360,256]{2,1,0:T(8,128)(2,1)} %slice.36), channel_id=1, source_target_pairs={{0,16},{16,0},{32,48},{48,32},{64,80},{80,64},{96,112},{112,96},{1... | collective-permute-start | bytes 552968 | tf_op jit(solution)/shard_map/ppermute | solution.py:237
  44.9 13.3 %all-to-all-done.1 = f32[128,8,128]{2,1,0:T(8,128)S(1)} async-done(((f32[128,8,128]{2,1,0:T(8,128)}), f32[128,8,128]{2,1,0:T(8,128)S(1)}, u32[]{:S(2)}, u32[]{:S(2)}) %all-to-all-start.1) | async-done | bytes 524320 | tf_op jit(solution)/shard_map/all_to_all | solution.py:245
  58.2 0.1 reduce_sum.9
  58.3 0.0 collective-permute-done.4.refs_2_
  58.3 0.0 collective-permute-done.5.refs_4_
  58.3 0.0 copy-start.4
  58.3 0.8 %broadcast_in_dim.36 = f32[128,8,128]{2,1,0:T(8,128)} broadcast(f32[8,128]{1,0:T(8,128)S(1)} %reduce_sum.9), dimensions={1,2} | broadcast | bytes 528384 | tf_op jit(solution)/shard_map/broadcast_in_dim | solution.py:250
  59.2 6.6 %all-to-all-start.2 = ((f32[128,8,128]{2,1,0:T(8,128)}), f32[128,8,128]{2,1,0:T(8,128)S(1)}, u32[]{:S(2)}, u32[]{:S(2)}) async-start(f32[128,8,128]{2,1,0:T(8,128)} %broadcast_in_dim.36), calls=%async_computation.2 | async-start | bytes 1048576 | tf_op jit(solution)/shard_map/all_to_all | solution.py:250
  65.9 2.7 %collective-permute-start.10 = (bf16[1,360,256]{2,1,0:T(8,128)(2,1)S(1)}, bf16[1,360,256]{2,1,0:T(8,128)(2,1)S(1)}, u32[]{:S(2)}, u32[]{:S(2)}) collective-permute-start(bf16[1,360,256]{2,1,0:T(8,128)(2,1)S(1)} %get-tuple-element.19), channel_id=1, source_target_pairs={{0,96},{16,112},{32,0},{48,16},{64,32},{80,48},{96,64},{112,80},{1... | collective-permute-start | bytes 552968 | tf_op jit(solution)/shard_map/ppermute | solution.py:253
  68.6 0.7 collective-permute-start.7
  69.3 0.1 collective-permute-start.8
  69.4 0.0 collective-permute-start.9
  69.4 7.5 %collective-permute-done.10 = bf16[1,360,256]{2,1,0:T(8,128)(2,1)S(1)} collective-permute-done((bf16[1,360,256]{2,1,0:T(8,128)(2,1)S(1)}, bf16[1,360,256]{2,1,0:T(8,128)(2,1)S(1)}, u32[]{:S(2)}, u32[]{:S(2)}) %collective-permute-start.10) | collective-permute-done | bytes 184352 | tf_op jit(solution)/shard_map/ppermute | solution.py:253
  76.9 0.9 %collective-permute-start.11 = (bf16[1,360,256]{2,1,0:T(8,128)(2,1)S(1)}, bf16[1,360,256]{2,1,0:T(8,128)(2,1)S(1)}, u32[]{:S(2)}, u32[]{:S(2)}) collective-permute-start(bf16[1,360,256]{2,1,0:T(8,128)(2,1)S(1)} %collective-permute-done.10), channel_id=1, source_target_pairs={{0,16},{16,0},{32,48},{48,32},{64,80},{80,64},{96,112},{112,96},{1... | collective-permute-start | bytes 552968 | tf_op jit(solution)/shard_map/ppermute | solution.py:256
  77.8 0.0 copy-done.4
  77.8 0.0 collective-permute-done.6.refs_1_
  77.8 0.0 collective-permute-done.7.refs_3_
  77.8 0.0 collective-permute-done.8.refs_5_
  77.8 0.4 collective-permute-done.9.refs_6_
  78.2 0.6 collective-permute-done.11.refs_7_
  78.8 2.1 %shard_map.49.z_ref = bf16[8,360,256]{2,1,0:T(8,128)(2,1)S(1)} custom-call(s32[8]{0:T(128)S(1)} %fusion.15.place_ref, bf16[2,360,256]{2,1,0:T(8,128)(2,1)S(1)} %slice.35.refs_0_, bf16[1,360,256]{2,1,0:T(8,128)(2,1)} %collective-permute-done.6.refs_1_, bf16[3,360,256]{2,1,0:T(8,128)(2,1)S(1)} %collective-permute-done.4.refs_2_, ...), custom_call_target="tpu_custom_call" | custom-call | bytes 11796480 | tf_op jit(solution)/shard_map/pallas_call | solution.py:151
  80.9 0.0 all-to-all-done.2
  80.9 1.5 %shard_map.50 = f32[4,64,90]{2,1,0:T(8,128)} custom-call(f32[8,16,8,128]{3,2,1,0:T(8,128)S(1)} %bitcast.29, bf16[8,360,256]{2,1,0:T(8,128)(2,1)S(1)} %shard_map.49.z_ref, f32[4,90]{1,0:T(4,128)S(1)} %broadcast_multiply_fusion.factor_ref), custom_call_target="tpu_custom_call" | custom-call | flops 94371840 | bytes 1998848 | tf_op jit(solution)/shard_map/pallas_call | solution.py:189
  (12 shorter events, 0.1 us)
Async XLA Ops:
  0.7 10.5 %collective-permute-start = (f32[4,90]{1,0:T(4,128)S(1)}, f32[4,90]{1,0:T(4,128)S(1)}, u32[]{:S(2)}, u32[]{:S(2)}) collective-permute-start(f32[4,90]{1,0:T(4,128)S(1)} %get-tuple-element.25), channel_id=1, source_target_pairs={{0,16},{16,0},{32,48},{48,32},{64,80},{80,64},{96,112},{112,96},{1... | collective-permute-start | bytes 4328 | tf_op jit(solution)/shard_map/ppermute | solution.py:221
  2.1 24.7 %all-to-all-start = ((bf16[8,360,256]{2,1,0:T(8,128)(2,1)}), bf16[8,360,256]{2,1,0:T(8,128)(2,1)S(1)}, u32[]{:S(2)}, u32[]{:S(2)}) async-start(bf16[8,360,256]{2,1,0:T(8,128)(2,1)} %bitcast.32), calls=%async_computation | async-start | bytes 2949120 | tf_op jit(solution)/shard_map/all_to_all | solution.py:219
  6.6 1.4 %copy-start.2 = (bf16[32,90,256]{2,0,1:T(8,128)(2,1)S(1)}, bf16[32,90,256]{2,0,1:T(8,128)(2,1)}, u32[]{:S(2)}) copy-start(bf16[32,90,256]{2,0,1:T(8,128)(2,1)} %param.5) | copy-start | bytes 4423684
  8.9 1.2 %copy-start.3 = (f32[2048,64]{0,1:T(8,128)S(1)}, f32[2048,64]{0,1:T(8,128)}, u32[]{:S(2)}) copy-start(f32[2048,64]{0,1:T(8,128)} %param.6) | copy-start | bytes 1572868
  10.3 0.9 %copy-start = (bf16[192,2048]{1,0:T(8,128)(2,1)}, bf16[192,2048]{1,0:T(8,128)(2,1)S(1)}, u32[]{:S(2)}) copy-start(bf16[192,2048]{1,0:T(8,128)(2,1)S(1)} %shard_map.46.e_ref) | copy-start | bytes 2359300
  11.2 11.9 %collective-permute-start.1 = (f32[2,4,90]{2,1,0:T(4,128)S(1)}, f32[2,4,90]{2,1,0:T(4,128)S(1)}, u32[]{:S(2)}, u32[]{:S(2)}) collective-permute-start(f32[2,4,90]{2,1,0:T(4,128)S(1)} %maximum_select_fusion.1), channel_id=1, source_target_pairs={{0,32},{16,48},{32,64},{48,80},{64,96},{80,112},{96,0},{112,16},{1... | collective-permute-start | bytes 8648 | tf_op jit(solution)/shard_map/ppermute | solution.py:225
  12.6 13.8 %collective-permute-start.2 = (f32[2,4,90]{2,1,0:T(4,128)S(1)}, f32[2,4,90]{2,1,0:T(4,128)S(1)}, u32[]{:S(2)}, u32[]{:S(2)}) collective-permute-start(f32[2,4,90]{2,1,0:T(4,128)S(1)} %maximum_select_fusion.1), channel_id=1, source_target_pairs={{0,64},{16,80},{32,96},{48,112},{64,0},{80,16},{96,32},{112,48},{1... | collective-permute-start | bytes 8648 | tf_op jit(solution)/shard_map/ppermute | solution.py:225
  15.0 11.4 %collective-permute-start.3 = (f32[2,4,90]{2,1,0:T(4,128)S(1)}, f32[2,4,90]{2,1,0:T(4,128)S(1)}, u32[]{:S(2)}, u32[]{:S(2)}) collective-permute-start(f32[2,4,90]{2,1,0:T(4,128)S(1)} %maximum_select_fusion.1), channel_id=1, source_target_pairs={{0,96},{16,112},{32,0},{48,16},{64,32},{80,48},{96,64},{112,80},{1... | collective-permute-start | bytes 8648 | tf_op jit(solution)/shard_map/ppermute | solution.py:225
  26.9 1.1 %copy-start.1 = (bf16[192,2048]{1,0:T(8,128)(2,1)S(1)}, bf16[192,2048]{1,0:T(8,128)(2,1)}, u32[]{:S(2)}) copy-start(bf16[192,2048]{1,0:T(8,128)(2,1)} %copy-done) | copy-start | bytes 2359300
  31.4 26.9 %collective-permute-start.4 = (bf16[3,360,256]{2,1,0:T(8,128)(2,1)}, bf16[3,360,256]{2,1,0:T(8,128)(2,1)S(1)}, u32[]{:S(2)}, u32[]{:S(2)}) collective-permute-start(bf16[3,360,256]{2,1,0:T(8,128)(2,1)} %get-tuple-element.12), channel_id=1, source_target_pairs={{0,32},{16,48},{32,64},{48,80},{64,96},{80,112},{96,0},{112,16},{1... | collective-permute-start | bytes 1658888 | tf_op jit(solution)/shard_map/ppermute | solution.py:246
  31.6 26.7 %collective-permute-start.5 = (bf16[3,360,256]{2,1,0:T(8,128)(2,1)}, bf16[3,360,256]{2,1,0:T(8,128)(2,1)S(1)}, u32[]{:S(2)}, u32[]{:S(2)}) collective-permute-start(bf16[3,360,256]{2,1,0:T(8,128)(2,1)} %get-tuple-element.13), channel_id=1, source_target_pairs={{0,96},{16,112},{32,0},{48,16},{64,32},{80,48},{96,64},{112,80},{1... | collective-permute-start | bytes 1658888 | tf_op jit(solution)/shard_map/ppermute | solution.py:247
  34.1 24.1 %all-to-all-start.1 = ((f32[128,8,128]{2,1,0:T(8,128)}), f32[128,8,128]{2,1,0:T(8,128)S(1)}, u32[]{:S(2)}, u32[]{:S(2)}) async-start(f32[128,8,128]{2,1,0:T(8,128)} %bitcast.15), calls=%async_computation.1 | async-start | bytes 1048576 | tf_op jit(solution)/shard_map/all_to_all | solution.py:245
  43.8 34.0 %collective-permute-start.6 = (bf16[1,360,256]{2,1,0:T(8,128)(2,1)}, bf16[1,360,256]{2,1,0:T(8,128)(2,1)}, u32[]{:S(2)}, u32[]{:S(2)}) collective-permute-start(bf16[1,360,256]{2,1,0:T(8,128)(2,1)} %slice.36), channel_id=1, source_target_pairs={{0,16},{16,0},{32,48},{48,32},{64,80},{80,64},{96,112},{112,96},{1... | collective-permute-start | bytes 552968 | tf_op jit(solution)/shard_map/ppermute | solution.py:237
  58.3 19.4 %copy-start.4 = (s32[4,90]{1,0:T(4,128)S(1)}, s32[4,90]{1,0:T(4,128)}, u32[]{:S(2)}) copy-start(s32[4,90]{1,0:T(4,128)} %param.7) | copy-start | bytes 4324
  59.2 21.7 %all-to-all-start.2 = ((f32[128,8,128]{2,1,0:T(8,128)}), f32[128,8,128]{2,1,0:T(8,128)S(1)}, u32[]{:S(2)}, u32[]{:S(2)}) async-start(f32[128,8,128]{2,1,0:T(8,128)} %broadcast_in_dim.36), calls=%async_computation.2 | async-start | bytes 1048576 | tf_op jit(solution)/shard_map/all_to_all | solution.py:250
  65.9 11.0 %collective-permute-start.10 = (bf16[1,360,256]{2,1,0:T(8,128)(2,1)S(1)}, bf16[1,360,256]{2,1,0:T(8,128)(2,1)S(1)}, u32[]{:S(2)}, u32[]{:S(2)}) collective-permute-start(bf16[1,360,256]{2,1,0:T(8,128)(2,1)S(1)} %get-tuple-element.19), channel_id=1, source_target_pairs={{0,96},{16,112},{32,0},{48,16},{64,32},{80,48},{96,64},{112,80},{1... | collective-permute-start | bytes 552968 | tf_op jit(solution)/shard_map/ppermute | solution.py:253
  68.6 9.2 %collective-permute-start.7 = (bf16[1,360,256]{2,1,0:T(8,128)(2,1)S(1)}, bf16[1,360,256]{2,1,0:T(8,128)(2,1)S(1)}, u32[]{:S(2)}, u32[]{:S(2)}) collective-permute-start(bf16[1,360,256]{2,1,0:T(8,128)(2,1)S(1)} %get-tuple-element.22), channel_id=1, source_target_pairs={{0,16},{16,0},{32,48},{48,32},{64,80},{80,64},{96,112},{112,96},{1... | collective-permute-start | bytes 552968 | tf_op jit(solution)/shard_map/ppermute | solution.py:254
  69.3 8.5 %collective-permute-start.8 = (bf16[1,360,256]{2,1,0:T(8,128)(2,1)S(1)}, bf16[1,360,256]{2,1,0:T(8,128)(2,1)S(1)}, u32[]{:S(2)}, u32[]{:S(2)}) collective-permute-start(bf16[1,360,256]{2,1,0:T(8,128)(2,1)S(1)} %get-tuple-element.20), channel_id=1, source_target_pairs={{0,16},{16,0},{32,48},{48,32},{64,80},{80,64},{96,112},{112,96},{1... | collective-permute-start | bytes 552968 | tf_op jit(solution)/shard_map/ppermute | solution.py:255
  69.4 8.8 %collective-permute-start.9 = (bf16[1,360,256]{2,1,0:T(8,128)(2,1)S(1)}, bf16[1,360,256]{2,1,0:T(8,128)(2,1)S(1)}, u32[]{:S(2)}, u32[]{:S(2)}) collective-permute-start(bf16[1,360,256]{2,1,0:T(8,128)(2,1)S(1)} %get-tuple-element.21), channel_id=1, source_target_pairs={{0,32},{16,48},{32,64},{48,80},{64,96},{80,112},{96,0},{112,16},{1... | collective-permute-start | bytes 552968 | tf_op jit(solution)/shard_map/ppermute | solution.py:252
  76.9 1.9 %collective-permute-start.11 = (bf16[1,360,256]{2,1,0:T(8,128)(2,1)S(1)}, bf16[1,360,256]{2,1,0:T(8,128)(2,1)S(1)}, u32[]{:S(2)}, u32[]{:S(2)}) collective-permute-start(bf16[1,360,256]{2,1,0:T(8,128)(2,1)S(1)} %collective-permute-done.10), channel_id=1, source_target_pairs={{0,16},{16,0},{32,48},{48,32},{64,80},{80,64},{96,112},{112,96},{1... | collective-permute-start | bytes 552968 | tf_op jit(solution)/shard_map/ppermute | solution.py:256

commit v4 on v3

--- a/solution.py
+++ b/solution.py
@@ -16,7 +16,7 @@
 
 
 def params():
-    return pltpu.CompilerParams(vmem_limit_bytes=40 * 1024 * 1024)
+    return pltpu.CompilerParams(vmem_limit_bytes=16 * 1024 * 1024)
 
 
 def row_chunks(rows, step):
@@ -31,25 +31,13 @@
     return high, middle, low
 
 
-def split_kernel(modes, e_ref, out_ref):
-    for n, term in enumerate(three_terms(e_ref[...])):
-        out_ref[n * modes : (n + 1) * modes, :] = term
-
-
-def split_columns(columns_t):
-    modes, hours = columns_t.shape
-    return pl.pallas_call(
-        lambda e_ref, out_ref: split_kernel(modes, e_ref, out_ref),
-        out_shape=jax.ShapeDtypeStruct((3 * modes, hours), BF16),
-        compiler_params=params(),
-        cost_estimate=pl.CostEstimate(flops=0, bytes_accessed=5 * modes * hours * 2, transcendentals=0),
-    )(columns_t)
-
-
-def temp_kernel(t_ref, e_ref, w_ref, out_ref, z_ref):
+def temp_kernel(t_ref, columns_ref, w_ref, out_ref, z_ref, e_ref, arrived):
     blocks, cells, width = t_ref.shape
     modes = out_ref.shape[0]
     hours = blocks * width
+    fetch = pltpu.make_async_copy(columns_ref, e_ref, arrived)
+    fetch.start()
+    weights = jnp.broadcast_to(w_ref[...], (128, cells)).T
     for start, size in row_chunks(cells, 48):
         rows = slice(start, start + size)
         total = jnp.zeros((size, width), F32)
@@ -61,15 +49,15 @@
             centered = t_ref[b, rows, :].astype(F32) - average
             square = square + centered * centered
         scale = lax.rsqrt(jnp.sum(square, axis=1, keepdims=True) / hours + EPS)
-        weight = w_ref[rows, :]
+        weight = weights[rows, :1]
         for b in range(blocks):
             centered = t_ref[b, rows, :].astype(F32) - average
             z_ref[b, rows, :] = ((centered * scale) * weight).astype(BF16)
+    fetch.wait()
     loadings = jnp.zeros((cells, 3 * modes), F32)
     for b in range(blocks):
-        loadings = loadings + lax.dot_general(
-            z_ref[b], e_ref[:, b * width : (b + 1) * width], NT, preferred_element_type=F32
-        )
+        columns = jnp.concatenate(three_terms(e_ref[:, b * width : (b + 1) * width]), axis=0)
+        loadings = loadings + lax.dot_general(z_ref[b], columns, NT, preferred_element_type=F32)
     turned = loadings.T
     turned = turned[:modes] + (turned[modes : 2 * modes] + turned[2 * modes :])
     stacked = jnp.concatenate(three_terms(turned), axis=0)
@@ -80,20 +68,52 @@
         )
 
 
-def temp_sums(temp, split, weight):
+def temp_sums(temp, columns_t, weight):
     blocks, cells, width = temp.shape
-    modes = split.shape[0] // 3
+    modes = columns_t.shape[0]
     return pl.pallas_call(
         temp_kernel,
         out_shape=jax.ShapeDtypeStruct((modes, blocks * width), F32),
-        scratch_shapes=[pltpu.VMEM((blocks, cells, width), BF16)],
+        in_specs=[
+            pl.BlockSpec(memory_space=pltpu.VMEM),
+            pl.BlockSpec(memory_space=pl.ANY),
+            pl.BlockSpec(memory_space=pltpu.VMEM),
+        ],
+        scratch_shapes=[
+            pltpu.VMEM((blocks, cells, width), BF16),
+            pltpu.VMEM(columns_t.shape, F32),
+            pltpu.SemaphoreType.DMA,
+        ],
         compiler_params=params(),
         cost_estimate=pl.CostEstimate(
             flops=12 * cells * modes * blocks * width,
-            bytes_accessed=2 * temp.size + 2 * split.size,
+            bytes_accessed=2 * temp.size + 4 * columns_t.size,
             transcendentals=cells,
         ),
-    )(temp, split, weight)
+    )(temp, columns_t, weight)
+
+
+def sum_kernel(got_ref, out_ref):
+    count = got_ref.shape[0]
+    parts = []
+    for n in range(8):
+        part = got_ref[n]
+        for m in range(n + 8, count, 8):
+            part = part + got_ref[m]
+        parts.append(part)
+    while len(parts) > 1:
+        parts = [parts[n] + parts[n + 1] for n in range(0, len(parts), 2)]
+    for n in range(count):
+        out_ref[n] = parts[0]
+
+
+def sum_for_all(got):
+    return pl.pallas_call(
+        sum_kernel,
+        out_shape=jax.ShapeDtypeStruct(got.shape, F32),
+        compiler_params=params(),
+        cost_estimate=pl.CostEstimate(flops=got.size, bytes_accessed=8 * got.size, transcendentals=0),
+    )(got)
 
 
 def band_kernel(place_ref, h_ref, out_ref):
@@ -218,15 +238,15 @@
     temp = thermal_reading.transpose(1, 0, 2).reshape(members, cells, width)
     temp = lax.all_to_all(temp, "tm", 0, 0)
 
-    other = lax.ppermute(mask_float, "tm", to_core)
-    pair = jnp.where(core == 0, jnp.stack([mask_float, other]), jnp.stack([other, mask_float]))
-    whole = jnp.zeros((chips, 2, lats, lons), F32)
+    other = lax.ppermute(marine_indicator, "tm", to_core)
+    pair = jnp.where(core == 0, jnp.stack([marine_indicator, other]), jnp.stack([other, marine_indicator]))
+    whole = jnp.zeros((chips, 2, lats, lons), jnp.int32)
     for d in range(chips):
         got = pair if d == 0 else lax.ppermute(pair, "tm", to_chip[d])
         whole = lax.dynamic_update_slice(whole, got[None], (lax.rem(chip + chips - d, chips), 0, 0, 0))
     sea = lax.dynamic_slice(whole.reshape(total_lat, lons).T.reshape(-1), (me * cells,), (cells,))
     lat_of_cell = lax.rem(me * cells + jnp.arange(cells, dtype=jnp.int32), total_lat)
-    weight = (area_root(lat_of_cell, total_lat) * sea)[:, None]
+    weight = (area_root(lat_of_cell, total_lat) * sea.astype(F32))[None, :]
 
     band = jnp.arange(members, dtype=jnp.int32)
     far = lax.rem(lax.div(band, 2) + chips - chip, chips)
@@ -236,23 +256,22 @@
     ahead, behind, own = laid[0:3], laid[3:6], laid[6:8]
     own_traded = lax.ppermute(own[1:2], "tm", to_core)
 
-    split = split_columns(gram_eigenvector_columns.T)
-    partial_t = temp_sums(temp, split, weight)
-
-    partial_t, ahead, behind = lax.optimization_barrier((partial_t, ahead, behind))
+    weight, ahead, behind = lax.optimization_barrier((weight, ahead, behind))
+    partial_t = temp_sums(temp, gram_eigenvector_columns.T, weight)
     blocks = partial_t.reshape(modes // 8, 8, hours // 128, 128)
     blocks = blocks.transpose(0, 2, 1, 3).reshape(-1, 8, 128)
     got = lax.all_to_all(blocks, BOTH, 0, 0)
     from_back = lax.ppermute(ahead, "tm", to_chip[1])
     from_front = lax.ppermute(behind, "tm", to_chip[chips - 1])
-    mine = jnp.sum(got, axis=0, keepdims=True)
-    mine, from_back, from_front = lax.optimization_barrier((mine, from_back, from_front))
-    pcs = lax.all_to_all(jnp.broadcast_to(mine, blocks.shape), BOTH, 0, 0)
-    pcs = pcs.reshape(modes // 8, hours // 128, 8, 128)
     far_first = lax.ppermute(from_back[2:3], "tm", to_chip[1])
     far_second = lax.ppermute(from_front[2:3], "tm", to_chip[chips - 1])
     back_traded = lax.ppermute(from_back[1:2], "tm", to_core)
     front_traded = lax.ppermute(from_front[1:2], "tm", to_core)
+    got, far_first, far_second, back_traded, front_traded = lax.optimization_barrier(
+        (got, far_first, far_second, back_traded, front_traded)
+    )
+    pcs = lax.all_to_all(sum_for_all(got), BOTH, 0, 0)
+    pcs = pcs.reshape(modes // 8, hours // 128, 8, 128)
     far_traded = lax.ppermute(far_second, "tm", to_core)
 
     pieces = [own, own_traded, from_back, back_traded, from_front, front_traded, far_first, far_traded]

time: 82.9 us -> 80.8 us (0.975)
  waiting for transfers between devices: 32.1 us -> 30.3 us
  local copies, waits for them, and re-layouts: 6.48 us -> 4.83 us
  Pallas kernels: 8.07 us -> 9.59 us
  starting transfers between devices: 34.6 us -> 35.5 us
    all_to_all x1, waiting for transfers between devices: 13.3 us -> 1.8 us  [per_device(): got = lax.all_to_all(blocks, BOTH, 0, 0)]
    all_to_all x1, waiting for transfers between devices: 0.01 us -> 8.94 us  [per_device(): pcs = lax.all_to_all(sum_for_all(got), BOTH, 0, 0)]
    ppermute x1, waiting for transfers between devices: 7.51 us -> 0.01 us  [per_device(): far_second = lax.ppermute(from_front[2:3], 'tm', to_chip[chips - 1])]
    ppermute x1, waiting for transfers between devices: 0.42 us -> 6.85 us  [per_device(): far_first = lax.ppermute(from_back[2:3], 'tm', to_chip[1])]
    ppermute x1, starting transfers between devices: 0.01 us -> 1.45 us  [per_device(): far_first = lax.ppermute(from_back[2:3], 'tm', to_chip[1])]
    all_to_all x1, starting transfers between devices: 4.49 us -> 5.93 us  [per_device(): temp = lax.all_to_all(temp, 'tm', 0, 0)]
    ppermute x1, starting transfers between devices: 1.42 us -> 0.09 us  [per_device(): other = lax.ppermute(marine_indicator, 'tm', to_core)]
    ppermute x1, starting transfers between devices: 2.67 us -> 1.36 us  [per_device(): far_second = lax.ppermute(from_front[2:3], 'tm', to_chip[chips - 1])]
  transfers between devices with their start and end apart: 15 -> 15, of which waited for: 6 -> 7; matrix products, arithmetic and copies ran while one was open for 4% -> 3% of each run, Pallas kernels for 4% -> 9%
where the time goes in v4:
time: 80.8 us; the launch traced here: 80.4 us
  starting transfers between devices  35.5 us (44%)
  waiting for transfers between devices  30.3 us (38%)
  Pallas kernels  9.59 us (12%)
  local copies, waits for them, and re-layouts  4.83 us (6%)
    ppermute x3, waiting for transfers between devices, per_device(): got = pair if d == 0 else lax.ppermute(pair, 'tm', to_chip[d])  11 us
    all_to_all x1, starting transfers between devices, per_device(): got = lax.all_to_all(blocks, BOTH, 0, 0)  8.97 us
    all_to_all x1, waiting for transfers between devices, per_device(): pcs = lax.all_to_all(sum_for_all(got), BOTH, 0, 0)  8.94 us
    ppermute x1, waiting for transfers between devices, per_device(): far_first = lax.ppermute(from_back[2:3], 'tm', to_chip[1])  6.85 us
    all_to_all x1, starting transfers between devices, per_device(): pcs = lax.all_to_all(sum_for_all(got), BOTH, 0, 0)  6.77 us
    all_to_all x1, starting transfers between devices, per_device(): temp = lax.all_to_all(temp, 'tm', 0, 0)  5.93 us
    ppermute x3, starting transfers between devices, per_device(): got = pair if d == 0 else lax.ppermute(pair, 'tm', to_chip[d])  5.3 us
    pallas_call x1, Pallas kernels, temp_sums(): pl.pallas_call(temp_kernel, out_shape=jax.ShapeDtypeStruct((modes, blocks...  4.13 us
  transfers between devices with their start and end apart: 15, of which 7 were waited for; matrix products, arithmetic and copies ran while one was open for 3% of the time, Pallas kernels for 9%

profile of v4, /device:TPU:1, one launch (start us, length us, event | category | flops | bytes accessed | tf_op | source)
XLA Modules:
  0.0 80.4 jit_solution(2045665046674896696)
XLA Ops:
  0.0 0.0 copy-start.2
  0.0 5.9 %all-to-all-start = ((bf16[8,360,256]{2,1,0:T(8,128)(2,1)}), bf16[8,360,256]{2,1,0:T(8,128)(2,1)S(1)}, u32[]{:S(2)}, u32[]{:S(2)}) async-start(bf16[8,360,256]{2,1,0:T(8,128)(2,1)} %bitcast.28), calls=%async_computation | async-start | bytes 2949120 | tf_op jit(solution)/shard_map/all_to_all | solution.py:239
  5.9 0.0 copy-done.2
  5.9 0.1 collective-permute-start
  6.0 0.0 copy-start
  6.0 1.4 %copy-done = bf16[32,90,256]{2,0,1:T(8,128)(2,1)S(1)} copy-done((bf16[32,90,256]{2,0,1:T(8,128)(2,1)S(1)}, bf16[32,90,256]{2,0,1:T(8,128)(2,1)}, u32[]{:S(2)}) %copy-start) | copy-done | bytes 1474584
  7.4 0.9 %shard_map.46 = bf16[8,360,256]{2,1,0:T(8,128)(2,1)S(1)} custom-call(s32[8]{0:T(128)S(1)} %compare_select_fusion.10.place_ref, bf16[90,32,256]{2,1,0:T(8,128)(2,1)S(1)} %bitcast.26), custom_call_target="tpu_custom_call" | custom-call | bytes 2949120 | tf_op jit(solution)/shard_map/pallas_call | solution.py:138
  8.3 1.1 %fusion.16 = (bf16[3,360,256]{2,1,0:T(8,128)(2,1)}, bf16[3,360,256]{2,1,0:T(8,128)(2,1)}) fusion(bf16[8,360,256]{2,1,0:T(8,128)(2,1)S(1)} %shard_map.46), kind=kLoop, calls=%fused_computation.36 | loop fusion | bytes 2211840 | tf_op jit(solution)/shard_map/slice | solution.py:256
  9.4 0.0 collective-permute-done
  9.4 1.7 %collective-permute-start.1 = (s32[2,4,90]{2,1,0:T(4,128)S(1)}, s32[2,4,90]{2,1,0:T(4,128)S(1)}, u32[]{:S(2)}, u32[]{:S(2)}) collective-permute-start(s32[2,4,90]{2,1,0:T(4,128)S(1)} %add_select_fusion.1), channel_id=1, source_target_pairs={{0,32},{16,48},{32,64},{48,80},{64,96},{80,112},{96,0},{112,16},{1... | collective-permute-start | bytes 8648 | tf_op jit(solution)/shard_map/ppermute | solution.py:245
  11.1 2.4 %collective-permute-start.2 = (s32[2,4,90]{2,1,0:T(4,128)S(1)}, s32[2,4,90]{2,1,0:T(4,128)S(1)}, u32[]{:S(2)}, u32[]{:S(2)}) collective-permute-start(s32[2,4,90]{2,1,0:T(4,128)S(1)} %add_select_fusion.1), channel_id=1, source_target_pairs={{0,64},{16,80},{32,96},{48,112},{64,0},{80,16},{96,32},{112,48},{1... | collective-permute-start | bytes 8648 | tf_op jit(solution)/shard_map/ppermute | solution.py:245
  13.5 1.2 %collective-permute-start.3 = (s32[2,4,90]{2,1,0:T(4,128)S(1)}, s32[2,4,90]{2,1,0:T(4,128)S(1)}, u32[]{:S(2)}, u32[]{:S(2)}) collective-permute-start(s32[2,4,90]{2,1,0:T(4,128)S(1)} %add_select_fusion.1), channel_id=1, source_target_pairs={{0,96},{16,112},{32,0},{48,16},{64,32},{80,48},{96,64},{112,80},{1... | collective-permute-start | bytes 8648 | tf_op jit(solution)/shard_map/ppermute | solution.py:245
  14.7 7.7 %collective-permute-done.1 = s32[2,4,90]{2,1,0:T(4,128)S(1)} collective-permute-done((s32[2,4,90]{2,1,0:T(4,128)S(1)}, s32[2,4,90]{2,1,0:T(4,128)S(1)}, u32[]{:S(2)}, u32[]{:S(2)}) %collective-permute-start.1) | collective-permute-done | bytes 2912 | tf_op jit(solution)/shard_map/ppermute | solution.py:245
  22.4 3.4 %collective-permute-done.2 = s32[2,4,90]{2,1,0:T(4,128)S(1)} collective-permute-done((s32[2,4,90]{2,1,0:T(4,128)S(1)}, s32[2,4,90]{2,1,0:T(4,128)S(1)}, u32[]{:S(2)}, u32[]{:S(2)}) %collective-permute-start.2) | collective-permute-done | bytes 2912 | tf_op jit(solution)/shard_map/ppermute | solution.py:245
  25.8 0.0 collective-permute-done.3
  25.8 0.1 copy.7
  25.9 0.1 reshape.79
  26.0 0.1 fusion.9
  26.1 0.3 collective-permute-start.4
  26.3 2.5 %collective-permute-start.6 = (bf16[3,360,256]{2,1,0:T(8,128)(2,1)}, bf16[3,360,256]{2,1,0:T(8,128)(2,1)}, u32[]{:S(2)}, u32[]{:S(2)}) collective-permute-start(bf16[3,360,256]{2,1,0:T(8,128)(2,1)} %get-tuple-element.15), channel_id=1, source_target_pairs={{0,96},{16,112},{32,0},{48,16},{64,32},{80,48},{96,64},{112,80},{1... | collective-permute-start | bytes 1658888 | tf_op jit(solution)/shard_map/ppermute | solution.py:265
  28.8 0.0 all-to-all-done.t_ref
  28.8 0.0 copy-start.1
  28.8 1.0 %copy-done.1 = f32[2048,64]{0,1:T(8,128)S(1)} copy-done((f32[2048,64]{0,1:T(8,128)S(1)}, f32[2048,64]{0,1:T(8,128)}, u32[]{:S(2)}) %copy-start.1) | copy-done | bytes 524312
  29.8 4.1 %shard_map.47 = f32[64,2048]{1,0:T(8,128)} custom-call(bf16[8,360,256]{2,1,0:T(8,128)(2,1)S(1)} %all-to-all-done.t_ref, f32[64,2048]{1,0:T(8,128)S(1)} %bitcast.27, f32[1,360]{1,0:T(1,128)S(1)} %broadcast_in_dim.23.w_ref), custom_call_target="tpu_custom_call" | custom-call | flops 566231040 | bytes 1998848 | tf_op jit(solution)/shard_map/pallas_call | solution.py:74
  34.0 9.0 %all-to-all-start.1 = ((f32[128,8,128]{2,1,0:T(8,128)}), f32[128,8,128]{2,1,0:T(8,128)S(1)}, u32[]{:S(2)}, u32[]{:S(2)}) async-start(f32[128,8,128]{2,1,0:T(8,128)} %bitcast.15), calls=%async_computation.1 | async-start | bytes 1048576 | tf_op jit(solution)/shard_map/all_to_all | solution.py:263
  43.0 0.0 collective-permute-done.4.refs_2_
  43.0 1.5 %collective-permute-start.5 = (bf16[1,360,256]{2,1,0:T(8,128)(2,1)S(1)}, bf16[1,360,256]{2,1,0:T(8,128)(2,1)S(1)}, u32[]{:S(2)}, u32[]{:S(2)}) collective-permute-start(bf16[1,360,256]{2,1,0:T(8,128)(2,1)S(1)} %get-tuple-element.26), channel_id=1, source_target_pairs={{0,32},{16,48},{32,64},{48,80},{64,96},{80,112},{96,0},{112,16},{1... | collective-permute-start | bytes 552968 | tf_op jit(solution)/shard_map/ppermute | solution.py:266
  44.5 0.0 collective-permute-done.6.refs_4_
  44.5 1.0 %fusion.17 = (bf16[1,360,256]{2,1,0:T(8,128)(2,1)S(1)}, bf16[1,360,256]{2,1,0:T(8,128)(2,1)S(1)}) fusion(bf16[3,360,256]{2,1,0:T(8,128)(2,1)} %collective-permute-done.6.refs_4_), kind=kLoop, calls=%fused_computation.37 | loop fusion | bytes 737280 | tf_op jit(solution)/shard_map/slice | solution.py:269
  45.5 1.4 %collective-permute-start.7 = (bf16[1,360,256]{2,1,0:T(8,128)(2,1)S(1)}, bf16[1,360,256]{2,1,0:T(8,128)(2,1)}, u32[]{:S(2)}, u32[]{:S(2)}) collective-permute-start(bf16[1,360,256]{2,1,0:T(8,128)(2,1)S(1)} %get-tuple-element.24), channel_id=1, source_target_pairs={{0,96},{16,112},{32,0},{48,16},{64,32},{80,48},{96,64},{112,80},{1... | collective-permute-start | bytes 552968 | tf_op jit(solution)/shard_map/ppermute | solution.py:267
  46.9 1.6 %collective-permute-start.8 = (bf16[1,360,256]{2,1,0:T(8,128)(2,1)S(1)}, bf16[1,360,256]{2,1,0:T(8,128)(2,1)S(1)}, u32[]{:S(2)}, u32[]{:S(2)}) collective-permute-start(bf16[1,360,256]{2,1,0:T(8,128)(2,1)S(1)} %get-tuple-element.25), channel_id=1, source_target_pairs={{0,16},{16,0},{32,48},{48,32},{64,80},{80,64},{96,112},{112,96},{1... | collective-permute-start | bytes 552968 | tf_op jit(solution)/shard_map/ppermute | solution.py:268
  48.5 0.0 collective-permute-start.9
  48.5 6.9 %collective-permute-done.5.refs_6_ = bf16[1,360,256]{2,1,0:T(8,128)(2,1)S(1)} collective-permute-done((bf16[1,360,256]{2,1,0:T(8,128)(2,1)S(1)}, bf16[1,360,256]{2,1,0:T(8,128)(2,1)S(1)}, u32[]{:S(2)}, u32[]{:S(2)}) %collective-permute-start.5) | collective-permute-done | bytes 184352 | tf_op jit(solution)/shard_map/ppermute | solution.py:266
  55.3 0.0 collective-permute-done.7
  55.3 0.0 collective-permute-done.8.refs_3_
  55.4 0.0 collective-permute-done.9.refs_5_
  55.4 1.8 %all-to-all-done.1.got_ref = f32[128,8,128]{2,1,0:T(8,128)S(1)} async-done(((f32[128,8,128]{2,1,0:T(8,128)}), f32[128,8,128]{2,1,0:T(8,128)S(1)}, u32[]{:S(2)}, u32[]{:S(2)}) %all-to-all-start.1) | async-done | bytes 524320 | tf_op jit(solution)/shard_map/all_to_all | solution.py:263
  57.2 0.9 %shard_map.48 = f32[128,8,128]{2,1,0:T(8,128)} custom-call(f32[128,8,128]{2,1,0:T(8,128)S(1)} %all-to-all-done.1.got_ref), custom_call_target="tpu_custom_call" | custom-call | flops 131072 | bytes 1048576 | tf_op jit(solution)/shard_map/pallas_call | solution.py:111
  58.0 6.8 %all-to-all-start.2 = ((f32[128,8,128]{2,1,0:T(8,128)}), f32[128,8,128]{2,1,0:T(8,128)S(1)}, u32[]{:S(2)}, u32[]{:S(2)}) async-start(f32[128,8,128]{2,1,0:T(8,128)} %shard_map.48), calls=%async_computation.2 | async-start | bytes 1048576 | tf_op jit(solution)/shard_map/all_to_all | solution.py:273
  64.8 1.1 %collective-permute-start.10 = (bf16[1,360,256]{2,1,0:T(8,128)(2,1)S(1)}, bf16[1,360,256]{2,1,0:T(8,128)(2,1)S(1)}, u32[]{:S(2)}, u32[]{:S(2)}) collective-permute-start(bf16[1,360,256]{2,1,0:T(8,128)(2,1)S(1)} %slice.40), channel_id=1, source_target_pairs={{0,16},{16,0},{32,48},{48,32},{64,80},{80,64},{96,112},{112,96},{1... | collective-permute-start | bytes 552968 | tf_op jit(solution)/shard_map/ppermute | solution.py:257
  66.0 0.1 collective-permute-start.11
  66.1 0.9 %collective-permute-done.10.refs_1_ = bf16[1,360,256]{2,1,0:T(8,128)(2,1)S(1)} collective-permute-done((bf16[1,360,256]{2,1,0:T(8,128)(2,1)S(1)}, bf16[1,360,256]{2,1,0:T(8,128)(2,1)S(1)}, u32[]{:S(2)}, u32[]{:S(2)}) %collective-permute-start.10) | collective-permute-done | bytes 184352 | tf_op jit(solution)/shard_map/ppermute | solution.py:257
  67.0 0.7 collective-permute-done.11.refs_7_
  67.7 2.2 %shard_map.49.z_ref = bf16[8,360,256]{2,1,0:T(8,128)(2,1)S(1)} custom-call(s32[8]{0:T(128)S(1)} %fusion.15.place_ref, bf16[2,360,256]{2,1,0:T(8,128)(2,1)S(1)} %slice.39.refs_0_, bf16[1,360,256]{2,1,0:T(8,128)(2,1)S(1)} %collective-permute-done.10.refs_1_, bf16[3,360,256]{2,1,0:T(8,128)(2,1)S(1)} %collective-permute-done.4.refs_2_, ...), custom_call_target="tpu_custom_call" | custom-call | bytes 11796480 | tf_op jit(solution)/shard_map/pallas_call | solution.py:171
  69.9 8.9 %all-to-all-done.2 = f32[128,8,128]{2,1,0:T(8,128)S(1)} async-done(((f32[128,8,128]{2,1,0:T(8,128)}), f32[128,8,128]{2,1,0:T(8,128)S(1)}, u32[]{:S(2)}, u32[]{:S(2)}) %all-to-all-start.2) | async-done | bytes 524320 | tf_op jit(solution)/shard_map/all_to_all | solution.py:273
  78.9 1.5 %shard_map.50 = f32[4,64,90]{2,1,0:T(8,128)} custom-call(f32[8,16,8,128]{3,2,1,0:T(8,128)S(1)} %bitcast.25, bf16[8,360,256]{2,1,0:T(8,128)(2,1)S(1)} %shard_map.49.z_ref, f32[4,90]{1,0:T(4,128)S(1)} %convert_multiply_fusion.factor_ref), custom_call_target="tpu_custom_call" | custom-call | flops 94371840 | bytes 1998848 | tf_op jit(solution)/shard_map/pallas_call | solution.py:209
  (13 shorter events, 0.1 us)
Async XLA Ops:
  0.0 5.9 %copy-start.2 = (s32[4,90]{1,0:T(4,128)S(1)}, s32[4,90]{1,0:T(4,128)}, u32[]{:S(2)}) copy-start(s32[4,90]{1,0:T(4,128)} %param.7) | copy-start | bytes 4324
  0.0 28.8 %all-to-all-start = ((bf16[8,360,256]{2,1,0:T(8,128)(2,1)}), bf16[8,360,256]{2,1,0:T(8,128)(2,1)S(1)}, u32[]{:S(2)}, u32[]{:S(2)}) async-start(bf16[8,360,256]{2,1,0:T(8,128)(2,1)} %bitcast.28), calls=%async_computation | async-start | bytes 2949120 | tf_op jit(solution)/shard_map/all_to_all | solution.py:239
  5.9 3.5 %collective-permute-start = (s32[4,90]{1,0:T(4,128)S(1)}, s32[4,90]{1,0:T(4,128)S(1)}, u32[]{:S(2)}, u32[]{:S(2)}) collective-permute-start(s32[4,90]{1,0:T(4,128)S(1)} %copy-done.2), channel_id=1, source_target_pairs={{0,16},{16,0},{32,48},{48,32},{64,80},{80,64},{96,112},{112,96},{1... | collective-permute-start | bytes 4328 | tf_op jit(solution)/shard_map/ppermute | solution.py:241
  6.0 1.4 %copy-start = (bf16[32,90,256]{2,0,1:T(8,128)(2,1)S(1)}, bf16[32,90,256]{2,0,1:T(8,128)(2,1)}, u32[]{:S(2)}) copy-start(bf16[32,90,256]{2,0,1:T(8,128)(2,1)} %param.5) | copy-start | bytes 4423684
  9.4 13.0 %collective-permute-start.1 = (s32[2,4,90]{2,1,0:T(4,128)S(1)}, s32[2,4,90]{2,1,0:T(4,128)S(1)}, u32[]{:S(2)}, u32[]{:S(2)}) collective-permute-start(s32[2,4,90]{2,1,0:T(4,128)S(1)} %add_select_fusion.1), channel_id=1, source_target_pairs={{0,32},{16,48},{32,64},{48,80},{64,96},{80,112},{96,0},{112,16},{1... | collective-permute-start | bytes 8648 | tf_op jit(solution)/shard_map/ppermute | solution.py:245
  11.1 14.6 %collective-permute-start.2 = (s32[2,4,90]{2,1,0:T(4,128)S(1)}, s32[2,4,90]{2,1,0:T(4,128)S(1)}, u32[]{:S(2)}, u32[]{:S(2)}) collective-permute-start(s32[2,4,90]{2,1,0:T(4,128)S(1)} %add_select_fusion.1), channel_id=1, source_target_pairs={{0,64},{16,80},{32,96},{48,112},{64,0},{80,16},{96,32},{112,48},{1... | collective-permute-start | bytes 8648 | tf_op jit(solution)/shard_map/ppermute | solution.py:245
  13.5 12.2 %collective-permute-start.3 = (s32[2,4,90]{2,1,0:T(4,128)S(1)}, s32[2,4,90]{2,1,0:T(4,128)S(1)}, u32[]{:S(2)}, u32[]{:S(2)}) collective-permute-start(s32[2,4,90]{2,1,0:T(4,128)S(1)} %add_select_fusion.1), channel_id=1, source_target_pairs={{0,96},{16,112},{32,0},{48,16},{64,32},{80,48},{96,64},{112,80},{1... | collective-permute-start | bytes 8648 | tf_op jit(solution)/shard_map/ppermute | solution.py:245
  26.1 16.9 %collective-permute-start.4 = (bf16[3,360,256]{2,1,0:T(8,128)(2,1)}, bf16[3,360,256]{2,1,0:T(8,128)(2,1)S(1)}, u32[]{:S(2)}, u32[]{:S(2)}) collective-permute-start(bf16[3,360,256]{2,1,0:T(8,128)(2,1)} %get-tuple-element.14), channel_id=1, source_target_pairs={{0,32},{16,48},{32,64},{48,80},{64,96},{80,112},{96,0},{112,16},{1... | collective-permute-start | bytes 1658888 | tf_op jit(solution)/shard_map/ppermute | solution.py:264
  26.3 18.1 %collective-permute-start.6 = (bf16[3,360,256]{2,1,0:T(8,128)(2,1)}, bf16[3,360,256]{2,1,0:T(8,128)(2,1)}, u32[]{:S(2)}, u32[]{:S(2)}) collective-permute-start(bf16[3,360,256]{2,1,0:T(8,128)(2,1)} %get-tuple-element.15), channel_id=1, source_target_pairs={{0,96},{16,112},{32,0},{48,16},{64,32},{80,48},{96,64},{112,80},{1... | collective-permute-start | bytes 1658888 | tf_op jit(solution)/shard_map/ppermute | solution.py:265
  28.8 1.0 %copy-start.1 = (f32[2048,64]{0,1:T(8,128)S(1)}, f32[2048,64]{0,1:T(8,128)}, u32[]{:S(2)}) copy-start(f32[2048,64]{0,1:T(8,128)} %param.6) | copy-start | bytes 1572868
  34.0 23.2 %all-to-all-start.1 = ((f32[128,8,128]{2,1,0:T(8,128)}), f32[128,8,128]{2,1,0:T(8,128)S(1)}, u32[]{:S(2)}, u32[]{:S(2)}) async-start(f32[128,8,128]{2,1,0:T(8,128)} %bitcast.15), calls=%async_computation.1 | async-start | bytes 1048576 | tf_op jit(solution)/shard_map/all_to_all | solution.py:263
  43.0 12.3 %collective-permute-start.5 = (bf16[1,360,256]{2,1,0:T(8,128)(2,1)S(1)}, bf16[1,360,256]{2,1,0:T(8,128)(2,1)S(1)}, u32[]{:S(2)}, u32[]{:S(2)}) collective-permute-start(bf16[1,360,256]{2,1,0:T(8,128)(2,1)S(1)} %get-tuple-element.26), channel_id=1, source_target_pairs={{0,32},{16,48},{32,64},{48,80},{64,96},{80,112},{96,0},{112,16},{1... | collective-permute-start | bytes 552968 | tf_op jit(solution)/shard_map/ppermute | solution.py:266
  45.5 9.8 %collective-permute-start.7 = (bf16[1,360,256]{2,1,0:T(8,128)(2,1)S(1)}, bf16[1,360,256]{2,1,0:T(8,128)(2,1)}, u32[]{:S(2)}, u32[]{:S(2)}) collective-permute-start(bf16[1,360,256]{2,1,0:T(8,128)(2,1)S(1)} %get-tuple-element.24), channel_id=1, source_target_pairs={{0,96},{16,112},{32,0},{48,16},{64,32},{80,48},{96,64},{112,80},{1... | collective-permute-start | bytes 552968 | tf_op jit(solution)/shard_map/ppermute | solution.py:267
  46.9 8.5 %collective-permute-start.8 = (bf16[1,360,256]{2,1,0:T(8,128)(2,1)S(1)}, bf16[1,360,256]{2,1,0:T(8,128)(2,1)S(1)}, u32[]{:S(2)}, u32[]{:S(2)}) collective-permute-start(bf16[1,360,256]{2,1,0:T(8,128)(2,1)S(1)} %get-tuple-element.25), channel_id=1, source_target_pairs={{0,16},{16,0},{32,48},{48,32},{64,80},{80,64},{96,112},{112,96},{1... | collective-permute-start | bytes 552968 | tf_op jit(solution)/shard_map/ppermute | solution.py:268
  48.5 6.9 %collective-permute-start.9 = (bf16[1,360,256]{2,1,0:T(8,128)(2,1)S(1)}, bf16[1,360,256]{2,1,0:T(8,128)(2,1)S(1)}, u32[]{:S(2)}, u32[]{:S(2)}) collective-permute-start(bf16[1,360,256]{2,1,0:T(8,128)(2,1)S(1)} %get-tuple-element.23), channel_id=1, source_target_pairs={{0,16},{16,0},{32,48},{48,32},{64,80},{80,64},{96,112},{112,96},{1... | collective-permute-start | bytes 552968 | tf_op jit(solution)/shard_map/ppermute | solution.py:269
  58.0 20.9 %all-to-all-start.2 = ((f32[128,8,128]{2,1,0:T(8,128)}), f32[128,8,128]{2,1,0:T(8,128)S(1)}, u32[]{:S(2)}, u32[]{:S(2)}) async-start(f32[128,8,128]{2,1,0:T(8,128)} %shard_map.48), calls=%async_computation.2 | async-start | bytes 1048576 | tf_op jit(solution)/shard_map/all_to_all | solution.py:273
  64.8 2.2 %collective-permute-start.10 = (bf16[1,360,256]{2,1,0:T(8,128)(2,1)S(1)}, bf16[1,360,256]{2,1,0:T(8,128)(2,1)S(1)}, u32[]{:S(2)}, u32[]{:S(2)}) collective-permute-start(bf16[1,360,256]{2,1,0:T(8,128)(2,1)S(1)} %slice.40), channel_id=1, source_target_pairs={{0,16},{16,0},{32,48},{48,32},{64,80},{80,64},{96,112},{112,96},{1... | collective-permute-start | bytes 552968 | tf_op jit(solution)/shard_map/ppermute | solution.py:257
  66.0 1.7 %collective-permute-start.11 = (bf16[1,360,256]{2,1,0:T(8,128)(2,1)}, bf16[1,360,256]{2,1,0:T(8,128)(2,1)S(1)}, u32[]{:S(2)}, u32[]{:S(2)}) collective-permute-start(bf16[1,360,256]{2,1,0:T(8,128)(2,1)} %collective-permute-done.7), channel_id=1, source_target_pairs={{0,16},{16,0},{32,48},{48,32},{64,80},{80,64},{96,112},{112,96},{1... | collective-permute-start | bytes 552968 | tf_op jit(solution)/shard_map/ppermute | solution.py:275

commit v5 on v4

--- a/solution.py
+++ b/solution.py
@@ -76,7 +76,7 @@
         out_shape=jax.ShapeDtypeStruct((modes, blocks * width), F32),
         in_specs=[
             pl.BlockSpec(memory_space=pltpu.VMEM),
-            pl.BlockSpec(memory_space=pl.ANY),
+            pl.BlockSpec(memory_space=pltpu.HBM),
             pl.BlockSpec(memory_space=pltpu.VMEM),
         ],
         scratch_shapes=[
@@ -238,8 +238,19 @@
     temp = thermal_reading.transpose(1, 0, 2).reshape(members, cells, width)
     temp = lax.all_to_all(temp, "tm", 0, 0)
 
+    band = jnp.arange(members, dtype=jnp.int32)
+    far = lax.rem(lax.div(band, 2) + chips - chip, chips)
+    slot = lax.rem(band + core, 2)
+    order = jnp.where(far == 0, 6 + slot, jnp.where(far == 1, slot, jnp.where(far == 2, 2 + 3 * slot, 3 + slot)))
+    laid = lay_out_bands(order, moisture_content.transpose(1, 0, 2))
+    ahead, behind, own = laid[0:3], laid[3:6], laid[6:8]
+    own_traded = lax.ppermute(own[1:2], "tm", to_core)
+
     other = lax.ppermute(marine_indicator, "tm", to_core)
     pair = jnp.where(core == 0, jnp.stack([marine_indicator, other]), jnp.stack([other, marine_indicator]))
+    pair, ahead, behind = lax.optimization_barrier((pair, ahead, behind))
+    from_back = lax.ppermute(ahead, "tm", to_chip[1])
+    from_front = lax.ppermute(behind, "tm", to_chip[chips - 1])
     whole = jnp.zeros((chips, 2, lats, lons), jnp.int32)
     for d in range(chips):
         got = pair if d == 0 else lax.ppermute(pair, "tm", to_chip[d])
@@ -248,21 +259,10 @@
     lat_of_cell = lax.rem(me * cells + jnp.arange(cells, dtype=jnp.int32), total_lat)
     weight = (area_root(lat_of_cell, total_lat) * sea.astype(F32))[None, :]
 
-    band = jnp.arange(members, dtype=jnp.int32)
-    far = lax.rem(lax.div(band, 2) + chips - chip, chips)
-    slot = lax.rem(band + core, 2)
-    order = jnp.where(far == 0, 6 + slot, jnp.where(far == 1, slot, jnp.where(far == 2, 2 + 3 * slot, 3 + slot)))
-    laid = lay_out_bands(order, moisture_content.transpose(1, 0, 2))
-    ahead, behind, own = laid[0:3], laid[3:6], laid[6:8]
-    own_traded = lax.ppermute(own[1:2], "tm", to_core)
-
-    weight, ahead, behind = lax.optimization_barrier((weight, ahead, behind))
     partial_t = temp_sums(temp, gram_eigenvector_columns.T, weight)
     blocks = partial_t.reshape(modes // 8, 8, hours // 128, 128)
     blocks = blocks.transpose(0, 2, 1, 3).reshape(-1, 8, 128)
     got = lax.all_to_all(blocks, BOTH, 0, 0)
-    from_back = lax.ppermute(ahead, "tm", to_chip[1])
-    from_front = lax.ppermute(behind, "tm", to_chip[chips - 1])
     far_first = lax.ppermute(from_back[2:3], "tm", to_chip[1])
     far_second = lax.ppermute(from_front[2:3], "tm", to_chip[chips - 1])
     back_traded = lax.ppermute(from_back[1:2], "tm", to_core)

time: 80.8 us -> 82.4 us (1.020)
  waiting for transfers between devices: 30.3 us -> 25.2 us
  local copies, waits for them, and re-layouts: 4.83 us -> 9.77 us
  starting transfers between devices: 35.5 us -> 36.4 us
    ppermute x3, waiting for transfers between devices: 11 us -> 6.6 us  [per_device(): got = pair if d == 0 else lax.ppermute(pair, 'tm', to_chip[d])]
    dynamic_update_slice x3 -> x4, local copies, waits for them, and re-layouts: 0.02 us -> 2.37 us  [per_device(): lax.dynamic_update_slice(whole, got[None], (lax.rem(chip + chips - d, chi...]
    unnamed x6 -> x8, local copies, waits for them, and re-layouts: 2.41 us -> 3.06 us
  transfers between devices with their start and end apart: 15 -> 15, of which waited for: 7 -> 7; matrix products, arithmetic and copies ran while one was open for 3% -> 9% of each run, Pallas kernels for 9% -> 9%
where the time goes in v5:
time: 82.4 us; the launch traced here: 81.9 us
  starting transfers between devices  36.4 us (44%)
  waiting for transfers between devices  25.2 us (31%)
  local copies, waits for them, and re-layouts  9.77 us (12%)
  Pallas kernels  9.59 us (12%)
    all_to_all x1, starting transfers between devices, per_device(): got = lax.all_to_all(blocks, BOTH, 0, 0)  9.39 us
    all_to_all x1, waiting for transfers between devices, per_device(): pcs = lax.all_to_all(sum_for_all(got), BOTH, 0, 0)  8.94 us
    all_to_all x1, starting transfers between devices, per_device(): pcs = lax.all_to_all(sum_for_all(got), BOTH, 0, 0)  7.31 us
    ppermute x1, waiting for transfers between devices, per_device(): far_first = lax.ppermute(from_back[2:3], 'tm', to_chip[1])  6.85 us
    ppermute x3, waiting for transfers between devices, per_device(): got = pair if d == 0 else lax.ppermute(pair, 'tm', to_chip[d])  6.6 us
    all_to_all x1, starting transfers between devices, per_device(): temp = lax.all_to_all(temp, 'tm', 0, 0)  5.93 us
    ppermute x3, starting transfers between devices, per_device(): got = pair if d == 0 else lax.ppermute(pair, 'tm', to_chip[d])  5.3 us
    pallas_call x1, Pallas kernels, temp_sums(): pl.pallas_call(temp_kernel, out_shape=jax.ShapeDtypeStruct((modes, blocks...  4.13 us
  transfers between devices with their start and end apart: 15, of which 7 were waited for; matrix products, arithmetic and copies ran while one was open for 9% of the time, Pallas kernels for 9%

profile of v5, /device:TPU:1, one launch (start us, length us, event | category | flops | bytes accessed | tf_op | source)
XLA Modules:
  0.0 81.9 jit_solution(2852288269834345702)
XLA Ops:
  0.0 0.0 copy-start.2
  0.0 5.9 %all-to-all-start = ((bf16[8,360,256]{2,1,0:T(8,128)(2,1)}), bf16[8,360,256]{2,1,0:T(8,128)(2,1)S(1)}, u32[]{:S(2)}, u32[]{:S(2)}) async-start(bf16[8,360,256]{2,1,0:T(8,128)(2,1)} %bitcast.28), calls=%async_computation | async-start | bytes 2949120 | tf_op jit(solution)/shard_map/all_to_all | solution.py:239
  5.9 0.0 copy-done.2
  5.9 0.1 collective-permute-start
  6.1 0.0 copy-start
  6.1 1.4 %copy-done = bf16[32,90,256]{2,0,1:T(8,128)(2,1)S(1)} copy-done((bf16[32,90,256]{2,0,1:T(8,128)(2,1)S(1)}, bf16[32,90,256]{2,0,1:T(8,128)(2,1)}, u32[]{:S(2)}) %copy-start) | copy-done | bytes 1474584
  7.4 0.9 %shard_map.46 = bf16[8,360,256]{2,1,0:T(8,128)(2,1)S(1)} custom-call(s32[8]{0:T(128)S(1)} %compare_select_fusion.10.place_ref, bf16[90,32,256]{2,1,0:T(8,128)(2,1)S(1)} %bitcast.26), custom_call_target="tpu_custom_call" | custom-call | bytes 2949120 | tf_op jit(solution)/shard_map/pallas_call | solution.py:138
  8.3 1.1 %fusion.15 = (bf16[3,360,256]{2,1,0:T(8,128)(2,1)}, bf16[3,360,256]{2,1,0:T(8,128)(2,1)}) fusion(bf16[8,360,256]{2,1,0:T(8,128)(2,1)S(1)} %shard_map.46), kind=kLoop, calls=%fused_computation.35 | loop fusion | bytes 2211840 | tf_op jit(solution)/shard_map/slice | solution.py:246
  9.4 0.0 collective-permute-done
  9.4 1.7 %collective-permute-start.1 = (s32[2,4,90]{2,1,0:T(4,128)S(1)}, s32[2,4,90]{2,1,0:T(4,128)S(1)}, u32[]{:S(2)}, u32[]{:S(2)}) collective-permute-start(s32[2,4,90]{2,1,0:T(4,128)S(1)} %add_select_fusion), channel_id=1, source_target_pairs={{0,32},{16,48},{32,64},{48,80},{64,96},{80,112},{96,0},{112,16},{1... | collective-permute-start | bytes 8648 | tf_op jit(solution)/shard_map/ppermute | solution.py:256
  11.2 2.4 %collective-permute-start.2 = (s32[2,4,90]{2,1,0:T(4,128)S(1)}, s32[2,4,90]{2,1,0:T(4,128)S(1)}, u32[]{:S(2)}, u32[]{:S(2)}) collective-permute-start(s32[2,4,90]{2,1,0:T(4,128)S(1)} %add_select_fusion), channel_id=1, source_target_pairs={{0,64},{16,80},{32,96},{48,112},{64,0},{80,16},{96,32},{112,48},{1... | collective-permute-start | bytes 8648 | tf_op jit(solution)/shard_map/ppermute | solution.py:256
  13.6 1.2 %collective-permute-start.3 = (s32[2,4,90]{2,1,0:T(4,128)S(1)}, s32[2,4,90]{2,1,0:T(4,128)S(1)}, u32[]{:S(2)}, u32[]{:S(2)}) collective-permute-start(s32[2,4,90]{2,1,0:T(4,128)S(1)} %add_select_fusion), channel_id=1, source_target_pairs={{0,96},{16,112},{32,0},{48,16},{64,32},{80,48},{96,64},{112,80},{1... | collective-permute-start | bytes 8648 | tf_op jit(solution)/shard_map/ppermute | solution.py:256
  14.7 0.3 collective-permute-start.4
  15.0 2.4 %collective-permute-start.6 = (bf16[3,360,256]{2,1,0:T(8,128)(2,1)}, bf16[3,360,256]{2,1,0:T(8,128)(2,1)}, u32[]{:S(2)}, u32[]{:S(2)}) collective-permute-start(bf16[3,360,256]{2,1,0:T(8,128)(2,1)} %get-tuple-element.15), channel_id=1, source_target_pairs={{0,96},{16,112},{32,0},{48,16},{64,32},{80,48},{96,64},{112,80},{1... | collective-permute-start | bytes 1658888 | tf_op jit(solution)/shard_map/ppermute | solution.py:253
  17.4 0.6 broadcast_in_dim.21
  18.0 0.6 bitcast_dynamic-update-slice_fusion.3
  18.6 3.8 %collective-permute-done.1 = s32[2,4,90]{2,1,0:T(4,128)S(1)} collective-permute-done((s32[2,4,90]{2,1,0:T(4,128)S(1)}, s32[2,4,90]{2,1,0:T(4,128)S(1)}, u32[]{:S(2)}, u32[]{:S(2)}) %collective-permute-start.1) | collective-permute-done | bytes 2912 | tf_op jit(solution)/shard_map/ppermute | solution.py:256
  22.4 0.6 bitcast_dynamic-update-slice_fusion.2
  23.0 2.8 %collective-permute-done.2 = s32[2,4,90]{2,1,0:T(4,128)S(1)} collective-permute-done((s32[2,4,90]{2,1,0:T(4,128)S(1)}, s32[2,4,90]{2,1,0:T(4,128)S(1)}, u32[]{:S(2)}, u32[]{:S(2)}) %collective-permute-start.2) | collective-permute-done | bytes 2912 | tf_op jit(solution)/shard_map/ppermute | solution.py:256
  25.8 0.6 bitcast_dynamic-update-slice_fusion.1
  26.4 0.0 collective-permute-done.3
  26.4 0.6 bitcast_dynamic-update-slice_fusion
  27.0 0.8 copy.7
  27.8 0.7 reshape.20
  28.5 0.8 fusion.8
  29.3 0.0 all-to-all-done.t_ref
  29.3 0.0 copy-start.1
  29.3 1.0 %copy-done.1 = f32[2048,64]{0,1:T(8,128)S(1)} copy-done((f32[2048,64]{0,1:T(8,128)S(1)}, f32[2048,64]{0,1:T(8,128)}, u32[]{:S(2)}) %copy-start.1) | copy-done | bytes 524312
  30.3 4.1 %shard_map.47 = f32[64,2048]{1,0:T(8,128)} custom-call(bf16[8,360,256]{2,1,0:T(8,128)(2,1)S(1)} %all-to-all-done.t_ref, f32[64,2048]{1,0:T(8,128)S(1)} %bitcast.27, f32[1,360]{1,0:T(1,128)S(1)} %broadcast_in_dim.26.w_ref), custom_call_target="tpu_custom_call" | custom-call | flops 566231040 | bytes 1998848 | tf_op jit(solution)/shard_map/pallas_call | solution.py:74
  34.5 9.4 %all-to-all-start.1 = ((f32[128,8,128]{2,1,0:T(8,128)}), f32[128,8,128]{2,1,0:T(8,128)S(1)}, u32[]{:S(2)}, u32[]{:S(2)}) async-start(f32[128,8,128]{2,1,0:T(8,128)} %bitcast.14), calls=%async_computation.1 | async-start | bytes 1048576 | tf_op jit(solution)/shard_map/all_to_all | solution.py:265
  43.9 0.0 collective-permute-done.4.refs_2_
  43.9 1.5 %collective-permute-start.5 = (bf16[1,360,256]{2,1,0:T(8,128)(2,1)S(1)}, bf16[1,360,256]{2,1,0:T(8,128)(2,1)S(1)}, u32[]{:S(2)}, u32[]{:S(2)}) collective-permute-start(bf16[1,360,256]{2,1,0:T(8,128)(2,1)S(1)} %get-tuple-element.26), channel_id=1, source_target_pairs={{0,32},{16,48},{32,64},{48,80},{64,96},{80,112},{96,0},{112,16},{1... | collective-permute-start | bytes 552968 | tf_op jit(solution)/shard_map/ppermute | solution.py:266
  45.4 0.0 collective-permute-done.6.refs_4_
  45.4 1.0 %fusion.16 = (bf16[1,360,256]{2,1,0:T(8,128)(2,1)S(1)}, bf16[1,360,256]{2,1,0:T(8,128)(2,1)S(1)}) fusion(bf16[3,360,256]{2,1,0:T(8,128)(2,1)} %collective-permute-done.6.refs_4_), kind=kLoop, calls=%fused_computation.36 | loop fusion | bytes 737280 | tf_op jit(solution)/shard_map/slice | solution.py:269
  46.4 1.4 %collective-permute-start.7 = (bf16[1,360,256]{2,1,0:T(8,128)(2,1)S(1)}, bf16[1,360,256]{2,1,0:T(8,128)(2,1)S(1)}, u32[]{:S(2)}, u32[]{:S(2)}) collective-permute-start(bf16[1,360,256]{2,1,0:T(8,128)(2,1)S(1)} %get-tuple-element.24), channel_id=1, source_target_pairs={{0,96},{16,112},{32,0},{48,16},{64,32},{80,48},{96,64},{112,80},{1... | collective-permute-start | bytes 552968 | tf_op jit(solution)/shard_map/ppermute | solution.py:267
  47.8 1.6 %collective-permute-start.8 = (bf16[1,360,256]{2,1,0:T(8,128)(2,1)S(1)}, bf16[1,360,256]{2,1,0:T(8,128)(2,1)S(1)}, u32[]{:S(2)}, u32[]{:S(2)}) collective-permute-start(bf16[1,360,256]{2,1,0:T(8,128)(2,1)S(1)} %get-tuple-element.25), channel_id=1, source_target_pairs={{0,16},{16,0},{32,48},{48,32},{64,80},{80,64},{96,112},{112,96},{1... | collective-permute-start | bytes 552968 | tf_op jit(solution)/shard_map/ppermute | solution.py:268
  49.4 0.0 collective-permute-start.9
  49.4 6.9 %collective-permute-done.5.refs_6_ = bf16[1,360,256]{2,1,0:T(8,128)(2,1)S(1)} collective-permute-done((bf16[1,360,256]{2,1,0:T(8,128)(2,1)S(1)}, bf16[1,360,256]{2,1,0:T(8,128)(2,1)S(1)}, u32[]{:S(2)}, u32[]{:S(2)}) %collective-permute-start.5) | collective-permute-done | bytes 184352 | tf_op jit(solution)/shard_map/ppermute | solution.py:266
  56.3 0.0 collective-permute-done.7
  56.3 0.0 copy-start.3
  56.3 0.0 collective-permute-done.8.refs_3_
  56.3 0.6 copy-done.3
  56.9 0.0 collective-permute-done.9.refs_5_
  56.9 1.1 %all-to-all-done.1.got_ref = f32[128,8,128]{2,1,0:T(8,128)S(1)} async-done(((f32[128,8,128]{2,1,0:T(8,128)}), f32[128,8,128]{2,1,0:T(8,128)S(1)}, u32[]{:S(2)}, u32[]{:S(2)}) %all-to-all-start.1) | async-done | bytes 524320 | tf_op jit(solution)/shard_map/all_to_all | solution.py:265
  58.1 0.9 %shard_map.48 = f32[128,8,128]{2,1,0:T(8,128)} custom-call(f32[128,8,128]{2,1,0:T(8,128)S(1)} %all-to-all-done.1.got_ref), custom_call_target="tpu_custom_call" | custom-call | flops 131072 | bytes 1048576 | tf_op jit(solution)/shard_map/pallas_call | solution.py:111
  58.9 7.3 %all-to-all-start.2 = ((f32[128,8,128]{2,1,0:T(8,128)}), f32[128,8,128]{2,1,0:T(8,128)S(1)}, u32[]{:S(2)}, u32[]{:S(2)}) async-start(f32[128,8,128]{2,1,0:T(8,128)} %shard_map.48), calls=%async_computation.2 | async-start | bytes 1048576 | tf_op jit(solution)/shard_map/all_to_all | solution.py:273
  66.3 1.1 %collective-permute-start.10 = (bf16[1,360,256]{2,1,0:T(8,128)(2,1)S(1)}, bf16[1,360,256]{2,1,0:T(8,128)(2,1)S(1)}, u32[]{:S(2)}, u32[]{:S(2)}) collective-permute-start(bf16[1,360,256]{2,1,0:T(8,128)(2,1)S(1)} %slice.40), channel_id=1, source_target_pairs={{0,16},{16,0},{32,48},{48,32},{64,80},{80,64},{96,112},{112,96},{1... | collective-permute-start | bytes 552968 | tf_op jit(solution)/shard_map/ppermute | solution.py:247
  67.5 0.1 collective-permute-start.11
  67.6 0.9 %collective-permute-done.10.refs_1_ = bf16[1,360,256]{2,1,0:T(8,128)(2,1)S(1)} collective-permute-done((bf16[1,360,256]{2,1,0:T(8,128)(2,1)S(1)}, bf16[1,360,256]{2,1,0:T(8,128)(2,1)S(1)}, u32[]{:S(2)}, u32[]{:S(2)}) %collective-permute-start.10) | collective-permute-done | bytes 184352 | tf_op jit(solution)/shard_map/ppermute | solution.py:247
  68.5 0.7 collective-permute-done.11.refs_7_
  69.2 2.2 %shard_map.49.z_ref = bf16[8,360,256]{2,1,0:T(8,128)(2,1)S(1)} custom-call(s32[8]{0:T(128)S(1)} %fusion.14.place_ref, bf16[2,360,256]{2,1,0:T(8,128)(2,1)S(1)} %slice.39.refs_0_, bf16[1,360,256]{2,1,0:T(8,128)(2,1)S(1)} %collective-permute-done.10.refs_1_, bf16[3,360,256]{2,1,0:T(8,128)(2,1)S(1)} %collective-permute-done.4.refs_2_, ...), custom_call_target="tpu_custom_call" | custom-call | bytes 11796480 | tf_op jit(solution)/shard_map/pallas_call | solution.py:171
  71.4 8.9 %all-to-all-done.2 = f32[128,8,128]{2,1,0:T(8,128)S(1)} async-done(((f32[128,8,128]{2,1,0:T(8,128)}), f32[128,8,128]{2,1,0:T(8,128)S(1)}, u32[]{:S(2)}, u32[]{:S(2)}) %all-to-all-start.2) | async-done | bytes 524320 | tf_op jit(solution)/shard_map/all_to_all | solution.py:273
  80.3 1.5 %shard_map.50 = f32[4,64,90]{2,1,0:T(8,128)} custom-call(f32[8,16,8,128]{3,2,1,0:T(8,128)S(1)} %bitcast.25, bf16[8,360,256]{2,1,0:T(8,128)(2,1)S(1)} %shard_map.49.z_ref, f32[4,90]{1,0:T(4,128)S(1)} %convert_multiply_fusion.factor_ref), custom_call_target="tpu_custom_call" | custom-call | flops 94371840 | bytes 1998848 | tf_op jit(solution)/shard_map/pallas_call | solution.py:209
  (8 shorter events, 0.1 us)
Async XLA Ops:
  0.0 5.9 %copy-start.2 = (s32[4,90]{1,0:T(4,128)S(1)}, s32[4,90]{1,0:T(4,128)}, u32[]{:S(2)}) copy-start(s32[4,90]{1,0:T(4,128)} %param.7) | copy-start | bytes 4324
  0.0 29.3 %all-to-all-start = ((bf16[8,360,256]{2,1,0:T(8,128)(2,1)}), bf16[8,360,256]{2,1,0:T(8,128)(2,1)S(1)}, u32[]{:S(2)}, u32[]{:S(2)}) async-start(bf16[8,360,256]{2,1,0:T(8,128)(2,1)} %bitcast.28), calls=%async_computation | async-start | bytes 2949120 | tf_op jit(solution)/shard_map/all_to_all | solution.py:239
  5.9 3.5 %collective-permute-start = (s32[4,90]{1,0:T(4,128)S(1)}, s32[4,90]{1,0:T(4,128)S(1)}, u32[]{:S(2)}, u32[]{:S(2)}) collective-permute-start(s32[4,90]{1,0:T(4,128)S(1)} %copy-done.2), channel_id=1, source_target_pairs={{0,16},{16,0},{32,48},{48,32},{64,80},{80,64},{96,112},{112,96},{1... | collective-permute-start | bytes 4328 | tf_op jit(solution)/shard_map/ppermute | solution.py:249
  6.1 1.4 %copy-start = (bf16[32,90,256]{2,0,1:T(8,128)(2,1)S(1)}, bf16[32,90,256]{2,0,1:T(8,128)(2,1)}, u32[]{:S(2)}) copy-start(bf16[32,90,256]{2,0,1:T(8,128)(2,1)} %param.5) | copy-start | bytes 4423684
  9.4 13.0 %collective-permute-start.1 = (s32[2,4,90]{2,1,0:T(4,128)S(1)}, s32[2,4,90]{2,1,0:T(4,128)S(1)}, u32[]{:S(2)}, u32[]{:S(2)}) collective-permute-start(s32[2,4,90]{2,1,0:T(4,128)S(1)} %add_select_fusion), channel_id=1, source_target_pairs={{0,32},{16,48},{32,64},{48,80},{64,96},{80,112},{96,0},{112,16},{1... | collective-permute-start | bytes 8648 | tf_op jit(solution)/shard_map/ppermute | solution.py:256
  11.2 14.7 %collective-permute-start.2 = (s32[2,4,90]{2,1,0:T(4,128)S(1)}, s32[2,4,90]{2,1,0:T(4,128)S(1)}, u32[]{:S(2)}, u32[]{:S(2)}) collective-permute-start(s32[2,4,90]{2,1,0:T(4,128)S(1)} %add_select_fusion), channel_id=1, source_target_pairs={{0,64},{16,80},{32,96},{48,112},{64,0},{80,16},{96,32},{112,48},{1... | collective-permute-start | bytes 8648 | tf_op jit(solution)/shard_map/ppermute | solution.py:256
  13.6 12.9 %collective-permute-start.3 = (s32[2,4,90]{2,1,0:T(4,128)S(1)}, s32[2,4,90]{2,1,0:T(4,128)S(1)}, u32[]{:S(2)}, u32[]{:S(2)}) collective-permute-start(s32[2,4,90]{2,1,0:T(4,128)S(1)} %add_select_fusion), channel_id=1, source_target_pairs={{0,96},{16,112},{32,0},{48,16},{64,32},{80,48},{96,64},{112,80},{1... | collective-permute-start | bytes 8648 | tf_op jit(solution)/shard_map/ppermute | solution.py:256
  14.7 29.1 %collective-permute-start.4 = (bf16[3,360,256]{2,1,0:T(8,128)(2,1)}, bf16[3,360,256]{2,1,0:T(8,128)(2,1)S(1)}, u32[]{:S(2)}, u32[]{:S(2)}) collective-permute-start(bf16[3,360,256]{2,1,0:T(8,128)(2,1)} %get-tuple-element.14), channel_id=1, source_target_pairs={{0,32},{16,48},{32,64},{48,80},{64,96},{80,112},{96,0},{112,16},{1... | collective-permute-start | bytes 1658888 | tf_op jit(solution)/shard_map/ppermute | solution.py:252
  15.0 30.3 %collective-permute-start.6 = (bf16[3,360,256]{2,1,0:T(8,128)(2,1)}, bf16[3,360,256]{2,1,0:T(8,128)(2,1)}, u32[]{:S(2)}, u32[]{:S(2)}) collective-permute-start(bf16[3,360,256]{2,1,0:T(8,128)(2,1)} %get-tuple-element.15), channel_id=1, source_target_pairs={{0,96},{16,112},{32,0},{48,16},{64,32},{80,48},{96,64},{112,80},{1... | collective-permute-start | bytes 1658888 | tf_op jit(solution)/shard_map/ppermute | solution.py:253
  29.3 1.0 %copy-start.1 = (f32[2048,64]{0,1:T(8,128)S(1)}, f32[2048,64]{0,1:T(8,128)}, u32[]{:S(2)}) copy-start(f32[2048,64]{0,1:T(8,128)} %param.6) | copy-start | bytes 1572868
  34.5 23.6 %all-to-all-start.1 = ((f32[128,8,128]{2,1,0:T(8,128)}), f32[128,8,128]{2,1,0:T(8,128)S(1)}, u32[]{:S(2)}, u32[]{:S(2)}) async-start(f32[128,8,128]{2,1,0:T(8,128)} %bitcast.14), calls=%async_computation.1 | async-start | bytes 1048576 | tf_op jit(solution)/shard_map/all_to_all | solution.py:265
  43.9 12.3 %collective-permute-start.5 = (bf16[1,360,256]{2,1,0:T(8,128)(2,1)S(1)}, bf16[1,360,256]{2,1,0:T(8,128)(2,1)S(1)}, u32[]{:S(2)}, u32[]{:S(2)}) collective-permute-start(bf16[1,360,256]{2,1,0:T(8,128)(2,1)S(1)} %get-tuple-element.26), channel_id=1, source_target_pairs={{0,32},{16,48},{32,64},{48,80},{64,96},{80,112},{96,0},{112,16},{1... | collective-permute-start | bytes 552968 | tf_op jit(solution)/shard_map/ppermute | solution.py:266
  46.4 9.8 %collective-permute-start.7 = (bf16[1,360,256]{2,1,0:T(8,128)(2,1)S(1)}, bf16[1,360,256]{2,1,0:T(8,128)(2,1)S(1)}, u32[]{:S(2)}, u32[]{:S(2)}) collective-permute-start(bf16[1,360,256]{2,1,0:T(8,128)(2,1)S(1)} %get-tuple-element.24), channel_id=1, source_target_pairs={{0,96},{16,112},{32,0},{48,16},{64,32},{80,48},{96,64},{112,80},{1... | collective-permute-start | bytes 552968 | tf_op jit(solution)/shard_map/ppermute | solution.py:267
  47.8 8.5 %collective-permute-start.8 = (bf16[1,360,256]{2,1,0:T(8,128)(2,1)S(1)}, bf16[1,360,256]{2,1,0:T(8,128)(2,1)S(1)}, u32[]{:S(2)}, u32[]{:S(2)}) collective-permute-start(bf16[1,360,256]{2,1,0:T(8,128)(2,1)S(1)} %get-tuple-element.25), channel_id=1, source_target_pairs={{0,16},{16,0},{32,48},{48,32},{64,80},{80,64},{96,112},{112,96},{1... | collective-permute-start | bytes 552968 | tf_op jit(solution)/shard_map/ppermute | solution.py:268
  49.4 7.5 %collective-permute-start.9 = (bf16[1,360,256]{2,1,0:T(8,128)(2,1)S(1)}, bf16[1,360,256]{2,1,0:T(8,128)(2,1)S(1)}, u32[]{:S(2)}, u32[]{:S(2)}) collective-permute-start(bf16[1,360,256]{2,1,0:T(8,128)(2,1)S(1)} %get-tuple-element.23), channel_id=1, source_target_pairs={{0,16},{16,0},{32,48},{48,32},{64,80},{80,64},{96,112},{112,96},{1... | collective-permute-start | bytes 552968 | tf_op jit(solution)/shard_map/ppermute | solution.py:269
  56.3 0.7 copy-start.3
  58.9 21.4 %all-to-all-start.2 = ((f32[128,8,128]{2,1,0:T(8,128)}), f32[128,8,128]{2,1,0:T(8,128)S(1)}, u32[]{:S(2)}, u32[]{:S(2)}) async-start(f32[128,8,128]{2,1,0:T(8,128)} %shard_map.48), calls=%async_computation.2 | async-start | bytes 1048576 | tf_op jit(solution)/shard_map/all_to_all | solution.py:273
  66.3 2.2 %collective-permute-start.10 = (bf16[1,360,256]{2,1,0:T(8,128)(2,1)S(1)}, bf16[1,360,256]{2,1,0:T(8,128)(2,1)S(1)}, u32[]{:S(2)}, u32[]{:S(2)}) collective-permute-start(bf16[1,360,256]{2,1,0:T(8,128)(2,1)S(1)} %slice.40), channel_id=1, source_target_pairs={{0,16},{16,0},{32,48},{48,32},{64,80},{80,64},{96,112},{112,96},{1... | collective-permute-start | bytes 552968 | tf_op jit(solution)/shard_map/ppermute | solution.py:247
  67.5 1.7 %collective-permute-start.11 = (bf16[1,360,256]{2,1,0:T(8,128)(2,1)}, bf16[1,360,256]{2,1,0:T(8,128)(2,1)S(1)}, u32[]{:S(2)}, u32[]{:S(2)}) collective-permute-start(bf16[1,360,256]{2,1,0:T(8,128)(2,1)} %copy-done.3), channel_id=1, source_target_pairs={{0,16},{16,0},{32,48},{48,32},{64,80},{80,64},{96,112},{112,96},{1... | collective-permute-start | bytes 552968 | tf_op jit(solution)/shard_map/ppermute | solution.py:275

commit v6 on v5

--- a/solution.py
+++ b/solution.py
@@ -11,6 +11,7 @@
 F32 = jnp.float32
 BF16 = jnp.bfloat16
 EPS = 1e-05
+PACK_VMEM = 56 * 1024 * 1024
 NT = (((1,), (1,)), ((), ()))
 NN = (((1,), (0,)), ((), ()))
 
@@ -31,7 +32,32 @@
     return high, middle, low
 
 
-def temp_kernel(t_ref, columns_ref, w_ref, out_ref, z_ref, e_ref, arrived):
+def pack_kernel(in_ref, out_ref, done):
+    halves, _, octets, _, _ = in_ref.shape
+    copies = []
+    for o in range(octets):
+        for h in range(halves):
+            copy = pltpu.make_async_copy(in_ref.at[h, :, o], out_ref.at[o, h], done.at[o * halves + h])
+            copy.start()
+            copies.append(copy)
+    for copy in copies:
+        copy.wait()
+
+
+def pack_octets(field):
+    halves, lons, octets, rows, width = field.shape
+    return pl.pallas_call(
+        pack_kernel,
+        in_specs=[pl.BlockSpec(memory_space=pl.ANY)],
+        out_specs=pl.BlockSpec(memory_space=pl.ANY),
+        out_shape=jax.ShapeDtypeStruct((octets, halves, lons, rows, width), field.dtype),
+        scratch_shapes=[pltpu.SemaphoreType.DMA((octets * halves,))],
+        compiler_params=pltpu.CompilerParams(vmem_limit_bytes=PACK_VMEM),
+        cost_estimate=pl.CostEstimate(flops=0, bytes_accessed=4 * field.size, transcendentals=0),
+    )(field)
+
+
+def temp_kernel(t_ref, columns_ref, w_ref, out_ref, z_ref, e_ref, sums_ref, arrived, stored):
     blocks, cells, width = t_ref.shape
     modes = out_ref.shape[0]
     hours = blocks * width
@@ -61,11 +87,16 @@
     turned = loadings.T
     turned = turned[:modes] + (turned[modes : 2 * modes] + turned[2 * modes :])
     stacked = jnp.concatenate(three_terms(turned), axis=0)
+    copies = []
     for b in range(blocks):
         sums = lax.dot_general(stacked, z_ref[b], NN, preferred_element_type=F32)
-        out_ref[:, b * width : (b + 1) * width] = sums[:modes] + (
-            sums[modes : 2 * modes] + sums[2 * modes :]
-        )
+        columns = slice(b * width, (b + 1) * width)
+        sums_ref[:, columns] = sums[:modes] + (sums[modes : 2 * modes] + sums[2 * modes :])
+        copy = pltpu.make_async_copy(sums_ref.at[:, columns], out_ref.at[:, columns], stored.at[b])
+        copy.start()
+        copies.append(copy)
+    for copy in copies:
+        copy.wait()
 
 
 def temp_sums(temp, columns_t, weight):
@@ -82,8 +113,11 @@
         scratch_shapes=[
             pltpu.VMEM((blocks, cells, width), BF16),
             pltpu.VMEM(columns_t.shape, F32),
+            pltpu.VMEM(columns_t.shape, F32),
             pltpu.SemaphoreType.DMA,
+            pltpu.SemaphoreType.DMA((blocks,)),
         ],
+        out_specs=pl.BlockSpec(memory_space=pl.ANY),
         compiler_params=params(),
         cost_estimate=pl.CostEstimate(
             flops=12 * cells * modes * blocks * width,
@@ -234,8 +268,9 @@
     to_chip = [[(n, (n + 2 * d) % members) for n in range(members)] for d in range(chips)]
     mask_float = marine_indicator.astype(F32)
 
-    cells = total_lat * lons // members
-    temp = thermal_reading.transpose(1, 0, 2).reshape(members, cells, width)
+    half = lons // 2
+    temp = thermal_reading.transpose(1, 0, 2).reshape(2, half, chips, 8, width)
+    temp = pack_octets(temp).reshape(members, 8 * half, width)
     temp = lax.all_to_all(temp, "tm", 0, 0)
 
     band = jnp.arange(members, dtype=jnp.int32)
@@ -251,13 +286,10 @@
     pair, ahead, behind = lax.optimization_barrier((pair, ahead, behind))
     from_back = lax.ppermute(ahead, "tm", to_chip[1])
     from_front = lax.ppermute(behind, "tm", to_chip[chips - 1])
-    whole = jnp.zeros((chips, 2, lats, lons), jnp.int32)
-    for d in range(chips):
-        got = pair if d == 0 else lax.ppermute(pair, "tm", to_chip[d])
-        whole = lax.dynamic_update_slice(whole, got[None], (lax.rem(chip + chips - d, chips), 0, 0, 0))
-    sea = lax.dynamic_slice(whole.reshape(total_lat, lons).T.reshape(-1), (me * cells,), (cells,))
-    lat_of_cell = lax.rem(me * cells + jnp.arange(cells, dtype=jnp.int32), total_lat)
-    weight = (area_root(lat_of_cell, total_lat) * sea.astype(F32))[None, :]
+    root = area_root(8 * chip + jnp.arange(8, dtype=jnp.int32), total_lat)
+    scaling = root[:, None] * pair.reshape(8, lons).astype(F32)
+    weight = lax.dynamic_slice(scaling.T, (core * half, 0), (half, 8)).reshape(1, 8 * half)
+    weight, own_traded = lax.optimization_barrier((weight, own_traded))
 
     partial_t = temp_sums(temp, gram_eigenvector_columns.T, weight)
     blocks = partial_t.reshape(modes // 8, 8, hours // 128, 128)
@@ -267,12 +299,12 @@
     far_second = lax.ppermute(from_front[2:3], "tm", to_chip[chips - 1])
     back_traded = lax.ppermute(from_back[1:2], "tm", to_core)
     front_traded = lax.ppermute(from_front[1:2], "tm", to_core)
-    got, far_first, far_second, back_traded, front_traded = lax.optimization_barrier(
-        (got, far_first, far_second, back_traded, front_traded)
+    far_traded = lax.ppermute(far_second, "tm", to_core)
+    got, far_first, far_traded, back_traded, front_traded = lax.optimization_barrier(
+        (got, far_first, far_traded, back_traded, front_traded)
     )
     pcs = lax.all_to_all(sum_for_all(got), BOTH, 0, 0)
     pcs = pcs.reshape(modes // 8, hours // 128, 8, 128)
-    far_traded = lax.ppermute(far_second, "tm", to_core)
 
     pieces = [own, own_traded, from_back, back_traded, from_front, front_traded, far_first, far_traded]
     step = lax.div(band, 2)

time: 82.4 us -> 125 us (1.52)
  Pallas kernels: 9.59 us -> 55.5 us
  waiting for transfers between devices: 25.2 us -> 32.1 us
  starting transfers between devices: 36.4 us -> 31.3 us
  local copies, waits for them, and re-layouts: 9.77 us -> 5.53 us
    pallas_call x0 -> x1, Pallas kernels: none -> 45.8 us  [pack_octets(): pl.pallas_call(pack_kernel, in_specs=[pl.BlockSpec(memory_space=pl.ANY)],...]
    all_to_all x1, waiting for transfers between devices: 0.01 us -> 10.8 us  [per_device(): temp = lax.all_to_all(temp, 'tm', 0, 0)]
    ppermute x3 -> x0, waiting for transfers between devices: 6.6 us -> none  [per_device(): got = pair if d == 0 else lax.ppermute(pair, 'tm', to_chip[d])]
    ppermute x1, waiting for transfers between devices: 0.01 us -> 6.4 us  [per_device(): far_second = lax.ppermute(from_front[2:3], 'tm', to_chip[chips - 1])]
    ppermute x1, waiting for transfers between devices: 6.85 us -> 0.55 us  [per_device(): far_first = lax.ppermute(from_back[2:3], 'tm', to_chip[1])]
    ppermute x3 -> x0, starting transfers between devices: 5.3 us -> none  [per_device(): got = pair if d == 0 else lax.ppermute(pair, 'tm', to_chip[d])]
    all_to_all x1, waiting for transfers between devices: 8.94 us -> 11.7 us  [per_device(): pcs = lax.all_to_all(sum_for_all(got), BOTH, 0, 0)]
    dynamic_update_slice x4 -> x0, local copies, waits for them, and re-layouts: 2.37 us -> none  [per_device(): lax.dynamic_update_slice(whole, got[None], (lax.rem(chip + chips - d, chi...]
  transfers between devices with their start and end apart: 15 -> 12, of which waited for: 7 -> 7; matrix products, arithmetic and copies ran while one was open for 9% -> 3% of each run, Pallas kernels for 9% -> 6%
where the time goes in v6:
time: 125 us
  Pallas kernels  55.5 us (44%)
  waiting for transfers between devices  32.1 us (26%)
  starting transfers between devices  31.3 us (25%)
  local copies, waits for them, and re-layouts  5.53 us (4%)
    pallas_call x1, Pallas kernels, pack_octets(): pl.pallas_call(pack_kernel, in_specs=[pl.BlockSpec(memory_space=pl.ANY)],...  45.8 us
    all_to_all x1, waiting for transfers between devices, per_device(): pcs = lax.all_to_all(sum_for_all(got), BOTH, 0, 0)  11.7 us
    all_to_all x1, waiting for transfers between devices, per_device(): temp = lax.all_to_all(temp, 'tm', 0, 0)  10.8 us
    all_to_all x1, starting transfers between devices, per_device(): got = lax.all_to_all(blocks, BOTH, 0, 0)  9.48 us
    all_to_all x1, starting transfers between devices, per_device(): pcs = lax.all_to_all(sum_for_all(got), BOTH, 0, 0)  8.08 us
    ppermute x1, waiting for transfers between devices, per_device(): far_second = lax.ppermute(from_front[2:3], 'tm', to_chip[chips - 1])  6.4 us
    all_to_all x1, starting transfers between devices, per_device(): temp = lax.all_to_all(temp, 'tm', 0, 0)  5.81 us
    pallas_call x1, Pallas kernels, temp_sums(): pl.pallas_call(temp_kernel, out_shape=jax.ShapeDtypeStruct((modes, blocks...  4.05 us
  transfers between devices with their start and end apart: 12, of which 7 were waited for; matrix products, arithmetic and copies ran while one was open for 3% of the time, Pallas kernels for 6%

profile of v6, /device:TPU:1, one launch (start us, length us, event | category | flops | bytes accessed | tf_op | source)
XLA Modules:
  0.0 124.7 jit_solution(7325602746420639997)
XLA Ops:
  0.0 45.8 %shard_map.46 = bf16[4,2,45,8,256]{4,3,2,1,0:T(8,128)(2,1)} custom-call(bf16[2,45,4,8,256]{4,3,2,1,0:T(8,128)(2,1)} %bitcast.22), custom_call_target="tpu_custom_call" | custom-call | bytes 2949120 | tf_op jit(solution)/shard_map/pallas_call | solution.py:49
  45.8 0.0 copy-start.2
  45.9 5.8 %all-to-all-start = ((bf16[8,360,256]{2,1,0:T(8,128)(2,1)}), bf16[8,360,256]{2,1,0:T(8,128)(2,1)S(1)}, u32[]{:S(2)}, u32[]{:S(2)}) async-start(bf16[8,360,256]{2,1,0:T(8,128)(2,1)} %bitcast.21), calls=%async_computation | async-start | bytes 2949120 | tf_op jit(solution)/shard_map/all_to_all | solution.py:274
  51.7 0.0 copy-done.2
  51.7 0.1 collective-permute-start
  51.8 0.0 copy-start
  51.8 1.4 %copy-done = bf16[32,90,256]{2,0,1:T(8,128)(2,1)S(1)} copy-done((bf16[32,90,256]{2,0,1:T(8,128)(2,1)S(1)}, bf16[32,90,256]{2,0,1:T(8,128)(2,1)}, u32[]{:S(2)}) %copy-start) | copy-done | bytes 1474584
  53.2 0.9 shard_map.47
  54.0 1.1 fusion.6
  55.1 0.0 collective-permute-done
  55.1 2.9 %collective-permute-start.4 = (bf16[3,360,256]{2,1,0:T(8,128)(2,1)}, bf16[3,360,256]{2,1,0:T(8,128)(2,1)S(1)}, u32[]{:S(2)}, u32[]{:S(2)}) collective-permute-start(bf16[3,360,256]{2,1,0:T(8,128)(2,1)} %get-tuple-element.18), channel_id=1, source_target_pairs={{0,96},{16,112},{32,0},{48,16},{64,32},{80,48},{96,64},{112,80},{1... | collective-permute-start | bytes 1658888 | tf_op jit(solution)/shard_map/ppermute | solution.py:288
  58.1 0.7 slice.35
  58.7 0.4 collective-permute-start.1
  59.3 0.1 collective-permute-start.2
  59.3 0.1 broadcast_multiply_fusion
  59.4 0.1 dynamic-slice_bitcast_fusion
  59.5 0.1 copy.7
  59.6 0.1 reshape.33.w_ref
  59.7 0.9 collective-permute-done.1.refs_1_
  60.6 10.8 %all-to-all-done.t_ref = bf16[8,360,256]{2,1,0:T(8,128)(2,1)S(1)} async-done(((bf16[8,360,256]{2,1,0:T(8,128)(2,1)}), bf16[8,360,256]{2,1,0:T(8,128)(2,1)S(1)}, u32[]{:S(2)}, u32[]{:S(2)}) %all-to-all-start) | async-done | bytes 1474592 | tf_op jit(solution)/shard_map/all_to_all | solution.py:274
  71.4 0.0 copy-start.1
  71.4 1.0 copy-done.1
  72.4 4.1 %shard_map.48 = f32[64,2048]{1,0:T(8,128)} custom-call(bf16[8,360,256]{2,1,0:T(8,128)(2,1)S(1)} %all-to-all-done.t_ref, f32[64,2048]{1,0:T(8,128)S(1)} %bitcast.20, f32[1,360]{1,0:T(1,128)S(1)} %reshape.33.w_ref), custom_call_target="tpu_custom_call" | custom-call | flops 566231040 | bytes 1998848 | tf_op jit(solution)/shard_map/pallas_call | solution.py:105
  76.5 9.5 %all-to-all-start.1 = ((f32[128,8,128]{2,1,0:T(8,128)}), f32[128,8,128]{2,1,0:T(8,128)S(1)}, u32[]{:S(2)}, u32[]{:S(2)}) async-start(f32[128,8,128]{2,1,0:T(8,128)} %bitcast.11), calls=%async_computation.1 | async-start | bytes 1048576 | tf_op jit(solution)/shard_map/all_to_all | solution.py:297
  86.0 0.0 collective-permute-done.4.refs_4_
  86.0 2.7 %collective-permute-start.5 = (bf16[1,360,256]{2,1,0:T(8,128)(2,1)S(1)}, bf16[1,360,256]{2,1,0:T(8,128)(2,1)S(1)}, u32[]{:S(2)}, u32[]{:S(2)}) collective-permute-start(bf16[1,360,256]{2,1,0:T(8,128)(2,1)S(1)} %get-tuple-element.28), channel_id=1, source_target_pairs={{0,96},{16,112},{32,0},{48,16},{64,32},{80,48},{96,64},{112,80},{1... | collective-permute-start | bytes 552968 | tf_op jit(solution)/shard_map/ppermute | solution.py:299
  88.7 0.0 collective-permute-done.2.refs_2_
  88.7 1.0 fusion.8
  89.7 0.1 collective-permute-start.3
  89.8 0.7 collective-permute-start.7
  90.5 0.1 collective-permute-start.8
  90.6 6.4 %collective-permute-done.5 = bf16[1,360,256]{2,1,0:T(8,128)(2,1)S(1)} collective-permute-done((bf16[1,360,256]{2,1,0:T(8,128)(2,1)S(1)}, bf16[1,360,256]{2,1,0:T(8,128)(2,1)S(1)}, u32[]{:S(2)}, u32[]{:S(2)}) %collective-permute-start.5) | collective-permute-done | bytes 184352 | tf_op jit(solution)/shard_map/ppermute | solution.py:299
  97.0 0.9 collective-permute-start.6
  97.9 0.5 collective-permute-done.3.refs_6_
  98.5 0.0 collective-permute-done.7.refs_3_
  98.5 0.0 collective-permute-done.8.refs_5_
  98.5 0.5 collective-permute-done.6.refs_7_
  99.0 1.2 all-to-all-done.1.got_ref
  100.2 0.9 shard_map.49
  101.0 8.1 %all-to-all-start.2 = ((f32[128,8,128]{2,1,0:T(8,128)}), f32[128,8,128]{2,1,0:T(8,128)S(1)}, u32[]{:S(2)}, u32[]{:S(2)}) async-start(f32[128,8,128]{2,1,0:T(8,128)} %shard_map.49), calls=%async_computation.2 | async-start | bytes 1048576 | tf_op jit(solution)/shard_map/all_to_all | solution.py:306
  109.2 2.3 %shard_map.50.z_ref = bf16[8,360,256]{2,1,0:T(8,128)(2,1)S(1)} custom-call(s32[8]{0:T(128)S(1)} %fusion.5.place_ref, bf16[2,360,256]{2,1,0:T(8,128)(2,1)S(1)} %slice.40.refs_0_, bf16[1,360,256]{2,1,0:T(8,128)(2,1)} %collective-permute-done.1.refs_1_, bf16[3,360,256]{2,1,0:T(8,128)(2,1)} %collective-permute-done.2.refs_2_, ...), custom_call_target="tpu_custom_call" | custom-call | bytes 11796480 | tf_op jit(solution)/shard_map/pallas_call | solution.py:205
  111.5 11.7 %all-to-all-done.2 = f32[128,8,128]{2,1,0:T(8,128)S(1)} async-done(((f32[128,8,128]{2,1,0:T(8,128)}), f32[128,8,128]{2,1,0:T(8,128)S(1)}, u32[]{:S(2)}, u32[]{:S(2)}) %all-to-all-start.2) | async-done | bytes 524320 | tf_op jit(solution)/shard_map/all_to_all | solution.py:306
  123.2 1.5 %shard_map.51 = f32[4,64,90]{2,1,0:T(8,128)} custom-call(f32[8,16,8,128]{3,2,1,0:T(8,128)S(1)} %bitcast.18, bf16[8,360,256]{2,1,0:T(8,128)(2,1)S(1)} %shard_map.50.z_ref, f32[4,90]{1,0:T(4,128)S(1)} %convert_multiply_fusion.factor_ref), custom_call_target="tpu_custom_call" | custom-call | flops 94371840 | bytes 1998848 | tf_op jit(solution)/shard_map/pallas_call | solution.py:243
  (8 shorter events, 0.1 us)
Async XLA Ops:
  45.8 5.8 %copy-start.2 = (s32[4,90]{1,0:T(4,128)S(1)}, s32[4,90]{1,0:T(4,128)}, u32[]{:S(2)}) copy-start(s32[4,90]{1,0:T(4,128)} %param.7) | copy-start | bytes 4324
  45.9 25.5 %all-to-all-start = ((bf16[8,360,256]{2,1,0:T(8,128)(2,1)}), bf16[8,360,256]{2,1,0:T(8,128)(2,1)S(1)}, u32[]{:S(2)}, u32[]{:S(2)}) async-start(bf16[8,360,256]{2,1,0:T(8,128)(2,1)} %bitcast.21), calls=%async_computation | async-start | bytes 2949120 | tf_op jit(solution)/shard_map/all_to_all | solution.py:274
  51.7 3.4 %collective-permute-start = (s32[4,90]{1,0:T(4,128)S(1)}, s32[4,90]{1,0:T(4,128)S(1)}, u32[]{:S(2)}, u32[]{:S(2)}) collective-permute-start(s32[4,90]{1,0:T(4,128)S(1)} %copy-done.2), channel_id=1, source_target_pairs={{0,16},{16,0},{32,48},{48,32},{64,80},{80,64},{96,112},{112,96},{1... | collective-permute-start | bytes 4328 | tf_op jit(solution)/shard_map/ppermute | solution.py:284
  51.8 1.4 %copy-start = (bf16[32,90,256]{2,0,1:T(8,128)(2,1)S(1)}, bf16[32,90,256]{2,0,1:T(8,128)(2,1)}, u32[]{:S(2)}) copy-start(bf16[32,90,256]{2,0,1:T(8,128)(2,1)} %param.5) | copy-start | bytes 4423684
  55.1 30.9 %collective-permute-start.4 = (bf16[3,360,256]{2,1,0:T(8,128)(2,1)}, bf16[3,360,256]{2,1,0:T(8,128)(2,1)S(1)}, u32[]{:S(2)}, u32[]{:S(2)}) collective-permute-start(bf16[3,360,256]{2,1,0:T(8,128)(2,1)} %get-tuple-element.18), channel_id=1, source_target_pairs={{0,96},{16,112},{32,0},{48,16},{64,32},{80,48},{96,64},{112,80},{1... | collective-permute-start | bytes 1658888 | tf_op jit(solution)/shard_map/ppermute | solution.py:288
  58.7 1.8 %collective-permute-start.1 = (bf16[1,360,256]{2,1,0:T(8,128)(2,1)}, bf16[1,360,256]{2,1,0:T(8,128)(2,1)}, u32[]{:S(2)}, u32[]{:S(2)}) collective-permute-start(bf16[1,360,256]{2,1,0:T(8,128)(2,1)} %slice.35), channel_id=1, source_target_pairs={{0,16},{16,0},{32,48},{48,32},{64,80},{80,64},{96,112},{112,96},{1... | collective-permute-start | bytes 552968 | tf_op jit(solution)/shard_map/ppermute | solution.py:282
  59.3 29.4 %collective-permute-start.2 = (bf16[3,360,256]{2,1,0:T(8,128)(2,1)}, bf16[3,360,256]{2,1,0:T(8,128)(2,1)}, u32[]{:S(2)}, u32[]{:S(2)}) collective-permute-start(bf16[3,360,256]{2,1,0:T(8,128)(2,1)} %get-tuple-element.17), channel_id=1, source_target_pairs={{0,32},{16,48},{32,64},{48,80},{64,96},{80,112},{96,0},{112,16},{1... | collective-permute-start | bytes 1658888 | tf_op jit(solution)/shard_map/ppermute | solution.py:287
  71.4 1.0 copy-start.1
  76.5 23.7 %all-to-all-start.1 = ((f32[128,8,128]{2,1,0:T(8,128)}), f32[128,8,128]{2,1,0:T(8,128)S(1)}, u32[]{:S(2)}, u32[]{:S(2)}) async-start(f32[128,8,128]{2,1,0:T(8,128)} %bitcast.11), calls=%async_computation.1 | async-start | bytes 1048576 | tf_op jit(solution)/shard_map/all_to_all | solution.py:297
  86.0 11.0 %collective-permute-start.5 = (bf16[1,360,256]{2,1,0:T(8,128)(2,1)S(1)}, bf16[1,360,256]{2,1,0:T(8,128)(2,1)S(1)}, u32[]{:S(2)}, u32[]{:S(2)}) collective-permute-start(bf16[1,360,256]{2,1,0:T(8,128)(2,1)S(1)} %get-tuple-element.28), channel_id=1, source_target_pairs={{0,96},{16,112},{32,0},{48,16},{64,32},{80,48},{96,64},{112,80},{1... | collective-permute-start | bytes 552968 | tf_op jit(solution)/shard_map/ppermute | solution.py:299
  89.7 8.7 %collective-permute-start.3 = (bf16[1,360,256]{2,1,0:T(8,128)(2,1)S(1)}, bf16[1,360,256]{2,1,0:T(8,128)(2,1)S(1)}, u32[]{:S(2)}, u32[]{:S(2)}) collective-permute-start(bf16[1,360,256]{2,1,0:T(8,128)(2,1)S(1)} %get-tuple-element.30), channel_id=1, source_target_pairs={{0,32},{16,48},{32,64},{48,80},{64,96},{80,112},{96,0},{112,16},{1... | collective-permute-start | bytes 552968 | tf_op jit(solution)/shard_map/ppermute | solution.py:298
  89.8 8.6 %collective-permute-start.7 = (bf16[1,360,256]{2,1,0:T(8,128)(2,1)S(1)}, bf16[1,360,256]{2,1,0:T(8,128)(2,1)S(1)}, u32[]{:S(2)}, u32[]{:S(2)}) collective-permute-start(bf16[1,360,256]{2,1,0:T(8,128)(2,1)S(1)} %get-tuple-element.29), channel_id=1, source_target_pairs={{0,16},{16,0},{32,48},{48,32},{64,80},{80,64},{96,112},{112,96},{1... | collective-permute-start | bytes 552968 | tf_op jit(solution)/shard_map/ppermute | solution.py:300
  90.5 7.9 %collective-permute-start.8 = (bf16[1,360,256]{2,1,0:T(8,128)(2,1)S(1)}, bf16[1,360,256]{2,1,0:T(8,128)(2,1)S(1)}, u32[]{:S(2)}, u32[]{:S(2)}) collective-permute-start(bf16[1,360,256]{2,1,0:T(8,128)(2,1)S(1)} %get-tuple-element.27), channel_id=1, source_target_pairs={{0,16},{16,0},{32,48},{48,32},{64,80},{80,64},{96,112},{112,96},{1... | collective-permute-start | bytes 552968 | tf_op jit(solution)/shard_map/ppermute | solution.py:301
  97.0 1.9 %collective-permute-start.6 = (bf16[1,360,256]{2,1,0:T(8,128)(2,1)S(1)}, bf16[1,360,256]{2,1,0:T(8,128)(2,1)S(1)}, u32[]{:S(2)}, u32[]{:S(2)}) collective-permute-start(bf16[1,360,256]{2,1,0:T(8,128)(2,1)S(1)} %collective-permute-done.5), channel_id=1, source_target_pairs={{0,16},{16,0},{32,48},{48,32},{64,80},{80,64},{96,112},{112,96},{1... | collective-permute-start | bytes 552968 | tf_op jit(solution)/shard_map/ppermute | solution.py:302
  101.0 22.2 %all-to-all-start.2 = ((f32[128,8,128]{2,1,0:T(8,128)}), f32[128,8,128]{2,1,0:T(8,128)S(1)}, u32[]{:S(2)}, u32[]{:S(2)}) async-start(f32[128,8,128]{2,1,0:T(8,128)} %shard_map.49), calls=%async_computation.2 | async-start | bytes 1048576 | tf_op jit(solution)/shard_map/all_to_all | solution.py:306

commit v7 on v5

--- a/solution.py
+++ b/solution.py
@@ -11,6 +11,7 @@
 F32 = jnp.float32
 BF16 = jnp.bfloat16
 EPS = 1e-05
+PACK_VMEM = 56 * 1024 * 1024
 NT = (((1,), (1,)), ((), ()))
 NN = (((1,), (0,)), ((), ()))
 
@@ -31,12 +32,62 @@
     return high, middle, low
 
 
-def temp_kernel(t_ref, columns_ref, w_ref, out_ref, z_ref, e_ref, arrived):
+def pack_kernel(in_ref, out_ref, held, loaded, stored):
+    halves, _, octets, _, _ = in_ref.shape
+    places = [(o, h) for o in range(octets) for h in range(halves)]
+    loads = [
+        pltpu.make_async_copy(in_ref.at[h, :, o], held.at[o, h], loaded.at[n])
+        for n, (o, h) in enumerate(places)
+    ]
+    stores = [
+        pltpu.make_async_copy(held.at[o, h], out_ref.at[o, h], stored.at[n])
+        for n, (o, h) in enumerate(places)
+    ]
+    for load in loads:
+        load.start()
+    for load, store in zip(loads, stores):
+        load.wait()
+        store.start()
+    for store in stores:
+        store.wait()
+
+
+def pack_octets(field):
+    halves, lons, octets, rows, width = field.shape
+    shape = (octets, halves, lons, rows, width)
+    return pl.pallas_call(
+        pack_kernel,
+        in_specs=[pl.BlockSpec(memory_space=pl.ANY)],
+        out_specs=pl.BlockSpec(memory_space=pl.ANY),
+        out_shape=jax.ShapeDtypeStruct(shape, field.dtype),
+        scratch_shapes=[
+            pltpu.VMEM(shape, field.dtype),
+            pltpu.SemaphoreType.DMA((octets * halves,)),
+            pltpu.SemaphoreType.DMA((octets * halves,)),
+        ],
+        compiler_params=pltpu.CompilerParams(vmem_limit_bytes=PACK_VMEM),
+        cost_estimate=pl.CostEstimate(flops=0, bytes_accessed=4 * field.size, transcendentals=0),
+    )(field)
+
+
+def split_kernel(modes, e_ref, out_ref):
+    for n, term in enumerate(three_terms(e_ref[...])):
+        out_ref[n * modes : (n + 1) * modes, :] = term
+
+
+def split_columns(columns_t):
+    modes, hours = columns_t.shape
+    return pl.pallas_call(
+        lambda e_ref, out_ref: split_kernel(modes, e_ref, out_ref),
+        out_shape=jax.ShapeDtypeStruct((3 * modes, hours), BF16),
+        compiler_params=params(),
+        cost_estimate=pl.CostEstimate(flops=0, bytes_accessed=5 * modes * hours * 2, transcendentals=0),
+    )(columns_t)
+
+
+def scores_kernel(t_ref, w_ref, z_ref):
     blocks, cells, width = t_ref.shape
-    modes = out_ref.shape[0]
     hours = blocks * width
-    fetch = pltpu.make_async_copy(columns_ref, e_ref, arrived)
-    fetch.start()
     weights = jnp.broadcast_to(w_ref[...], (128, cells)).T
     for start, size in row_chunks(cells, 48):
         rows = slice(start, start + size)
@@ -53,11 +104,16 @@
         for b in range(blocks):
             centered = t_ref[b, rows, :].astype(F32) - average
             z_ref[b, rows, :] = ((centered * scale) * weight).astype(BF16)
-    fetch.wait()
+
+
+def sums_kernel(z_ref, e_ref, out_ref):
+    blocks, cells, width = z_ref.shape
+    modes = out_ref.shape[0]
     loadings = jnp.zeros((cells, 3 * modes), F32)
     for b in range(blocks):
-        columns = jnp.concatenate(three_terms(e_ref[:, b * width : (b + 1) * width]), axis=0)
-        loadings = loadings + lax.dot_general(z_ref[b], columns, NT, preferred_element_type=F32)
+        loadings = loadings + lax.dot_general(
+            z_ref[b], e_ref[:, b * width : (b + 1) * width], NT, preferred_element_type=F32
+        )
     turned = loadings.T
     turned = turned[:modes] + (turned[modes : 2 * modes] + turned[2 * modes :])
     stacked = jnp.concatenate(three_terms(turned), axis=0)
@@ -68,29 +124,27 @@
         )
 
 
-def temp_sums(temp, columns_t, weight):
+def temp_sums(temp, split, weight):
     blocks, cells, width = temp.shape
-    modes = columns_t.shape[0]
-    return pl.pallas_call(
-        temp_kernel,
+    modes = split.shape[0] // 3
+    scores = pl.pallas_call(
+        scores_kernel,
+        out_shape=jax.ShapeDtypeStruct(temp.shape, BF16),
+        compiler_params=params(),
+        cost_estimate=pl.CostEstimate(
+            flops=16 * temp.size, bytes_accessed=4 * temp.size, transcendentals=cells
+        ),
+    )(temp, weight)
+    return pl.pallas_call(
+        sums_kernel,
         out_shape=jax.ShapeDtypeStruct((modes, blocks * width), F32),
-        in_specs=[
-            pl.BlockSpec(memory_space=pltpu.VMEM),
-            pl.BlockSpec(memory_space=pltpu.HBM),
-            pl.BlockSpec(memory_space=pltpu.VMEM),
-        ],
-        scratch_shapes=[
-            pltpu.VMEM((blocks, cells, width), BF16),
-            pltpu.VMEM(columns_t.shape, F32),
-            pltpu.SemaphoreType.DMA,
-        ],
         compiler_params=params(),
         cost_estimate=pl.CostEstimate(
             flops=12 * cells * modes * blocks * width,
-            bytes_accessed=2 * temp.size + 4 * columns_t.size,
-            transcendentals=cells,
+            bytes_accessed=2 * temp.size + 2 * split.size,
+            transcendentals=0,
         ),
-    )(temp, columns_t, weight)
+    )(scores, split)
 
 
 def sum_kernel(got_ref, out_ref):
@@ -234,8 +288,9 @@
     to_chip = [[(n, (n + 2 * d) % members) for n in range(members)] for d in range(chips)]
     mask_float = marine_indicator.astype(F32)
 
-    cells = total_lat * lons // members
-    temp = thermal_reading.transpose(1, 0, 2).reshape(members, cells, width)
+    half = lons // 2
+    temp = thermal_reading.transpose(1, 0, 2).reshape(2, half, chips, 8, width)
+    temp = pack_octets(temp).reshape(members, 8 * half, width)
     temp = lax.all_to_all(temp, "tm", 0, 0)
 
     band = jnp.arange(members, dtype=jnp.int32)
@@ -251,15 +306,11 @@
     pair, ahead, behind = lax.optimization_barrier((pair, ahead, behind))
     from_back = lax.ppermute(ahead, "tm", to_chip[1])
     from_front = lax.ppermute(behind, "tm", to_chip[chips - 1])
-    whole = jnp.zeros((chips, 2, lats, lons), jnp.int32)
-    for d in range(chips):
-        got = pair if d == 0 else lax.ppermute(pair, "tm", to_chip[d])
-        whole = lax.dynamic_update_slice(whole, got[None], (lax.rem(chip + chips - d, chips), 0, 0, 0))
-    sea = lax.dynamic_slice(whole.reshape(total_lat, lons).T.reshape(-1), (me * cells,), (cells,))
-    lat_of_cell = lax.rem(me * cells + jnp.arange(cells, dtype=jnp.int32), total_lat)
-    weight = (area_root(lat_of_cell, total_lat) * sea.astype(F32))[None, :]
-
-    partial_t = temp_sums(temp, gram_eigenvector_columns.T, weight)
+    root = area_root(8 * chip + jnp.arange(8, dtype=jnp.int32), total_lat)
+    scaling = root[:, None] * pair.reshape(8, lons).astype(F32)
+    weight = lax.dynamic_slice(scaling.T, (core * half, 0), (half, 8)).reshape(1, 8 * half)
+
+    partial_t = temp_sums(temp, split_columns(gram_eigenvector_columns.T), weight)
     blocks = partial_t.reshape(modes // 8, 8, hours // 128, 128)
     blocks = blocks.transpose(0, 2, 1, 3).reshape(-1, 8, 128)
     got = lax.all_to_all(blocks, BOTH, 0, 0)
@@ -270,9 +321,9 @@
     got, far_first, far_second, back_traded, front_traded = lax.optimization_barrier(
         (got, far_first, far_second, back_traded, front_traded)
     )
+    far_traded = lax.ppermute(far_second, "tm", to_core)
     pcs = lax.all_to_all(sum_for_all(got), BOTH, 0, 0)
     pcs = pcs.reshape(modes // 8, hours // 128, 8, 128)
-    far_traded = lax.ppermute(far_second, "tm", to_core)
 
     pieces = [own, own_traded, from_back, back_traded, from_front, front_traded, far_first, far_traded]
     step = lax.div(band, 2)

time: 82.4 us -> 79.9 us (0.970)
  starting transfers between devices: 36.4 us -> 31.4 us
  waiting for transfers between devices: 25.2 us -> 29.3 us
  local copies, waits for them, and re-layouts: 9.77 us -> 6.41 us
  Pallas kernels: 9.59 us -> 12 us
    all_to_all x1, waiting for transfers between devices: 0.01 us -> 10.8 us  [per_device(): temp = lax.all_to_all(temp, 'tm', 0, 0)]
    ppermute x3 -> x0, waiting for transfers between devices: 6.6 us -> none  [per_device(): got = pair if d == 0 else lax.ppermute(pair, 'tm', to_chip[d])]
    ppermute x3 -> x0, starting transfers between devices: 5.3 us -> none  [per_device(): got = pair if d == 0 else lax.ppermute(pair, 'tm', to_chip[d])]
    pallas_call x1 -> x4, Pallas kernels: 4.13 us -> 6.51 us  [the longest x1 2.73 us: temp_sums(): pl.pallas_call(sums_kernel, out_shape=jax.ShapeDtypeStruct((modes, blocks...]
    dynamic_update_slice x4 -> x0, local copies, waits for them, and re-layouts: 2.37 us -> none  [per_device(): lax.dynamic_update_slice(whole, got[None], (lax.rem(chip + chips - d, chi...]
    ppermute x1, starting transfers between devices: 0.28 us -> 1.73 us  [per_device(): from_back = lax.ppermute(ahead, 'tm', to_chip[1])]
    ppermute x1, starting transfers between devices: 2.39 us -> 1.3 us  [per_device(): from_front = lax.ppermute(behind, 'tm', to_chip[chips - 1])]
    unnamed x8 -> x14, local copies, waits for them, and re-layouts: 3.06 us -> 3.97 us
  transfers between devices with their start and end apart: 15 -> 12, of which waited for: 7 -> 6; matrix products, arithmetic and copies ran while one was open for 9% -> 3% of each run, Pallas kernels for 9% -> 9%
where the time goes in v7:
time: 79.9 us; the launch traced here: 79.4 us
  starting transfers between devices  31.4 us (39%)
  waiting for transfers between devices  29.3 us (37%)
  Pallas kernels  12 us (15%)
  local copies, waits for them, and re-layouts  6.41 us (8%)
    all_to_all x1, waiting for transfers between devices, per_device(): temp = lax.all_to_all(temp, 'tm', 0, 0)  10.8 us
    all_to_all x1, starting transfers between devices, per_device(): got = lax.all_to_all(blocks, BOTH, 0, 0)  9.48 us
    all_to_all x1, waiting for transfers between devices, per_device(): pcs = lax.all_to_all(sum_for_all(got), BOTH, 0, 0)  9.14 us
    all_to_all x1, starting transfers between devices, per_device(): pcs = lax.all_to_all(sum_for_all(got), BOTH, 0, 0)  7.34 us
    ppermute x1, waiting for transfers between devices, per_device(): far_first = lax.ppermute(from_back[2:3], 'tm', to_chip[1])  6.85 us
    all_to_all x1, starting transfers between devices, per_device(): temp = lax.all_to_all(temp, 'tm', 0, 0)  5.81 us
    unnamed x14, local copies, waits for them, and re-layouts  3.97 us
    pallas_call x1, Pallas kernels, temp_sums(): pl.pallas_call(sums_kernel, out_shape=jax.ShapeDtypeStruct((modes, blocks...  2.73 us
  transfers between devices with their start and end apart: 12, of which 6 were waited for; matrix products, arithmetic and copies ran while one was open for 3% of the time, Pallas kernels for 9%

profile of v7, /device:TPU:1, one launch (start us, length us, event | category | flops | bytes accessed | tf_op | source)
XLA Modules:
  0.0 79.4 jit_solution(5295350257682425436)
XLA Ops:
  0.0 2.3 %shard_map.46 = bf16[4,2,45,8,256]{4,3,2,1,0:T(8,128)(2,1)} custom-call(bf16[2,45,4,8,256]{4,3,2,1,0:T(8,128)(2,1)} %bitcast.22), custom_call_target="tpu_custom_call" | custom-call | bytes 2949120 | tf_op jit(solution)/shard_map/pallas_call | solution.py:58
  2.3 0.0 copy-start.4
  2.3 5.8 %all-to-all-start = ((bf16[8,360,256]{2,1,0:T(8,128)(2,1)}), bf16[8,360,256]{2,1,0:T(8,128)(2,1)S(1)}, u32[]{:S(2)}, u32[]{:S(2)}) async-start(bf16[8,360,256]{2,1,0:T(8,128)(2,1)} %bitcast.21), calls=%async_computation | async-start | bytes 2949120 | tf_op jit(solution)/shard_map/all_to_all | solution.py:294
  8.1 0.0 copy-done.4
  8.1 0.1 collective-permute-start
  8.2 0.0 copy-start.2
  8.2 1.4 %copy-done.2 = bf16[32,90,256]{2,0,1:T(8,128)(2,1)S(1)} copy-done((bf16[32,90,256]{2,0,1:T(8,128)(2,1)S(1)}, bf16[32,90,256]{2,0,1:T(8,128)(2,1)}, u32[]{:S(2)}) %copy-start.2) | copy-done | bytes 1474584
  9.6 0.9 %shard_map.47 = bf16[8,360,256]{2,1,0:T(8,128)(2,1)S(1)} custom-call(s32[8]{0:T(128)S(1)} %compare_select_fusion.10.place_ref, bf16[90,32,256]{2,1,0:T(8,128)(2,1)S(1)} %bitcast.19), custom_call_target="tpu_custom_call" | custom-call | bytes 2949120 | tf_op jit(solution)/shard_map/pallas_call | solution.py:192
  10.5 1.1 %fusion.6 = (bf16[3,360,256]{2,1,0:T(8,128)(2,1)}, bf16[3,360,256]{2,1,0:T(8,128)(2,1)}) fusion(bf16[8,360,256]{2,1,0:T(8,128)(2,1)S(1)} %shard_map.47), kind=kLoop, calls=%fused_computation.23 | loop fusion | bytes 2211840 | tf_op jit(solution)/shard_map/slice | solution.py:301
  11.6 0.0 collective-permute-done
  11.6 1.7 %collective-permute-start.1 = (bf16[3,360,256]{2,1,0:T(8,128)(2,1)}, bf16[3,360,256]{2,1,0:T(8,128)(2,1)S(1)}, u32[]{:S(2)}, u32[]{:S(2)}) collective-permute-start(bf16[3,360,256]{2,1,0:T(8,128)(2,1)} %get-tuple-element.14), channel_id=1, source_target_pairs={{0,32},{16,48},{32,64},{48,80},{64,96},{80,112},{96,0},{112,16},{1... | collective-permute-start | bytes 1658888 | tf_op jit(solution)/shard_map/ppermute | solution.py:307
  13.3 0.0 copy-start.3
  13.3 1.0 %copy-done.3 = f32[2048,64]{0,1:T(8,128)S(1)} copy-done((f32[2048,64]{0,1:T(8,128)S(1)}, f32[2048,64]{0,1:T(8,128)}, u32[]{:S(2)}) %copy-start.3) | copy-done | bytes 524312
  14.4 0.2 shard_map.49.e_ref
  14.5 0.0 copy-start
  14.5 0.9 %copy-done = bf16[192,2048]{1,0:T(8,128)(2,1)} copy-done((bf16[192,2048]{1,0:T(8,128)(2,1)}, bf16[192,2048]{1,0:T(8,128)(2,1)S(1)}, u32[]{:S(2)}) %copy-start) | copy-done | bytes 786456
  15.5 1.3 %collective-permute-start.3 = (bf16[3,360,256]{2,1,0:T(8,128)(2,1)}, bf16[3,360,256]{2,1,0:T(8,128)(2,1)}, u32[]{:S(2)}, u32[]{:S(2)}) collective-permute-start(bf16[3,360,256]{2,1,0:T(8,128)(2,1)} %get-tuple-element.15), channel_id=1, source_target_pairs={{0,96},{16,112},{32,0},{48,16},{64,32},{80,48},{96,64},{112,80},{1... | collective-permute-start | bytes 1658888 | tf_op jit(solution)/shard_map/ppermute | solution.py:308
  16.8 0.1 broadcast_multiply_fusion
  16.8 0.1 dynamic-slice_bitcast_fusion
  16.9 0.1 copy.7
  17.0 0.1 reshape.33.w_ref
  17.1 10.8 %all-to-all-done.t_ref = bf16[8,360,256]{2,1,0:T(8,128)(2,1)S(1)} async-done(((bf16[8,360,256]{2,1,0:T(8,128)(2,1)}), bf16[8,360,256]{2,1,0:T(8,128)(2,1)S(1)}, u32[]{:S(2)}, u32[]{:S(2)}) %all-to-all-start) | async-done | bytes 1474592 | tf_op jit(solution)/shard_map/all_to_all | solution.py:294
  27.8 0.0 copy-start.1
  27.8 1.3 %shard_map.48.z_ref = bf16[8,360,256]{2,1,0:T(8,128)(2,1)S(1)} custom-call(bf16[8,360,256]{2,1,0:T(8,128)(2,1)S(1)} %all-to-all-done.t_ref, f32[1,360]{1,0:T(1,128)S(1)} %reshape.33.w_ref), custom_call_target="tpu_custom_call" | custom-call | flops 11796480 | bytes 2949120 | tf_op jit(solution)/shard_map/pallas_call | solution.py:130
  29.2 0.0 copy-done.1
  29.2 2.7 %shard_map.50 = f32[64,2048]{1,0:T(8,128)} custom-call(bf16[8,360,256]{2,1,0:T(8,128)(2,1)S(1)} %shard_map.48.z_ref, bf16[192,2048]{1,0:T(8,128)(2,1)S(1)} %copy-done.1), custom_call_target="tpu_custom_call" | custom-call | flops 566231040 | bytes 2260992 | tf_op jit(solution)/shard_map/pallas_call | solution.py:138
  31.9 9.5 %all-to-all-start.1 = ((f32[128,8,128]{2,1,0:T(8,128)}), f32[128,8,128]{2,1,0:T(8,128)S(1)}, u32[]{:S(2)}, u32[]{:S(2)}) async-start(f32[128,8,128]{2,1,0:T(8,128)} %bitcast.11), calls=%async_computation.1 | async-start | bytes 1048576 | tf_op jit(solution)/shard_map/all_to_all | solution.py:316
  41.4 0.0 collective-permute-done.1.refs_2_
  41.5 1.5 %collective-permute-start.2 = (bf16[1,360,256]{2,1,0:T(8,128)(2,1)S(1)}, bf16[1,360,256]{2,1,0:T(8,128)(2,1)S(1)}, u32[]{:S(2)}, u32[]{:S(2)}) collective-permute-start(bf16[1,360,256]{2,1,0:T(8,128)(2,1)S(1)} %get-tuple-element.26), channel_id=1, source_target_pairs={{0,32},{16,48},{32,64},{48,80},{64,96},{80,112},{96,0},{112,16},{1... | collective-permute-start | bytes 552968 | tf_op jit(solution)/shard_map/ppermute | solution.py:317
  42.9 0.0 collective-permute-done.3.refs_4_
  42.9 1.0 %fusion.7 = (bf16[1,360,256]{2,1,0:T(8,128)(2,1)S(1)}, bf16[1,360,256]{2,1,0:T(8,128)(2,1)S(1)}) fusion(bf16[3,360,256]{2,1,0:T(8,128)(2,1)} %collective-permute-done.3.refs_4_), kind=kLoop, calls=%fused_computation.24 | loop fusion | bytes 737280 | tf_op jit(solution)/shard_map/slice | solution.py:320
  44.0 1.4 %collective-permute-start.4 = (bf16[1,360,256]{2,1,0:T(8,128)(2,1)S(1)}, bf16[1,360,256]{2,1,0:T(8,128)(2,1)S(1)}, u32[]{:S(2)}, u32[]{:S(2)}) collective-permute-start(bf16[1,360,256]{2,1,0:T(8,128)(2,1)S(1)} %get-tuple-element.24), channel_id=1, source_target_pairs={{0,96},{16,112},{32,0},{48,16},{64,32},{80,48},{96,64},{112,80},{1... | collective-permute-start | bytes 552968 | tf_op jit(solution)/shard_map/ppermute | solution.py:318
  45.3 1.6 %collective-permute-start.5 = (bf16[1,360,256]{2,1,0:T(8,128)(2,1)S(1)}, bf16[1,360,256]{2,1,0:T(8,128)(2,1)S(1)}, u32[]{:S(2)}, u32[]{:S(2)}) collective-permute-start(bf16[1,360,256]{2,1,0:T(8,128)(2,1)S(1)} %get-tuple-element.25), channel_id=1, source_target_pairs={{0,16},{16,0},{32,48},{48,32},{64,80},{80,64},{96,112},{112,96},{1... | collective-permute-start | bytes 552968 | tf_op jit(solution)/shard_map/ppermute | solution.py:319
  46.9 0.0 collective-permute-start.6
  46.9 6.9 %collective-permute-done.2.refs_6_ = bf16[1,360,256]{2,1,0:T(8,128)(2,1)S(1)} collective-permute-done((bf16[1,360,256]{2,1,0:T(8,128)(2,1)S(1)}, bf16[1,360,256]{2,1,0:T(8,128)(2,1)S(1)}, u32[]{:S(2)}, u32[]{:S(2)}) %collective-permute-start.2) | collective-permute-done | bytes 184352 | tf_op jit(solution)/shard_map/ppermute | solution.py:317
  53.8 0.0 collective-permute-done.4
  53.8 0.0 copy-start.5
  53.8 0.0 collective-permute-done.5.refs_3_
  53.8 0.7 copy-done.5
  54.5 0.0 collective-permute-done.6.refs_5_
  54.5 0.0 copy-start.6
  54.5 1.1 %all-to-all-done.1.got_ref = f32[128,8,128]{2,1,0:T(8,128)S(1)} async-done(((f32[128,8,128]{2,1,0:T(8,128)}), f32[128,8,128]{2,1,0:T(8,128)S(1)}, u32[]{:S(2)}, u32[]{:S(2)}) %all-to-all-start.1) | async-done | bytes 524320 | tf_op jit(solution)/shard_map/all_to_all | solution.py:316
  55.6 0.9 %shard_map.51 = f32[128,8,128]{2,1,0:T(8,128)} custom-call(f32[128,8,128]{2,1,0:T(8,128)S(1)} %all-to-all-done.1.got_ref), custom_call_target="tpu_custom_call" | custom-call | flops 131072 | bytes 1048576 | tf_op jit(solution)/shard_map/pallas_call | solution.py:165
  56.5 7.3 %all-to-all-start.2 = ((f32[128,8,128]{2,1,0:T(8,128)}), f32[128,8,128]{2,1,0:T(8,128)S(1)}, u32[]{:S(2)}, u32[]{:S(2)}) async-start(f32[128,8,128]{2,1,0:T(8,128)} %shard_map.51), calls=%async_computation.2 | async-start | bytes 1048576 | tf_op jit(solution)/shard_map/all_to_all | solution.py:325
  63.8 1.1 %collective-permute-start.7 = (bf16[1,360,256]{2,1,0:T(8,128)(2,1)S(1)}, bf16[1,360,256]{2,1,0:T(8,128)(2,1)S(1)}, u32[]{:S(2)}, u32[]{:S(2)}) collective-permute-start(bf16[1,360,256]{2,1,0:T(8,128)(2,1)S(1)} %slice.40), channel_id=1, source_target_pairs={{0,16},{16,0},{32,48},{48,32},{64,80},{80,64},{96,112},{112,96},{1... | collective-permute-start | bytes 552968 | tf_op jit(solution)/shard_map/ppermute | solution.py:302
  65.0 0.0 copy-done.6
  65.1 0.1 collective-permute-start.8
  65.2 0.9 %collective-permute-done.7.refs_1_ = bf16[1,360,256]{2,1,0:T(8,128)(2,1)S(1)} collective-permute-done((bf16[1,360,256]{2,1,0:T(8,128)(2,1)S(1)}, bf16[1,360,256]{2,1,0:T(8,128)(2,1)S(1)}, u32[]{:S(2)}, u32[]{:S(2)}) %collective-permute-start.7) | collective-permute-done | bytes 184352 | tf_op jit(solution)/shard_map/ppermute | solution.py:302
  66.1 0.5 collective-permute-done.8.refs_7_
  66.6 2.2 %shard_map.52.z_ref = bf16[8,360,256]{2,1,0:T(8,128)(2,1)S(1)} custom-call(s32[8]{0:T(128)S(1)} %fusion.5.place_ref, bf16[2,360,256]{2,1,0:T(8,128)(2,1)S(1)} %slice.39.refs_0_, bf16[1,360,256]{2,1,0:T(8,128)(2,1)S(1)} %collective-permute-done.7.refs_1_, bf16[3,360,256]{2,1,0:T(8,128)(2,1)S(1)} %collective-permute-done.1.refs_2_, ...), custom_call_target="tpu_custom_call" | custom-call | bytes 11796480 | tf_op jit(solution)/shard_map/pallas_call | solution.py:225
  68.8 9.1 %all-to-all-done.2 = f32[128,8,128]{2,1,0:T(8,128)S(1)} async-done(((f32[128,8,128]{2,1,0:T(8,128)}), f32[128,8,128]{2,1,0:T(8,128)S(1)}, u32[]{:S(2)}, u32[]{:S(2)}) %all-to-all-start.2) | async-done | bytes 524320 | tf_op jit(solution)/shard_map/all_to_all | solution.py:325
  77.9 1.5 %shard_map.53 = f32[4,64,90]{2,1,0:T(8,128)} custom-call(f32[8,16,8,128]{3,2,1,0:T(8,128)S(1)} %bitcast.18, bf16[8,360,256]{2,1,0:T(8,128)(2,1)S(1)} %shard_map.52.z_ref, f32[4,90]{1,0:T(4,128)S(1)} %convert_multiply_fusion.factor_ref), custom_call_target="tpu_custom_call" | custom-call | flops 94371840 | bytes 1998848 | tf_op jit(solution)/shard_map/pallas_call | solution.py:263
  (9 shorter events, 0.2 us)
Async XLA Ops:
  2.3 5.8 %copy-start.4 = (s32[4,90]{1,0:T(4,128)S(1)}, s32[4,90]{1,0:T(4,128)}, u32[]{:S(2)}) copy-start(s32[4,90]{1,0:T(4,128)} %param.7) | copy-start | bytes 4324
  2.3 25.5 %all-to-all-start = ((bf16[8,360,256]{2,1,0:T(8,128)(2,1)}), bf16[8,360,256]{2,1,0:T(8,128)(2,1)S(1)}, u32[]{:S(2)}, u32[]{:S(2)}) async-start(bf16[8,360,256]{2,1,0:T(8,128)(2,1)} %bitcast.21), calls=%async_computation | async-start | bytes 2949120 | tf_op jit(solution)/shard_map/all_to_all | solution.py:294
  8.1 3.4 %collective-permute-start = (s32[4,90]{1,0:T(4,128)S(1)}, s32[4,90]{1,0:T(4,128)S(1)}, u32[]{:S(2)}, u32[]{:S(2)}) collective-permute-start(s32[4,90]{1,0:T(4,128)S(1)} %copy-done.4), channel_id=1, source_target_pairs={{0,16},{16,0},{32,48},{48,32},{64,80},{80,64},{96,112},{112,96},{1... | collective-permute-start | bytes 4328 | tf_op jit(solution)/shard_map/ppermute | solution.py:304
  8.2 1.4 %copy-start.2 = (bf16[32,90,256]{2,0,1:T(8,128)(2,1)S(1)}, bf16[32,90,256]{2,0,1:T(8,128)(2,1)}, u32[]{:S(2)}) copy-start(bf16[32,90,256]{2,0,1:T(8,128)(2,1)} %param.5) | copy-start | bytes 4423684
  11.6 29.8 %collective-permute-start.1 = (bf16[3,360,256]{2,1,0:T(8,128)(2,1)}, bf16[3,360,256]{2,1,0:T(8,128)(2,1)S(1)}, u32[]{:S(2)}, u32[]{:S(2)}) collective-permute-start(bf16[3,360,256]{2,1,0:T(8,128)(2,1)} %get-tuple-element.14), channel_id=1, source_target_pairs={{0,32},{16,48},{32,64},{48,80},{64,96},{80,112},{96,0},{112,16},{1... | collective-permute-start | bytes 1658888 | tf_op jit(solution)/shard_map/ppermute | solution.py:307
  13.3 1.0 %copy-start.3 = (f32[2048,64]{0,1:T(8,128)S(1)}, f32[2048,64]{0,1:T(8,128)}, u32[]{:S(2)}) copy-start(f32[2048,64]{0,1:T(8,128)} %param.6) | copy-start | bytes 1572868
  14.5 0.9 %copy-start = (bf16[192,2048]{1,0:T(8,128)(2,1)}, bf16[192,2048]{1,0:T(8,128)(2,1)S(1)}, u32[]{:S(2)}) copy-start(bf16[192,2048]{1,0:T(8,128)(2,1)S(1)} %shard_map.49.e_ref) | copy-start | bytes 2359300
  15.5 27.5 %collective-permute-start.3 = (bf16[3,360,256]{2,1,0:T(8,128)(2,1)}, bf16[3,360,256]{2,1,0:T(8,128)(2,1)}, u32[]{:S(2)}, u32[]{:S(2)}) collective-permute-start(bf16[3,360,256]{2,1,0:T(8,128)(2,1)} %get-tuple-element.15), channel_id=1, source_target_pairs={{0,96},{16,112},{32,0},{48,16},{64,32},{80,48},{96,64},{112,80},{1... | collective-permute-start | bytes 1658888 | tf_op jit(solution)/shard_map/ppermute | solution.py:308
  27.8 1.3 %copy-start.1 = (bf16[192,2048]{1,0:T(8,128)(2,1)S(1)}, bf16[192,2048]{1,0:T(8,128)(2,1)}, u32[]{:S(2)}) copy-start(bf16[192,2048]{1,0:T(8,128)(2,1)} %copy-done) | copy-start | bytes 2359300
  31.9 23.7 %all-to-all-start.1 = ((f32[128,8,128]{2,1,0:T(8,128)}), f32[128,8,128]{2,1,0:T(8,128)S(1)}, u32[]{:S(2)}, u32[]{:S(2)}) async-start(f32[128,8,128]{2,1,0:T(8,128)} %bitcast.11), calls=%async_computation.1 | async-start | bytes 1048576 | tf_op jit(solution)/shard_map/all_to_all | solution.py:316
  41.5 12.3 %collective-permute-start.2 = (bf16[1,360,256]{2,1,0:T(8,128)(2,1)S(1)}, bf16[1,360,256]{2,1,0:T(8,128)(2,1)S(1)}, u32[]{:S(2)}, u32[]{:S(2)}) collective-permute-start(bf16[1,360,256]{2,1,0:T(8,128)(2,1)S(1)} %get-tuple-element.26), channel_id=1, source_target_pairs={{0,32},{16,48},{32,64},{48,80},{64,96},{80,112},{96,0},{112,16},{1... | collective-permute-start | bytes 552968 | tf_op jit(solution)/shard_map/ppermute | solution.py:317
  44.0 9.8 %collective-permute-start.4 = (bf16[1,360,256]{2,1,0:T(8,128)(2,1)S(1)}, bf16[1,360,256]{2,1,0:T(8,128)(2,1)S(1)}, u32[]{:S(2)}, u32[]{:S(2)}) collective-permute-start(bf16[1,360,256]{2,1,0:T(8,128)(2,1)S(1)} %get-tuple-element.24), channel_id=1, source_target_pairs={{0,96},{16,112},{32,0},{48,16},{64,32},{80,48},{96,64},{112,80},{1... | collective-permute-start | bytes 552968 | tf_op jit(solution)/shard_map/ppermute | solution.py:318
  45.3 8.5 %collective-permute-start.5 = (bf16[1,360,256]{2,1,0:T(8,128)(2,1)S(1)}, bf16[1,360,256]{2,1,0:T(8,128)(2,1)S(1)}, u32[]{:S(2)}, u32[]{:S(2)}) collective-permute-start(bf16[1,360,256]{2,1,0:T(8,128)(2,1)S(1)} %get-tuple-element.25), channel_id=1, source_target_pairs={{0,16},{16,0},{32,48},{48,32},{64,80},{80,64},{96,112},{112,96},{1... | collective-permute-start | bytes 552968 | tf_op jit(solution)/shard_map/ppermute | solution.py:319
  46.9 7.5 %collective-permute-start.6 = (bf16[1,360,256]{2,1,0:T(8,128)(2,1)S(1)}, bf16[1,360,256]{2,1,0:T(8,128)(2,1)S(1)}, u32[]{:S(2)}, u32[]{:S(2)}) collective-permute-start(bf16[1,360,256]{2,1,0:T(8,128)(2,1)S(1)} %get-tuple-element.23), channel_id=1, source_target_pairs={{0,16},{16,0},{32,48},{48,32},{64,80},{80,64},{96,112},{112,96},{1... | collective-permute-start | bytes 552968 | tf_op jit(solution)/shard_map/ppermute | solution.py:320
  53.8 0.7 copy-start.5
  54.5 10.6 %copy-start.6 = (bf16[1,360,256]{2,1,0:T(8,128)(2,1)S(1)}, bf16[1,360,256]{2,1,0:T(8,128)(2,1)}, u32[]{:S(2)}) copy-start(bf16[1,360,256]{2,1,0:T(8,128)(2,1)} %copy-done.5) | copy-start | bytes 552964
  56.5 21.4 %all-to-all-start.2 = ((f32[128,8,128]{2,1,0:T(8,128)}), f32[128,8,128]{2,1,0:T(8,128)S(1)}, u32[]{:S(2)}, u32[]{:S(2)}) async-start(f32[128,8,128]{2,1,0:T(8,128)} %shard_map.51), calls=%async_computation.2 | async-start | bytes 1048576 | tf_op jit(solution)/shard_map/all_to_all | solution.py:325
  63.8 2.2 %collective-permute-start.7 = (bf16[1,360,256]{2,1,0:T(8,128)(2,1)S(1)}, bf16[1,360,256]{2,1,0:T(8,128)(2,1)S(1)}, u32[]{:S(2)}, u32[]{:S(2)}) collective-permute-start(bf16[1,360,256]{2,1,0:T(8,128)(2,1)S(1)} %slice.40), channel_id=1, source_target_pairs={{0,16},{16,0},{32,48},{48,32},{64,80},{80,64},{96,112},{112,96},{1... | collective-permute-start | bytes 552968 | tf_op jit(solution)/shard_map/ppermute | solution.py:302
  65.1 1.5 %collective-permute-start.8 = (bf16[1,360,256]{2,1,0:T(8,128)(2,1)S(1)}, bf16[1,360,256]{2,1,0:T(8,128)(2,1)S(1)}, u32[]{:S(2)}, u32[]{:S(2)}) collective-permute-start(bf16[1,360,256]{2,1,0:T(8,128)(2,1)S(1)} %copy-done.6), channel_id=1, source_target_pairs={{0,16},{16,0},{32,48},{48,32},{64,80},{80,64},{96,112},{112,96},{1... | collective-permute-start | bytes 552968 | tf_op jit(solution)/shard_map/ppermute | solution.py:324

commit v8 on v7

--- a/solution.py
+++ b/solution.py
@@ -103,25 +103,20 @@
         weight = weights[rows, :1]
         for b in range(blocks):
             centered = t_ref[b, rows, :].astype(F32) - average
-            z_ref[b, rows, :] = ((centered * scale) * weight).astype(BF16)
+            z_ref[rows, b * width : (b + 1) * width] = ((centered * scale) * weight).astype(BF16)
 
 
 def sums_kernel(z_ref, e_ref, out_ref):
-    blocks, cells, width = z_ref.shape
     modes = out_ref.shape[0]
-    loadings = jnp.zeros((cells, 3 * modes), F32)
-    for b in range(blocks):
-        loadings = loadings + lax.dot_general(
-            z_ref[b], e_ref[:, b * width : (b + 1) * width], NT, preferred_element_type=F32
-        )
+    loadings = lax.dot_general(z_ref[...], e_ref[...], NT, preferred_element_type=F32)
     turned = loadings.T
     turned = turned[:modes] + (turned[modes : 2 * modes] + turned[2 * modes :])
     stacked = jnp.concatenate(three_terms(turned), axis=0)
-    for b in range(blocks):
-        sums = lax.dot_general(stacked, z_ref[b], NN, preferred_element_type=F32)
-        out_ref[:, b * width : (b + 1) * width] = sums[:modes] + (
-            sums[modes : 2 * modes] + sums[2 * modes :]
-        )
+    hours = out_ref.shape[1]
+    for start, size in row_chunks(hours, 512):
+        columns = slice(start, start + size)
+        sums = lax.dot_general(stacked, z_ref[:, columns], NN, preferred_element_type=F32)
+        out_ref[:, columns] = sums[:modes] + (sums[modes : 2 * modes] + sums[2 * modes :])
 
 
 def temp_sums(temp, split, weight):
@@ -129,7 +124,7 @@
     modes = split.shape[0] // 3
     scores = pl.pallas_call(
         scores_kernel,
-        out_shape=jax.ShapeDtypeStruct(temp.shape, BF16),
+        out_shape=jax.ShapeDtypeStruct((cells, blocks * width), BF16),
         compiler_params=params(),
         cost_estimate=pl.CostEstimate(
             flops=16 * temp.size, bytes_accessed=4 * temp.size, transcendentals=cells
@@ -216,7 +211,8 @@
         scale = lax.rsqrt(jnp.sum(square, axis=1, keepdims=True) / hours + EPS)
         for n, piece in enumerate(pieces):
             centered = piece[0, rows, :].astype(F32) - average
-            out_ref[place_ref[n], rows, :] = (centered * scale).astype(BF16)
+            columns = pl.ds(pl.multiple_of(place_ref[n] * width, width), width)
+            out_ref[rows, columns] = (centered * scale).astype(BF16)
 
 
 def hum_scores(places, pieces):
@@ -226,7 +222,7 @@
         hum_kernel,
         in_specs=[pl.BlockSpec(memory_space=pltpu.SMEM)]
         + [pl.BlockSpec(memory_space=pltpu.VMEM)] * count,
-        out_shape=jax.ShapeDtypeStruct((count, cells, width), BF16),
+        out_shape=jax.ShapeDtypeStruct((cells, count * width), BF16),
         compiler_params=params(),
         cost_estimate=pl.CostEstimate(
             flops=0, bytes_accessed=16 * cells * width * count, transcendentals=0
@@ -236,7 +232,6 @@
 
 def final_kernel(pcs_ref, z_ref, factor_ref, out_ref, rows_ref):
     octets, runs, _, _ = pcs_ref.shape
-    blocks, cells, width = z_ref.shape
     lats, modes, lons = out_ref.shape
     hours = runs * 128
     rows = []
@@ -246,12 +241,7 @@
         variance = jnp.sum(centered * centered, axis=1, keepdims=True) / hours
         rows.append(centered * lax.rsqrt(variance + EPS))
     pcz = jnp.concatenate(rows, axis=0).astype(BF16)
-    total = jnp.zeros((cells, modes), F32)
-    for b in range(blocks):
-        total = total + lax.dot_general(
-            z_ref[b], pcz[:, b * width : (b + 1) * width], NT, preferred_element_type=F32
-        )
-    rows_ref[:, :modes] = total
+    rows_ref[:, :modes] = lax.dot_general(z_ref[...], pcz, NT, preferred_element_type=F32)
     for i in range(lats):
         picked = rows_ref[pl.ds(i, lons, stride=lats), :]
         out_ref[i] = picked.T[:modes] * factor_ref[i : i + 1, :]
@@ -294,18 +284,15 @@
     temp = lax.all_to_all(temp, "tm", 0, 0)
 
     band = jnp.arange(members, dtype=jnp.int32)
-    far = lax.rem(lax.div(band, 2) + chips - chip, chips)
-    slot = lax.rem(band + core, 2)
-    order = jnp.where(far == 0, 6 + slot, jnp.where(far == 1, slot, jnp.where(far == 2, 2 + 3 * slot, 3 + slot)))
+    far = lax.rem(lax.div(band, 2) + 2 * chips - chip - 1, chips)
+    order = 2 * far + lax.rem(band + core, 2)
     laid = lay_out_bands(order, moisture_content.transpose(1, 0, 2))
-    ahead, behind, own = laid[0:3], laid[3:6], laid[6:8]
-    own_traded = lax.ppermute(own[1:2], "tm", to_core)
+    sent, own = [laid[2 * d : 2 * d + 2] for d in range(chips - 1)], laid[2 * chips - 2 :]
 
     other = lax.ppermute(marine_indicator, "tm", to_core)
     pair = jnp.where(core == 0, jnp.stack([marine_indicator, other]), jnp.stack([other, marine_indicator]))
-    pair, ahead, behind = lax.optimization_barrier((pair, ahead, behind))
-    from_back = lax.ppermute(ahead, "tm", to_chip[1])
-    from_front = lax.ppermute(behind, "tm", to_chip[chips - 1])
+    pair, *sent = lax.optimization_barrier((pair, *sent))
+    arrived = [lax.ppermute(sent[d - 1], "tm", to_chip[d]) for d in range(1, chips)]
     root = area_root(8 * chip + jnp.arange(8, dtype=jnp.int32), total_lat)
     scaling = root[:, None] * pair.reshape(8, lons).astype(F32)
     weight = lax.dynamic_slice(scaling.T, (core * half, 0), (half, 8)).reshape(1, 8 * half)
@@ -314,21 +301,13 @@
     blocks = partial_t.reshape(modes // 8, 8, hours // 128, 128)
     blocks = blocks.transpose(0, 2, 1, 3).reshape(-1, 8, 128)
     got = lax.all_to_all(blocks, BOTH, 0, 0)
-    far_first = lax.ppermute(from_back[2:3], "tm", to_chip[1])
-    far_second = lax.ppermute(from_front[2:3], "tm", to_chip[chips - 1])
-    back_traded = lax.ppermute(from_back[1:2], "tm", to_core)
-    front_traded = lax.ppermute(from_front[1:2], "tm", to_core)
-    got, far_first, far_second, back_traded, front_traded = lax.optimization_barrier(
-        (got, far_first, far_second, back_traded, front_traded)
-    )
-    far_traded = lax.ppermute(far_second, "tm", to_core)
+    traded = [lax.ppermute(blocks[1:2], "tm", to_core) for blocks in [own, *arrived]]
+    got, *traded = lax.optimization_barrier((got, *traded))
     pcs = lax.all_to_all(sum_for_all(got), BOTH, 0, 0)
     pcs = pcs.reshape(modes // 8, hours // 128, 8, 128)
 
-    pieces = [own, own_traded, from_back, back_traded, from_front, front_traded, far_first, far_traded]
-    step = lax.div(band, 2)
-    distance = jnp.where(step == 0, 0, jnp.where(step == 1, chips - 1, step - 1))
-    places = 2 * lax.rem(chip + distance, chips) + lax.rem(band + core, 2)
+    pieces = [piece for both in zip([own, *arrived], traded) for piece in both]
+    places = 2 * lax.rem(chip + chips - lax.div(band, 2), chips) + lax.rem(band + core, 2)
     scores = hum_scores(places, pieces)
     return correlate(pcs, scores, mask_float / hours).transpose(0, 2, 1)
 

time: 79.9 us -> 76.6 us (0.959)
  starting transfers between devices: 31.4 us -> 27 us
  local copies, waits for them, and re-layouts: 6.41 us -> 7.37 us
    ppermute x8 -> x7, waiting for transfers between devices: 8.26 us -> 1.46 us  [the longest x4 1.39 us: per_device(): lax.ppermute(blocks[1:2], 'tm', to_core)]
    all_to_all x1, waiting for transfers between devices: 1.13 us -> 7.46 us  [per_device(): got = lax.all_to_all(blocks, BOTH, 0, 0)]
    all_to_all x1, starting transfers between devices: 7.34 us -> 4 us  [per_device(): pcs = lax.all_to_all(sum_for_all(got), BOTH, 0, 0)]
    all_to_all x1, waiting for transfers between devices: 9.14 us -> 11.8 us  [per_device(): pcs = lax.all_to_all(sum_for_all(got), BOTH, 0, 0)]
    all_to_all x1, waiting for transfers between devices: 10.8 us -> 8.54 us  [per_device(): temp = lax.all_to_all(temp, 'tm', 0, 0)]
    slice x5, local copies, waits for them, and re-layouts: 2.18 us -> 3.83 us  [the longest x4 2.82 us: per_device(): blocks[1:2]]
    ppermute x8 -> x7, starting transfers between devices: 8.72 us -> 7.6 us  [the longest x3 5.3 us: per_device(): lax.ppermute(sent[d - 1], 'tm', to_chip[d])]
    unnamed x14 -> x10, local copies, waits for them, and re-layouts: 3.97 us -> 3.28 us
  transfers between devices with their start and end apart: 12 -> 11, of which waited for: 6 -> 5; matrix products, arithmetic and copies ran while one was open for 3% -> 6% of each run, Pallas kernels for 9% -> 10%
where the time goes in v8:
time: 76.6 us; the launch traced here: 76.2 us
  waiting for transfers between devices  29.3 us (38%)
  starting transfers between devices  27 us (35%)
  Pallas kernels  12.1 us (16%)
  local copies, waits for them, and re-layouts  7.37 us (10%)
    all_to_all x1, waiting for transfers between devices, per_device(): pcs = lax.all_to_all(sum_for_all(got), BOTH, 0, 0)  11.8 us
    all_to_all x1, starting transfers between devices, per_device(): got = lax.all_to_all(blocks, BOTH, 0, 0)  9.53 us
    all_to_all x1, waiting for transfers between devices, per_device(): temp = lax.all_to_all(temp, 'tm', 0, 0)  8.54 us
    all_to_all x1, waiting for transfers between devices, per_device(): got = lax.all_to_all(blocks, BOTH, 0, 0)  7.46 us
    all_to_all x1, starting transfers between devices, per_device(): temp = lax.all_to_all(temp, 'tm', 0, 0)  5.81 us
    ppermute x3, starting transfers between devices, per_device(): lax.ppermute(sent[d - 1], 'tm', to_chip[d])  5.3 us
    all_to_all x1, starting transfers between devices, per_device(): pcs = lax.all_to_all(sum_for_all(got), BOTH, 0, 0)  4 us
    unnamed x10, local copies, waits for them, and re-layouts  3.28 us
  transfers between devices with their start and end apart: 11, of which 5 were waited for; matrix products, arithmetic and copies ran while one was open for 6% of the time, Pallas kernels for 10%

profile of v8, /device:TPU:1, one launch (start us, length us, event | category | flops | bytes accessed | tf_op | source)
XLA Modules:
  0.0 76.2 jit_solution(15278940879402254764)
XLA Ops:
  0.0 2.3 %shard_map.46 = bf16[4,2,45,8,256]{4,3,2,1,0:T(8,128)(2,1)} custom-call(bf16[2,45,4,8,256]{4,3,2,1,0:T(8,128)(2,1)} %bitcast.22), custom_call_target="tpu_custom_call" | custom-call | bytes 2949120 | tf_op jit(solution)/shard_map/pallas_call | solution.py:58
  2.3 0.0 copy-start.4
  2.3 5.8 %all-to-all-start = ((bf16[8,360,256]{2,1,0:T(8,128)(2,1)}), bf16[8,360,256]{2,1,0:T(8,128)(2,1)S(1)}, u32[]{:S(2)}, u32[]{:S(2)}) async-start(bf16[8,360,256]{2,1,0:T(8,128)(2,1)} %bitcast.21), calls=%async_computation | async-start | bytes 2949120 | tf_op jit(solution)/shard_map/all_to_all | solution.py:284
  8.1 0.0 copy-done.4
  8.1 0.1 collective-permute-start
  8.2 0.0 copy-start.2
  8.3 1.4 %copy-done.2 = bf16[32,90,256]{2,0,1:T(8,128)(2,1)S(1)} copy-done((bf16[32,90,256]{2,0,1:T(8,128)(2,1)S(1)}, bf16[32,90,256]{2,0,1:T(8,128)(2,1)}, u32[]{:S(2)}) %copy-start.2) | copy-done | bytes 1474584
  9.6 0.9 %shard_map.47 = bf16[8,360,256]{2,1,0:T(8,128)(2,1)S(1)} custom-call(s32[8]{0:T(128)S(1)} %fusion.2.place_ref, bf16[90,32,256]{2,1,0:T(8,128)(2,1)S(1)} %bitcast.19), custom_call_target="tpu_custom_call" | custom-call | bytes 2949120 | tf_op jit(solution)/shard_map/pallas_call | solution.py:187
  10.5 1.0 %fusion.7 = (bf16[2,360,256]{2,1,0:T(8,128)(2,1)S(1)}, bf16[2,360,256]{2,1,0:T(8,128)(2,1)}, bf16[2,360,256]{2,1,0:T(8,128)(2,1)}, bf16[2,360,256]{2,1,0:T(8,128)(2,1)}) fusion(bf16[8,360,256]{2,1,0:T(8,128)(2,1)S(1)} %shard_map.47), kind=kLoop, calls=%fused_computation.19 | loop fusion | bytes 2949120 | tf_op jit(solution)/shard_map/slice | solution.py:290
  11.6 0.0 copy-start.3
  11.6 1.0 %copy-done.3 = f32[2048,64]{0,1:T(8,128)S(1)} copy-done((f32[2048,64]{0,1:T(8,128)S(1)}, f32[2048,64]{0,1:T(8,128)}, u32[]{:S(2)}) %copy-start.3) | copy-done | bytes 524312
  12.6 0.2 shard_map.49.e_ref
  12.8 0.0 copy-start
  12.8 0.9 %copy-done = bf16[192,2048]{1,0:T(8,128)(2,1)} copy-done((bf16[192,2048]{1,0:T(8,128)(2,1)}, bf16[192,2048]{1,0:T(8,128)(2,1)S(1)}, u32[]{:S(2)}) %copy-start) | copy-done | bytes 786456
  13.6 0.0 collective-permute-done
  13.7 0.1 broadcast_multiply_fusion
  13.7 0.1 dynamic-slice_bitcast_fusion
  13.8 0.1 copy.7
  13.9 0.1 reshape.33.w_ref
  14.0 1.7 %collective-permute-start.2 = (bf16[2,360,256]{2,1,0:T(8,128)(2,1)}, bf16[2,360,256]{2,1,0:T(8,128)(2,1)}, u32[]{:S(2)}, u32[]{:S(2)}) collective-permute-start(bf16[2,360,256]{2,1,0:T(8,128)(2,1)} %get-tuple-element.15), channel_id=1, source_target_pairs={{0,32},{16,48},{32,64},{48,80},{64,96},{80,112},{96,0},{112,16},{1... | collective-permute-start | bytes 1105928 | tf_op jit(solution)/shard_map/ppermute | solution.py:295
  15.7 2.4 %collective-permute-start.4 = (bf16[2,360,256]{2,1,0:T(8,128)(2,1)}, bf16[2,360,256]{2,1,0:T(8,128)(2,1)}, u32[]{:S(2)}, u32[]{:S(2)}) collective-permute-start(bf16[2,360,256]{2,1,0:T(8,128)(2,1)} %get-tuple-element.16), channel_id=1, source_target_pairs={{0,64},{16,80},{32,96},{48,112},{64,0},{80,16},{96,32},{112,48},{1... | collective-permute-start | bytes 1105928 | tf_op jit(solution)/shard_map/ppermute | solution.py:295
  18.1 1.2 %collective-permute-start.6 = (bf16[2,360,256]{2,1,0:T(8,128)(2,1)}, bf16[2,360,256]{2,1,0:T(8,128)(2,1)}, u32[]{:S(2)}, u32[]{:S(2)}) collective-permute-start(bf16[2,360,256]{2,1,0:T(8,128)(2,1)} %get-tuple-element.17), channel_id=1, source_target_pairs={{0,96},{16,112},{32,0},{48,16},{64,32},{80,48},{96,64},{112,80},{1... | collective-permute-start | bytes 1105928 | tf_op jit(solution)/shard_map/ppermute | solution.py:295
  19.3 8.5 %all-to-all-done.t_ref = bf16[8,360,256]{2,1,0:T(8,128)(2,1)S(1)} async-done(((bf16[8,360,256]{2,1,0:T(8,128)(2,1)}), bf16[8,360,256]{2,1,0:T(8,128)(2,1)S(1)}, u32[]{:S(2)}, u32[]{:S(2)}) %all-to-all-start) | async-done | bytes 1474592 | tf_op jit(solution)/shard_map/all_to_all | solution.py:284
  27.8 0.0 copy-start.1
  27.9 1.3 %shard_map.48.z_ref = bf16[360,2048]{1,0:T(8,128)(2,1)S(1)} custom-call(bf16[8,360,256]{2,1,0:T(8,128)(2,1)S(1)} %all-to-all-done.t_ref, f32[1,360]{1,0:T(1,128)S(1)} %reshape.33.w_ref), custom_call_target="tpu_custom_call" | custom-call | flops 11796480 | bytes 2949120 | tf_op jit(solution)/shard_map/pallas_call | solution.py:125
  29.2 0.0 copy-done.1
  29.2 2.7 %shard_map.50 = f32[64,2048]{1,0:T(8,128)} custom-call(bf16[360,2048]{1,0:T(8,128)(2,1)S(1)} %shard_map.48.z_ref, bf16[192,2048]{1,0:T(8,128)(2,1)S(1)} %copy-done.1), custom_call_target="tpu_custom_call" | custom-call | flops 566231040 | bytes 2260992 | tf_op jit(solution)/shard_map/pallas_call | solution.py:133
  31.9 9.5 %all-to-all-start.1 = ((f32[128,8,128]{2,1,0:T(8,128)}), f32[128,8,128]{2,1,0:T(8,128)S(1)}, u32[]{:S(2)}, u32[]{:S(2)}) async-start(f32[128,8,128]{2,1,0:T(8,128)} %bitcast.11), calls=%async_computation.1 | async-start | bytes 1048576 | tf_op jit(solution)/shard_map/all_to_all | solution.py:303
  41.5 1.1 %collective-permute-start.1 = (bf16[1,360,256]{2,1,0:T(8,128)(2,1)S(1)}, bf16[1,360,256]{2,1,0:T(8,128)(2,1)S(1)}, u32[]{:S(2)}, u32[]{:S(2)}) collective-permute-start(bf16[1,360,256]{2,1,0:T(8,128)(2,1)S(1)} %slice.36), channel_id=1, source_target_pairs={{0,16},{16,0},{32,48},{48,32},{64,80},{80,64},{96,112},{112,96},{1... | collective-permute-start | bytes 552968 | tf_op jit(solution)/shard_map/ppermute | solution.py:304
  42.6 0.0 collective-permute-done.2.refs_2_
  42.6 0.9 %slice.37 = bf16[1,360,256]{2,1,0:T(8,128)(2,1)S(1)} slice(bf16[2,360,256]{2,1,0:T(8,128)(2,1)} %collective-permute-done.2.refs_2_), slice={[1:2], [0:360], [0:256]} | slice | bytes 368640 | tf_op jit(solution)/shard_map/slice | solution.py:304
  43.6 0.1 collective-permute-start.3
  43.7 0.1 collective-permute-done.4.refs_4_
  43.8 0.9 %slice.38 = bf16[1,360,256]{2,1,0:T(8,128)(2,1)S(1)} slice(bf16[2,360,256]{2,1,0:T(8,128)(2,1)} %collective-permute-done.4.refs_4_), slice={[1:2], [0:360], [0:256]} | slice | bytes 368640 | tf_op jit(solution)/shard_map/slice | solution.py:304
  44.7 1.0 %collective-permute-start.5 = (bf16[1,360,256]{2,1,0:T(8,128)(2,1)S(1)}, bf16[1,360,256]{2,1,0:T(8,128)(2,1)S(1)}, u32[]{:S(2)}, u32[]{:S(2)}) collective-permute-start(bf16[1,360,256]{2,1,0:T(8,128)(2,1)S(1)} %slice.38), channel_id=1, source_target_pairs={{0,16},{16,0},{32,48},{48,32},{64,80},{80,64},{96,112},{112,96},{1... | collective-permute-start | bytes 552968 | tf_op jit(solution)/shard_map/ppermute | solution.py:304
  45.6 0.0 collective-permute-done.6.refs_6_
  45.6 0.9 %slice.39 = bf16[1,360,256]{2,1,0:T(8,128)(2,1)S(1)} slice(bf16[2,360,256]{2,1,0:T(8,128)(2,1)} %collective-permute-done.6.refs_6_), slice={[1:2], [0:360], [0:256]} | slice | bytes 368640 | tf_op jit(solution)/shard_map/slice | solution.py:304
  46.6 0.1 collective-permute-start.7
  46.7 0.0 collective-permute-done.1.refs_1_
  46.7 0.0 collective-permute-done.3.refs_3_
  46.7 0.0 collective-permute-done.5.refs_5_
  46.7 1.4 %collective-permute-done.7.refs_7_ = bf16[1,360,256]{2,1,0:T(8,128)(2,1)S(1)} collective-permute-done((bf16[1,360,256]{2,1,0:T(8,128)(2,1)S(1)}, bf16[1,360,256]{2,1,0:T(8,128)(2,1)S(1)}, u32[]{:S(2)}, u32[]{:S(2)}) %collective-permute-start.7) | collective-permute-done | bytes 184352 | tf_op jit(solution)/shard_map/ppermute | solution.py:304
  48.1 7.5 %all-to-all-done.1.got_ref = f32[128,8,128]{2,1,0:T(8,128)S(1)} async-done(((f32[128,8,128]{2,1,0:T(8,128)}), f32[128,8,128]{2,1,0:T(8,128)S(1)}, u32[]{:S(2)}, u32[]{:S(2)}) %all-to-all-start.1) | async-done | bytes 524320 | tf_op jit(solution)/shard_map/all_to_all | solution.py:303
  55.6 0.9 %shard_map.51 = f32[128,8,128]{2,1,0:T(8,128)} custom-call(f32[128,8,128]{2,1,0:T(8,128)S(1)} %all-to-all-done.1.got_ref), custom_call_target="tpu_custom_call" | custom-call | flops 131072 | bytes 1048576 | tf_op jit(solution)/shard_map/pallas_call | solution.py:160
  56.4 4.0 %all-to-all-start.2 = ((f32[128,8,128]{2,1,0:T(8,128)}), f32[128,8,128]{2,1,0:T(8,128)S(1)}, u32[]{:S(2)}, u32[]{:S(2)}) async-start(f32[128,8,128]{2,1,0:T(8,128)} %shard_map.51), calls=%async_computation.2 | async-start | bytes 1048576 | tf_op jit(solution)/shard_map/all_to_all | solution.py:306
  60.5 2.4 %shard_map.52.z_ref = bf16[360,2048]{1,0:T(8,128)(2,1)S(1)} custom-call(s32[8]{0:T(128)S(1)} %fusion.6.place_ref, bf16[2,360,256]{2,1,0:T(8,128)(2,1)S(1)} %get-tuple-element.23.refs_0_, bf16[1,360,256]{2,1,0:T(8,128)(2,1)S(1)} %collective-permute-done.1.refs_1_, bf16[2,360,256]{2,1,0:T(8,128)(2,1)} %collective-permute-done.2.refs_2_, ...), custom_call_target="tpu_custom_call" | custom-call | bytes 11796480 | tf_op jit(solution)/shard_map/pallas_call | solution.py:221
  62.8 11.8 %all-to-all-done.2 = f32[128,8,128]{2,1,0:T(8,128)S(1)} async-done(((f32[128,8,128]{2,1,0:T(8,128)}), f32[128,8,128]{2,1,0:T(8,128)S(1)}, u32[]{:S(2)}, u32[]{:S(2)}) %all-to-all-start.2) | async-done | bytes 524320 | tf_op jit(solution)/shard_map/all_to_all | solution.py:306
  74.6 1.5 %shard_map.53 = f32[4,64,90]{2,1,0:T(8,128)} custom-call(f32[8,16,8,128]{3,2,1,0:T(8,128)S(1)} %bitcast.18, bf16[360,2048]{1,0:T(8,128)(2,1)S(1)} %shard_map.52.z_ref, f32[4,90]{1,0:T(4,128)S(1)} %convert_multiply_fusion.factor_ref), custom_call_target="tpu_custom_call" | custom-call | flops 94371840 | bytes 1998848 | tf_op jit(solution)/shard_map/pallas_call | solution.py:253
  (7 shorter events, 0.1 us)
Async XLA Ops:
  2.3 5.8 %copy-start.4 = (s32[4,90]{1,0:T(4,128)S(1)}, s32[4,90]{1,0:T(4,128)}, u32[]{:S(2)}) copy-start(s32[4,90]{1,0:T(4,128)} %param.7) | copy-start | bytes 4324
  2.3 25.5 %all-to-all-start = ((bf16[8,360,256]{2,1,0:T(8,128)(2,1)}), bf16[8,360,256]{2,1,0:T(8,128)(2,1)S(1)}, u32[]{:S(2)}, u32[]{:S(2)}) async-start(bf16[8,360,256]{2,1,0:T(8,128)(2,1)} %bitcast.21), calls=%async_computation | async-start | bytes 2949120 | tf_op jit(solution)/shard_map/all_to_all | solution.py:284
  8.1 5.5 %collective-permute-start = (s32[4,90]{1,0:T(4,128)S(1)}, s32[4,90]{1,0:T(4,128)S(1)}, u32[]{:S(2)}, u32[]{:S(2)}) collective-permute-start(s32[4,90]{1,0:T(4,128)S(1)} %copy-done.4), channel_id=1, source_target_pairs={{0,16},{16,0},{32,48},{48,32},{64,80},{80,64},{96,112},{112,96},{1... | collective-permute-start | bytes 4328 | tf_op jit(solution)/shard_map/ppermute | solution.py:292
  8.2 1.4 %copy-start.2 = (bf16[32,90,256]{2,0,1:T(8,128)(2,1)S(1)}, bf16[32,90,256]{2,0,1:T(8,128)(2,1)}, u32[]{:S(2)}) copy-start(bf16[32,90,256]{2,0,1:T(8,128)(2,1)} %param.5) | copy-start | bytes 4423684
  11.6 1.0 %copy-start.3 = (f32[2048,64]{0,1:T(8,128)S(1)}, f32[2048,64]{0,1:T(8,128)}, u32[]{:S(2)}) copy-start(f32[2048,64]{0,1:T(8,128)} %param.6) | copy-start | bytes 1572868
  12.8 0.9 %copy-start = (bf16[192,2048]{1,0:T(8,128)(2,1)}, bf16[192,2048]{1,0:T(8,128)(2,1)S(1)}, u32[]{:S(2)}) copy-start(bf16[192,2048]{1,0:T(8,128)(2,1)S(1)} %shard_map.49.e_ref) | copy-start | bytes 2359300
  14.0 28.6 %collective-permute-start.2 = (bf16[2,360,256]{2,1,0:T(8,128)(2,1)}, bf16[2,360,256]{2,1,0:T(8,128)(2,1)}, u32[]{:S(2)}, u32[]{:S(2)}) collective-permute-start(bf16[2,360,256]{2,1,0:T(8,128)(2,1)} %get-tuple-element.15), channel_id=1, source_target_pairs={{0,32},{16,48},{32,64},{48,80},{64,96},{80,112},{96,0},{112,16},{1... | collective-permute-start | bytes 1105928 | tf_op jit(solution)/shard_map/ppermute | solution.py:295
  15.7 28.0 %collective-permute-start.4 = (bf16[2,360,256]{2,1,0:T(8,128)(2,1)}, bf16[2,360,256]{2,1,0:T(8,128)(2,1)}, u32[]{:S(2)}, u32[]{:S(2)}) collective-permute-start(bf16[2,360,256]{2,1,0:T(8,128)(2,1)} %get-tuple-element.16), channel_id=1, source_target_pairs={{0,64},{16,80},{32,96},{48,112},{64,0},{80,16},{96,32},{112,48},{1... | collective-permute-start | bytes 1105928 | tf_op jit(solution)/shard_map/ppermute | solution.py:295
  18.1 27.5 %collective-permute-start.6 = (bf16[2,360,256]{2,1,0:T(8,128)(2,1)}, bf16[2,360,256]{2,1,0:T(8,128)(2,1)}, u32[]{:S(2)}, u32[]{:S(2)}) collective-permute-start(bf16[2,360,256]{2,1,0:T(8,128)(2,1)} %get-tuple-element.17), channel_id=1, source_target_pairs={{0,96},{16,112},{32,0},{48,16},{64,32},{80,48},{96,64},{112,80},{1... | collective-permute-start | bytes 1105928 | tf_op jit(solution)/shard_map/ppermute | solution.py:295
  27.8 1.4 %copy-start.1 = (bf16[192,2048]{1,0:T(8,128)(2,1)S(1)}, bf16[192,2048]{1,0:T(8,128)(2,1)}, u32[]{:S(2)}) copy-start(bf16[192,2048]{1,0:T(8,128)(2,1)} %copy-done) | copy-start | bytes 2359300
  31.9 23.6 %all-to-all-start.1 = ((f32[128,8,128]{2,1,0:T(8,128)}), f32[128,8,128]{2,1,0:T(8,128)S(1)}, u32[]{:S(2)}, u32[]{:S(2)}) async-start(f32[128,8,128]{2,1,0:T(8,128)} %bitcast.11), calls=%async_computation.1 | async-start | bytes 1048576 | tf_op jit(solution)/shard_map/all_to_all | solution.py:303
  41.5 5.2 %collective-permute-start.1 = (bf16[1,360,256]{2,1,0:T(8,128)(2,1)S(1)}, bf16[1,360,256]{2,1,0:T(8,128)(2,1)S(1)}, u32[]{:S(2)}, u32[]{:S(2)}) collective-permute-start(bf16[1,360,256]{2,1,0:T(8,128)(2,1)S(1)} %slice.36), channel_id=1, source_target_pairs={{0,16},{16,0},{32,48},{48,32},{64,80},{80,64},{96,112},{112,96},{1... | collective-permute-start | bytes 552968 | tf_op jit(solution)/shard_map/ppermute | solution.py:304
  43.6 3.1 %collective-permute-start.3 = (bf16[1,360,256]{2,1,0:T(8,128)(2,1)S(1)}, bf16[1,360,256]{2,1,0:T(8,128)(2,1)S(1)}, u32[]{:S(2)}, u32[]{:S(2)}) collective-permute-start(bf16[1,360,256]{2,1,0:T(8,128)(2,1)S(1)} %slice.37), channel_id=1, source_target_pairs={{0,16},{16,0},{32,48},{48,32},{64,80},{80,64},{96,112},{112,96},{1... | collective-permute-start | bytes 552968 | tf_op jit(solution)/shard_map/ppermute | solution.py:304
  44.7 2.0 %collective-permute-start.5 = (bf16[1,360,256]{2,1,0:T(8,128)(2,1)S(1)}, bf16[1,360,256]{2,1,0:T(8,128)(2,1)S(1)}, u32[]{:S(2)}, u32[]{:S(2)}) collective-permute-start(bf16[1,360,256]{2,1,0:T(8,128)(2,1)S(1)} %slice.38), channel_id=1, source_target_pairs={{0,16},{16,0},{32,48},{48,32},{64,80},{80,64},{96,112},{112,96},{1... | collective-permute-start | bytes 552968 | tf_op jit(solution)/shard_map/ppermute | solution.py:304
  46.6 1.5 %collective-permute-start.7 = (bf16[1,360,256]{2,1,0:T(8,128)(2,1)S(1)}, bf16[1,360,256]{2,1,0:T(8,128)(2,1)S(1)}, u32[]{:S(2)}, u32[]{:S(2)}) collective-permute-start(bf16[1,360,256]{2,1,0:T(8,128)(2,1)S(1)} %slice.39), channel_id=1, source_target_pairs={{0,16},{16,0},{32,48},{48,32},{64,80},{80,64},{96,112},{112,96},{1... | collective-permute-start | bytes 552968 | tf_op jit(solution)/shard_map/ppermute | solution.py:304
  56.4 18.2 %all-to-all-start.2 = ((f32[128,8,128]{2,1,0:T(8,128)}), f32[128,8,128]{2,1,0:T(8,128)S(1)}, u32[]{:S(2)}, u32[]{:S(2)}) async-start(f32[128,8,128]{2,1,0:T(8,128)} %shard_map.51), calls=%async_computation.2 | async-start | bytes 1048576 | tf_op jit(solution)/shard_map/all_to_all | solution.py:306

commit v9 on v8

--- a/solution.py
+++ b/solution.py
@@ -12,6 +12,7 @@
 BF16 = jnp.bfloat16
 EPS = 1e-05
 PACK_VMEM = 56 * 1024 * 1024
+PARTS = 3
 NT = (((1,), (1,)), ((), ()))
 NN = (((1,), (0,)), ((), ()))
 
@@ -33,15 +34,21 @@
 
 
 def pack_kernel(in_ref, out_ref, held, loaded, stored):
-    halves, _, octets, _, _ = in_ref.shape
-    places = [(o, h) for o in range(octets) for h in range(halves)]
+    halves, lons, octets, _, _ = in_ref.shape
+    part = lons // PARTS
+    places = [
+        (o, h, slice(p * part, (p + 1) * part if p < PARTS - 1 else lons))
+        for o in range(octets)
+        for h in range(halves)
+        for p in range(PARTS)
+    ]
     loads = [
-        pltpu.make_async_copy(in_ref.at[h, :, o], held.at[o, h], loaded.at[n])
-        for n, (o, h) in enumerate(places)
+        pltpu.make_async_copy(in_ref.at[h, run, o], held.at[o, h, run], loaded.at[n])
+        for n, (o, h, run) in enumerate(places)
     ]
     stores = [
-        pltpu.make_async_copy(held.at[o, h], out_ref.at[o, h], stored.at[n])
-        for n, (o, h) in enumerate(places)
+        pltpu.make_async_copy(held.at[o, h, run], out_ref.at[o, h, run], stored.at[n])
+        for n, (o, h, run) in enumerate(places)
     ]
     for load in loads:
         load.start()
@@ -62,8 +69,8 @@
         out_shape=jax.ShapeDtypeStruct(shape, field.dtype),
         scratch_shapes=[
             pltpu.VMEM(shape, field.dtype),
-            pltpu.SemaphoreType.DMA((octets * halves,)),
-            pltpu.SemaphoreType.DMA((octets * halves,)),
+            pltpu.SemaphoreType.DMA((octets * halves * PARTS,)),
+            pltpu.SemaphoreType.DMA((octets * halves * PARTS,)),
         ],
         compiler_params=pltpu.CompilerParams(vmem_limit_bytes=PACK_VMEM),
         cost_estimate=pl.CostEstimate(flops=0, bytes_accessed=4 * field.size, transcendentals=0),
@@ -108,8 +115,7 @@
 
 def sums_kernel(z_ref, e_ref, out_ref):
     modes = out_ref.shape[0]
-    loadings = lax.dot_general(z_ref[...], e_ref[...], NT, preferred_element_type=F32)
-    turned = loadings.T
+    turned = lax.dot_general(e_ref[...], z_ref[...], NT, preferred_element_type=F32)
     turned = turned[:modes] + (turned[modes : 2 * modes] + turned[2 * modes :])
     stacked = jnp.concatenate(three_terms(turned), axis=0)
     hours = out_ref.shape[1]

time: 76.6 us -> 76.7 us (level)
  transfers between devices with their start and end apart: 11 -> 11, of which waited for: 5 -> 5; matrix products, arithmetic and copies ran while one was open for 6% -> 6% of each run, Pallas kernels for 10% -> 9%
where the time goes in v9:
time: 76.7 us; the launch traced here: 76.2 us
  waiting for transfers between devices  29.7 us (39%)
  starting transfers between devices  27 us (35%)
  Pallas kernels  11.7 us (15%)
  local copies, waits for them, and re-layouts  7.37 us (10%)
    all_to_all x1, waiting for transfers between devices, per_device(): pcs = lax.all_to_all(sum_for_all(got), BOTH, 0, 0)  11.7 us
    all_to_all x1, starting transfers between devices, per_device(): got = lax.all_to_all(blocks, BOTH, 0, 0)  9.54 us
    all_to_all x1, waiting for transfers between devices, per_device(): temp = lax.all_to_all(temp, 'tm', 0, 0)  8.54 us
    all_to_all x1, waiting for transfers between devices, per_device(): got = lax.all_to_all(blocks, BOTH, 0, 0)  7.41 us
    all_to_all x1, starting transfers between devices, per_device(): temp = lax.all_to_all(temp, 'tm', 0, 0)  5.81 us
    ppermute x3, starting transfers between devices, per_device(): lax.ppermute(sent[d - 1], 'tm', to_chip[d])  5.3 us
    all_to_all x1, starting transfers between devices, per_device(): pcs = lax.all_to_all(sum_for_all(got), BOTH, 0, 0)  4 us
    unnamed x10, local copies, waits for them, and re-layouts  3.28 us
  transfers between devices with their start and end apart: 11, of which 5 were waited for; matrix products, arithmetic and copies ran while one was open for 6% of the time, Pallas kernels for 9%

profile of v9, /device:TPU:1, one launch (start us, length us, event | category | flops | bytes accessed | tf_op | source)
XLA Modules:
  0.0 76.2 jit_solution(3777219755287375272)
XLA Ops:
  0.0 2.5 %shard_map.46 = bf16[4,2,45,8,256]{4,3,2,1,0:T(8,128)(2,1)} custom-call(bf16[2,45,4,8,256]{4,3,2,1,0:T(8,128)(2,1)} %bitcast.22), custom_call_target="tpu_custom_call" | custom-call | bytes 2949120 | tf_op jit(solution)/shard_map/pallas_call | solution.py:65
  2.5 0.0 copy-start.4
  2.5 5.8 %all-to-all-start = ((bf16[8,360,256]{2,1,0:T(8,128)(2,1)}), bf16[8,360,256]{2,1,0:T(8,128)(2,1)S(1)}, u32[]{:S(2)}, u32[]{:S(2)}) async-start(bf16[8,360,256]{2,1,0:T(8,128)(2,1)} %bitcast.21), calls=%async_computation | async-start | bytes 2949120 | tf_op jit(solution)/shard_map/all_to_all | solution.py:290
  8.3 0.0 copy-done.4
  8.3 0.1 collective-permute-start
  8.4 0.0 copy-start.2
  8.4 1.4 %copy-done.2 = bf16[32,90,256]{2,0,1:T(8,128)(2,1)S(1)} copy-done((bf16[32,90,256]{2,0,1:T(8,128)(2,1)S(1)}, bf16[32,90,256]{2,0,1:T(8,128)(2,1)}, u32[]{:S(2)}) %copy-start.2) | copy-done | bytes 1474584
  9.8 0.9 %shard_map.47 = bf16[8,360,256]{2,1,0:T(8,128)(2,1)S(1)} custom-call(s32[8]{0:T(128)S(1)} %fusion.2.place_ref, bf16[90,32,256]{2,1,0:T(8,128)(2,1)S(1)} %bitcast.19), custom_call_target="tpu_custom_call" | custom-call | bytes 2949120 | tf_op jit(solution)/shard_map/pallas_call | solution.py:193
  10.7 1.0 %fusion.7 = (bf16[2,360,256]{2,1,0:T(8,128)(2,1)S(1)}, bf16[2,360,256]{2,1,0:T(8,128)(2,1)}, bf16[2,360,256]{2,1,0:T(8,128)(2,1)}, bf16[2,360,256]{2,1,0:T(8,128)(2,1)}) fusion(bf16[8,360,256]{2,1,0:T(8,128)(2,1)S(1)} %shard_map.47), kind=kLoop, calls=%fused_computation.19 | loop fusion | bytes 2949120 | tf_op jit(solution)/shard_map/slice | solution.py:296
  11.8 0.0 copy-start.3
  11.8 1.0 %copy-done.3 = f32[2048,64]{0,1:T(8,128)S(1)} copy-done((f32[2048,64]{0,1:T(8,128)S(1)}, f32[2048,64]{0,1:T(8,128)}, u32[]{:S(2)}) %copy-start.3) | copy-done | bytes 524312
  12.8 0.2 shard_map.49.e_ref
  13.0 0.0 copy-start
  13.0 0.9 %copy-done = bf16[192,2048]{1,0:T(8,128)(2,1)} copy-done((bf16[192,2048]{1,0:T(8,128)(2,1)}, bf16[192,2048]{1,0:T(8,128)(2,1)S(1)}, u32[]{:S(2)}) %copy-start) | copy-done | bytes 786456
  13.8 0.0 collective-permute-done
  13.9 0.1 broadcast_multiply_fusion
  13.9 0.1 dynamic-slice_bitcast_fusion
  14.0 0.1 copy.7
  14.1 0.1 reshape.33.w_ref
  14.2 1.7 %collective-permute-start.2 = (bf16[2,360,256]{2,1,0:T(8,128)(2,1)}, bf16[2,360,256]{2,1,0:T(8,128)(2,1)}, u32[]{:S(2)}, u32[]{:S(2)}) collective-permute-start(bf16[2,360,256]{2,1,0:T(8,128)(2,1)} %get-tuple-element.15), channel_id=1, source_target_pairs={{0,32},{16,48},{32,64},{48,80},{64,96},{80,112},{96,0},{112,16},{1... | collective-permute-start | bytes 1105928 | tf_op jit(solution)/shard_map/ppermute | solution.py:301
  15.9 2.4 %collective-permute-start.4 = (bf16[2,360,256]{2,1,0:T(8,128)(2,1)}, bf16[2,360,256]{2,1,0:T(8,128)(2,1)}, u32[]{:S(2)}, u32[]{:S(2)}) collective-permute-start(bf16[2,360,256]{2,1,0:T(8,128)(2,1)} %get-tuple-element.16), channel_id=1, source_target_pairs={{0,64},{16,80},{32,96},{48,112},{64,0},{80,16},{96,32},{112,48},{1... | collective-permute-start | bytes 1105928 | tf_op jit(solution)/shard_map/ppermute | solution.py:301
  18.3 1.2 %collective-permute-start.6 = (bf16[2,360,256]{2,1,0:T(8,128)(2,1)}, bf16[2,360,256]{2,1,0:T(8,128)(2,1)}, u32[]{:S(2)}, u32[]{:S(2)}) collective-permute-start(bf16[2,360,256]{2,1,0:T(8,128)(2,1)} %get-tuple-element.17), channel_id=1, source_target_pairs={{0,96},{16,112},{32,0},{48,16},{64,32},{80,48},{96,64},{112,80},{1... | collective-permute-start | bytes 1105928 | tf_op jit(solution)/shard_map/ppermute | solution.py:301
  19.5 8.5 %all-to-all-done.t_ref = bf16[8,360,256]{2,1,0:T(8,128)(2,1)S(1)} async-done(((bf16[8,360,256]{2,1,0:T(8,128)(2,1)}), bf16[8,360,256]{2,1,0:T(8,128)(2,1)S(1)}, u32[]{:S(2)}, u32[]{:S(2)}) %all-to-all-start) | async-done | bytes 1474592 | tf_op jit(solution)/shard_map/all_to_all | solution.py:290
  28.0 0.0 copy-start.1
  28.0 1.3 %shard_map.48.z_ref = bf16[360,2048]{1,0:T(8,128)(2,1)S(1)} custom-call(bf16[8,360,256]{2,1,0:T(8,128)(2,1)S(1)} %all-to-all-done.t_ref, f32[1,360]{1,0:T(1,128)S(1)} %reshape.33.w_ref), custom_call_target="tpu_custom_call" | custom-call | flops 11796480 | bytes 2949120 | tf_op jit(solution)/shard_map/pallas_call | solution.py:131
  29.4 0.0 copy-done.1
  29.4 2.1 %shard_map.50 = f32[64,2048]{1,0:T(8,128)} custom-call(bf16[360,2048]{1,0:T(8,128)(2,1)S(1)} %shard_map.48.z_ref, bf16[192,2048]{1,0:T(8,128)(2,1)S(1)} %copy-done.1), custom_call_target="tpu_custom_call" | custom-call | flops 566231040 | bytes 2260992 | tf_op jit(solution)/shard_map/pallas_call | solution.py:139
  31.5 9.5 %all-to-all-start.1 = ((f32[128,8,128]{2,1,0:T(8,128)}), f32[128,8,128]{2,1,0:T(8,128)S(1)}, u32[]{:S(2)}, u32[]{:S(2)}) async-start(f32[128,8,128]{2,1,0:T(8,128)} %bitcast.11), calls=%async_computation.1 | async-start | bytes 1048576 | tf_op jit(solution)/shard_map/all_to_all | solution.py:309
  41.1 1.1 %collective-permute-start.1 = (bf16[1,360,256]{2,1,0:T(8,128)(2,1)S(1)}, bf16[1,360,256]{2,1,0:T(8,128)(2,1)S(1)}, u32[]{:S(2)}, u32[]{:S(2)}) collective-permute-start(bf16[1,360,256]{2,1,0:T(8,128)(2,1)S(1)} %slice.36), channel_id=1, source_target_pairs={{0,16},{16,0},{32,48},{48,32},{64,80},{80,64},{96,112},{112,96},{1... | collective-permute-start | bytes 552968 | tf_op jit(solution)/shard_map/ppermute | solution.py:310
  42.3 0.0 collective-permute-done.2.refs_2_
  42.3 0.9 %slice.37 = bf16[1,360,256]{2,1,0:T(8,128)(2,1)S(1)} slice(bf16[2,360,256]{2,1,0:T(8,128)(2,1)} %collective-permute-done.2.refs_2_), slice={[1:2], [0:360], [0:256]} | slice | bytes 368640 | tf_op jit(solution)/shard_map/slice | solution.py:310
  43.2 0.1 collective-permute-start.3
  43.3 0.6 collective-permute-done.4.refs_4_
  43.9 0.9 %slice.38 = bf16[1,360,256]{2,1,0:T(8,128)(2,1)S(1)} slice(bf16[2,360,256]{2,1,0:T(8,128)(2,1)} %collective-permute-done.4.refs_4_), slice={[1:2], [0:360], [0:256]} | slice | bytes 368640 | tf_op jit(solution)/shard_map/slice | solution.py:310
  44.9 1.0 %collective-permute-start.5 = (bf16[1,360,256]{2,1,0:T(8,128)(2,1)S(1)}, bf16[1,360,256]{2,1,0:T(8,128)(2,1)S(1)}, u32[]{:S(2)}, u32[]{:S(2)}) collective-permute-start(bf16[1,360,256]{2,1,0:T(8,128)(2,1)S(1)} %slice.38), channel_id=1, source_target_pairs={{0,16},{16,0},{32,48},{48,32},{64,80},{80,64},{96,112},{112,96},{1... | collective-permute-start | bytes 552968 | tf_op jit(solution)/shard_map/ppermute | solution.py:310
  45.8 0.0 collective-permute-done.6.refs_6_
  45.8 0.9 %slice.39 = bf16[1,360,256]{2,1,0:T(8,128)(2,1)S(1)} slice(bf16[2,360,256]{2,1,0:T(8,128)(2,1)} %collective-permute-done.6.refs_6_), slice={[1:2], [0:360], [0:256]} | slice | bytes 368640 | tf_op jit(solution)/shard_map/slice | solution.py:310
  46.8 0.1 collective-permute-start.7
  46.9 0.0 collective-permute-done.1.refs_1_
  46.9 0.0 collective-permute-done.3.refs_3_
  46.9 0.0 collective-permute-done.5.refs_5_
  46.9 1.4 %collective-permute-done.7.refs_7_ = bf16[1,360,256]{2,1,0:T(8,128)(2,1)S(1)} collective-permute-done((bf16[1,360,256]{2,1,0:T(8,128)(2,1)S(1)}, bf16[1,360,256]{2,1,0:T(8,128)(2,1)S(1)}, u32[]{:S(2)}, u32[]{:S(2)}) %collective-permute-start.7) | collective-permute-done | bytes 184352 | tf_op jit(solution)/shard_map/ppermute | solution.py:310
  48.3 7.4 %all-to-all-done.1.got_ref = f32[128,8,128]{2,1,0:T(8,128)S(1)} async-done(((f32[128,8,128]{2,1,0:T(8,128)}), f32[128,8,128]{2,1,0:T(8,128)S(1)}, u32[]{:S(2)}, u32[]{:S(2)}) %all-to-all-start.1) | async-done | bytes 524320 | tf_op jit(solution)/shard_map/all_to_all | solution.py:309
  55.7 0.9 %shard_map.51 = f32[128,8,128]{2,1,0:T(8,128)} custom-call(f32[128,8,128]{2,1,0:T(8,128)S(1)} %all-to-all-done.1.got_ref), custom_call_target="tpu_custom_call" | custom-call | flops 131072 | bytes 1048576 | tf_op jit(solution)/shard_map/pallas_call | solution.py:166
  56.6 4.0 %all-to-all-start.2 = ((f32[128,8,128]{2,1,0:T(8,128)}), f32[128,8,128]{2,1,0:T(8,128)S(1)}, u32[]{:S(2)}, u32[]{:S(2)}) async-start(f32[128,8,128]{2,1,0:T(8,128)} %shard_map.51), calls=%async_computation.2 | async-start | bytes 1048576 | tf_op jit(solution)/shard_map/all_to_all | solution.py:312
  60.6 2.4 %shard_map.52.z_ref = bf16[360,2048]{1,0:T(8,128)(2,1)S(1)} custom-call(s32[8]{0:T(128)S(1)} %fusion.6.place_ref, bf16[2,360,256]{2,1,0:T(8,128)(2,1)S(1)} %get-tuple-element.23.refs_0_, bf16[1,360,256]{2,1,0:T(8,128)(2,1)S(1)} %collective-permute-done.1.refs_1_, bf16[2,360,256]{2,1,0:T(8,128)(2,1)} %collective-permute-done.2.refs_2_, ...), custom_call_target="tpu_custom_call" | custom-call | bytes 11796480 | tf_op jit(solution)/shard_map/pallas_call | solution.py:227
  62.9 11.7 %all-to-all-done.2 = f32[128,8,128]{2,1,0:T(8,128)S(1)} async-done(((f32[128,8,128]{2,1,0:T(8,128)}), f32[128,8,128]{2,1,0:T(8,128)S(1)}, u32[]{:S(2)}, u32[]{:S(2)}) %all-to-all-start.2) | async-done | bytes 524320 | tf_op jit(solution)/shard_map/all_to_all | solution.py:312
  74.6 1.5 %shard_map.53 = f32[4,64,90]{2,1,0:T(8,128)} custom-call(f32[8,16,8,128]{3,2,1,0:T(8,128)S(1)} %bitcast.18, bf16[360,2048]{1,0:T(8,128)(2,1)S(1)} %shard_map.52.z_ref, f32[4,90]{1,0:T(4,128)S(1)} %convert_multiply_fusion.factor_ref), custom_call_target="tpu_custom_call" | custom-call | flops 94371840 | bytes 1998848 | tf_op jit(solution)/shard_map/pallas_call | solution.py:259
  (7 shorter events, 0.1 us)
Async XLA Ops:
  2.5 5.8 %copy-start.4 = (s32[4,90]{1,0:T(4,128)S(1)}, s32[4,90]{1,0:T(4,128)}, u32[]{:S(2)}) copy-start(s32[4,90]{1,0:T(4,128)} %param.7) | copy-start | bytes 4324
  2.5 25.5 %all-to-all-start = ((bf16[8,360,256]{2,1,0:T(8,128)(2,1)}), bf16[8,360,256]{2,1,0:T(8,128)(2,1)S(1)}, u32[]{:S(2)}, u32[]{:S(2)}) async-start(bf16[8,360,256]{2,1,0:T(8,128)(2,1)} %bitcast.21), calls=%async_computation | async-start | bytes 2949120 | tf_op jit(solution)/shard_map/all_to_all | solution.py:290
  8.3 5.5 %collective-permute-start = (s32[4,90]{1,0:T(4,128)S(1)}, s32[4,90]{1,0:T(4,128)S(1)}, u32[]{:S(2)}, u32[]{:S(2)}) collective-permute-start(s32[4,90]{1,0:T(4,128)S(1)} %copy-done.4), channel_id=1, source_target_pairs={{0,16},{16,0},{32,48},{48,32},{64,80},{80,64},{96,112},{112,96},{1... | collective-permute-start | bytes 4328 | tf_op jit(solution)/shard_map/ppermute | solution.py:298
  8.4 1.4 %copy-start.2 = (bf16[32,90,256]{2,0,1:T(8,128)(2,1)S(1)}, bf16[32,90,256]{2,0,1:T(8,128)(2,1)}, u32[]{:S(2)}) copy-start(bf16[32,90,256]{2,0,1:T(8,128)(2,1)} %param.5) | copy-start | bytes 4423684
  11.8 1.0 %copy-start.3 = (f32[2048,64]{0,1:T(8,128)S(1)}, f32[2048,64]{0,1:T(8,128)}, u32[]{:S(2)}) copy-start(f32[2048,64]{0,1:T(8,128)} %param.6) | copy-start | bytes 1572868
  13.0 0.9 %copy-start = (bf16[192,2048]{1,0:T(8,128)(2,1)}, bf16[192,2048]{1,0:T(8,128)(2,1)S(1)}, u32[]{:S(2)}) copy-start(bf16[192,2048]{1,0:T(8,128)(2,1)S(1)} %shard_map.49.e_ref) | copy-start | bytes 2359300
  14.2 28.1 %collective-permute-start.2 = (bf16[2,360,256]{2,1,0:T(8,128)(2,1)}, bf16[2,360,256]{2,1,0:T(8,128)(2,1)}, u32[]{:S(2)}, u32[]{:S(2)}) collective-permute-start(bf16[2,360,256]{2,1,0:T(8,128)(2,1)} %get-tuple-element.15), channel_id=1, source_target_pairs={{0,32},{16,48},{32,64},{48,80},{64,96},{80,112},{96,0},{112,16},{1... | collective-permute-start | bytes 1105928 | tf_op jit(solution)/shard_map/ppermute | solution.py:301
  15.9 28.0 %collective-permute-start.4 = (bf16[2,360,256]{2,1,0:T(8,128)(2,1)}, bf16[2,360,256]{2,1,0:T(8,128)(2,1)}, u32[]{:S(2)}, u32[]{:S(2)}) collective-permute-start(bf16[2,360,256]{2,1,0:T(8,128)(2,1)} %get-tuple-element.16), channel_id=1, source_target_pairs={{0,64},{16,80},{32,96},{48,112},{64,0},{80,16},{96,32},{112,48},{1... | collective-permute-start | bytes 1105928 | tf_op jit(solution)/shard_map/ppermute | solution.py:301
  18.3 27.5 %collective-permute-start.6 = (bf16[2,360,256]{2,1,0:T(8,128)(2,1)}, bf16[2,360,256]{2,1,0:T(8,128)(2,1)}, u32[]{:S(2)}, u32[]{:S(2)}) collective-permute-start(bf16[2,360,256]{2,1,0:T(8,128)(2,1)} %get-tuple-element.17), channel_id=1, source_target_pairs={{0,96},{16,112},{32,0},{48,16},{64,32},{80,48},{96,64},{112,80},{1... | collective-permute-start | bytes 1105928 | tf_op jit(solution)/shard_map/ppermute | solution.py:301
  28.0 1.4 %copy-start.1 = (bf16[192,2048]{1,0:T(8,128)(2,1)S(1)}, bf16[192,2048]{1,0:T(8,128)(2,1)}, u32[]{:S(2)}) copy-start(bf16[192,2048]{1,0:T(8,128)(2,1)} %copy-done) | copy-start | bytes 2359300
  31.5 24.1 %all-to-all-start.1 = ((f32[128,8,128]{2,1,0:T(8,128)}), f32[128,8,128]{2,1,0:T(8,128)S(1)}, u32[]{:S(2)}, u32[]{:S(2)}) async-start(f32[128,8,128]{2,1,0:T(8,128)} %bitcast.11), calls=%async_computation.1 | async-start | bytes 1048576 | tf_op jit(solution)/shard_map/all_to_all | solution.py:309
  41.1 5.8 %collective-permute-start.1 = (bf16[1,360,256]{2,1,0:T(8,128)(2,1)S(1)}, bf16[1,360,256]{2,1,0:T(8,128)(2,1)S(1)}, u32[]{:S(2)}, u32[]{:S(2)}) collective-permute-start(bf16[1,360,256]{2,1,0:T(8,128)(2,1)S(1)} %slice.36), channel_id=1, source_target_pairs={{0,16},{16,0},{32,48},{48,32},{64,80},{80,64},{96,112},{112,96},{1... | collective-permute-start | bytes 552968 | tf_op jit(solution)/shard_map/ppermute | solution.py:310
  43.2 3.7 %collective-permute-start.3 = (bf16[1,360,256]{2,1,0:T(8,128)(2,1)S(1)}, bf16[1,360,256]{2,1,0:T(8,128)(2,1)S(1)}, u32[]{:S(2)}, u32[]{:S(2)}) collective-permute-start(bf16[1,360,256]{2,1,0:T(8,128)(2,1)S(1)} %slice.37), channel_id=1, source_target_pairs={{0,16},{16,0},{32,48},{48,32},{64,80},{80,64},{96,112},{112,96},{1... | collective-permute-start | bytes 552968 | tf_op jit(solution)/shard_map/ppermute | solution.py:310
  44.9 2.0 %collective-permute-start.5 = (bf16[1,360,256]{2,1,0:T(8,128)(2,1)S(1)}, bf16[1,360,256]{2,1,0:T(8,128)(2,1)S(1)}, u32[]{:S(2)}, u32[]{:S(2)}) collective-permute-start(bf16[1,360,256]{2,1,0:T(8,128)(2,1)S(1)} %slice.38), channel_id=1, source_target_pairs={{0,16},{16,0},{32,48},{48,32},{64,80},{80,64},{96,112},{112,96},{1... | collective-permute-start | bytes 552968 | tf_op jit(solution)/shard_map/ppermute | solution.py:310
  46.8 1.5 %collective-permute-start.7 = (bf16[1,360,256]{2,1,0:T(8,128)(2,1)S(1)}, bf16[1,360,256]{2,1,0:T(8,128)(2,1)S(1)}, u32[]{:S(2)}, u32[]{:S(2)}) collective-permute-start(bf16[1,360,256]{2,1,0:T(8,128)(2,1)S(1)} %slice.39), channel_id=1, source_target_pairs={{0,16},{16,0},{32,48},{48,32},{64,80},{80,64},{96,112},{112,96},{1... | collective-permute-start | bytes 552968 | tf_op jit(solution)/shard_map/ppermute | solution.py:310
  56.6 18.1 %all-to-all-start.2 = ((f32[128,8,128]{2,1,0:T(8,128)}), f32[128,8,128]{2,1,0:T(8,128)S(1)}, u32[]{:S(2)}, u32[]{:S(2)}) async-start(f32[128,8,128]{2,1,0:T(8,128)} %shard_map.51), calls=%async_computation.2 | async-start | bytes 1048576 | tf_op jit(solution)/shard_map/all_to_all | solution.py:312

commit v10 on v9

--- a/solution.py
+++ b/solution.py
@@ -158,14 +158,14 @@
         parts.append(part)
     while len(parts) > 1:
         parts = [parts[n] + parts[n + 1] for n in range(0, len(parts), 2)]
-    for n in range(count):
+    for n in range(out_ref.shape[0]):
         out_ref[n] = parts[0]
 
 
-def sum_for_all(got):
+def sum_for_all(got, copies):
     return pl.pallas_call(
         sum_kernel,
-        out_shape=jax.ShapeDtypeStruct(got.shape, F32),
+        out_shape=jax.ShapeDtypeStruct((copies, *got.shape[1:]), F32),
         compiler_params=params(),
         cost_estimate=pl.CostEstimate(flops=got.size, bytes_accessed=8 * got.size, transcendentals=0),
     )(got)
@@ -236,13 +236,16 @@
     )(places, *pieces)
 
 
-def final_kernel(pcs_ref, z_ref, factor_ref, out_ref, rows_ref):
-    octets, runs, _, _ = pcs_ref.shape
+def final_kernel(core_ref, own_ref, other_ref, z_ref, factor_ref, out_ref, rows_ref):
+    octets, runs, _, _ = own_ref.shape
+    core = core_ref[0]
     lats, modes, lons = out_ref.shape
     hours = runs * 128
     rows = []
-    for r in range(octets):
-        pcs = jnp.concatenate([pcs_ref[r, c] for c in range(runs)], axis=1)
+    for r in range(2 * octets):
+        own = jnp.concatenate([own_ref[r // 2, c] for c in range(runs)], axis=1)
+        other = jnp.concatenate([other_ref[r // 2, c] for c in range(runs)], axis=1)
+        pcs = jnp.where(core == r % 2, own, other)
         centered = pcs - jnp.sum(pcs, axis=1, keepdims=True) / hours
         variance = jnp.sum(centered * centered, axis=1, keepdims=True) / hours
         rows.append(centered * lax.rsqrt(variance + EPS))
@@ -253,18 +256,20 @@
         out_ref[i] = picked.T[:modes] * factor_ref[i : i + 1, :]
 
 
-def correlate(pcs, scores, factor):
+def correlate(core, own, other, scores, factor):
     lats, lons = factor.shape
-    modes = pcs.shape[0] * pcs.shape[2]
+    modes = 2 * own.shape[0] * own.shape[2]
+    vmem = pl.BlockSpec(memory_space=pltpu.VMEM)
     return pl.pallas_call(
         final_kernel,
+        in_specs=[pl.BlockSpec(memory_space=pltpu.SMEM), vmem, vmem, vmem, vmem],
         out_shape=jax.ShapeDtypeStruct((lats, modes, lons), F32),
         scratch_shapes=[pltpu.VMEM((lats * lons, 128), F32)],
         compiler_params=params(),
         cost_estimate=pl.CostEstimate(
-            flops=2 * scores.size * modes, bytes_accessed=4 * pcs.size + 2 * scores.size, transcendentals=0
+            flops=2 * scores.size * modes, bytes_accessed=8 * own.size + 2 * scores.size, transcendentals=0
         ),
-    )(pcs, scores, factor)
+    )(core.reshape(1), own, other, scores, factor)
 
 
 def area_root(rows, total_lat):
@@ -277,6 +282,7 @@
     lats = marine_indicator.shape[0]
     hours, modes = gram_eigenvector_columns.shape
     members = lax.axis_size("tm")
+    others = lax.axis_size("space")
     chips = members // 2
     me = lax.axis_index("tm")
     chip, core = lax.div(me, 2), lax.rem(me, 2)
@@ -309,13 +315,17 @@
     got = lax.all_to_all(blocks, BOTH, 0, 0)
     traded = [lax.ppermute(blocks[1:2], "tm", to_core) for blocks in [own, *arrived]]
     got, *traded = lax.optimization_barrier((got, *traded))
-    pcs = lax.all_to_all(sum_for_all(got), BOTH, 0, 0)
-    pcs = pcs.reshape(modes // 8, hours // 128, 8, 128)
+    kinds = [
+        [t * others + n for t in range(kind, members, 2) for n in range(others)] for kind in range(2)
+    ]
+    pcs = lax.all_to_all(sum_for_all(got, chips * others), BOTH, 0, 0, axis_index_groups=kinds)
+    pcs = pcs.reshape(chips, others, 8, 128)
+    pcs_other = lax.ppermute(pcs, "tm", to_core)
 
     pieces = [piece for both in zip([own, *arrived], traded) for piece in both]
     places = 2 * lax.rem(chip + chips - lax.div(band, 2), chips) + lax.rem(band + core, 2)
     scores = hum_scores(places, pieces)
-    return correlate(pcs, scores, mask_float / hours).transpose(0, 2, 1)
+    return correlate(core, pcs, pcs_other, scores, mask_float / hours).transpose(0, 2, 1)
 
 
 def solution(mesh):

time: 76.7 us -> 76.9 us (level)
  starting transfers between devices: 27 us -> 29.7 us
  waiting for transfers between devices: 29.7 us -> 27.3 us
    all_to_all x1, waiting for transfers between devices: 11.7 us -> 9.33 us  [per_device(): lax.all_to_all(sum_for_all(got, chips * others), BOTH, 0, 0, axis_index_g...]
    ppermute x0 -> x1, starting transfers between devices: none -> 2.04 us  [per_device(): pcs_other = lax.ppermute(pcs, 'tm', to_core)]
  transfers between devices with their start and end apart: 11 -> 12, of which waited for: 5 -> 5; matrix products, arithmetic and copies ran while one was open for 6% -> 6% of each run, Pallas kernels for 9% -> 9%
where the time goes in v10:
time: 76.9 us; the launch traced here: 76.4 us
  starting transfers between devices  29.7 us (39%)
  waiting for transfers between devices  27.3 us (36%)
  Pallas kernels  11.6 us (15%)
  local copies, waits for them, and re-layouts  7.41 us (10%)
    all_to_all x1, starting transfers between devices, per_device(): got = lax.all_to_all(blocks, BOTH, 0, 0)  9.54 us
    all_to_all x1, waiting for transfers between devices, per_device(): lax.all_to_all(sum_for_all(got, chips * others), BOTH, 0, 0, axis_index_g...  9.33 us
    all_to_all x1, waiting for transfers between devices, per_device(): temp = lax.all_to_all(temp, 'tm', 0, 0)  8.51 us
    all_to_all x1, waiting for transfers between devices, per_device(): got = lax.all_to_all(blocks, BOTH, 0, 0)  7.41 us
    all_to_all x1, starting transfers between devices, per_device(): temp = lax.all_to_all(temp, 'tm', 0, 0)  5.81 us
    ppermute x3, starting transfers between devices, per_device(): lax.ppermute(sent[d - 1], 'tm', to_chip[d])  5.3 us
    all_to_all x1, starting transfers between devices, per_device(): lax.all_to_all(sum_for_all(got, chips * others), BOTH, 0, 0, axis_index_g...  4.61 us
    unnamed x10, local copies, waits for them, and re-layouts  3.29 us
  transfers between devices with their start and end apart: 12, of which 5 were waited for; matrix products, arithmetic and copies ran while one was open for 6% of the time, Pallas kernels for 9%

profile of v10, /device:TPU:1, one launch (start us, length us, event | category | flops | bytes accessed | tf_op | source)
XLA Modules:
  0.0 76.4 jit_solution(5035268401109554264)
XLA Ops:
  0.0 2.5 %shard_map.46 = bf16[4,2,45,8,256]{4,3,2,1,0:T(8,128)(2,1)} custom-call(bf16[2,45,4,8,256]{4,3,2,1,0:T(8,128)(2,1)} %bitcast.24), custom_call_target="tpu_custom_call" | custom-call | bytes 2949120 | tf_op jit(solution)/shard_map/pallas_call | solution.py:65
  2.5 0.0 copy-start.4
  2.5 5.8 %all-to-all-start = ((bf16[8,360,256]{2,1,0:T(8,128)(2,1)}), bf16[8,360,256]{2,1,0:T(8,128)(2,1)S(1)}, u32[]{:S(2)}, u32[]{:S(2)}) async-start(bf16[8,360,256]{2,1,0:T(8,128)(2,1)} %bitcast.23), calls=%async_computation | async-start | bytes 2949120 | tf_op jit(solution)/shard_map/all_to_all | solution.py:296
  8.3 0.0 copy-done.4
  8.3 0.1 collective-permute-start
  8.4 0.0 copy-start.2
  8.5 1.4 %copy-done.2 = bf16[32,90,256]{2,0,1:T(8,128)(2,1)S(1)} copy-done((bf16[32,90,256]{2,0,1:T(8,128)(2,1)S(1)}, bf16[32,90,256]{2,0,1:T(8,128)(2,1)}, u32[]{:S(2)}) %copy-start.2) | copy-done | bytes 1474584
  9.8 0.9 %shard_map.47 = bf16[8,360,256]{2,1,0:T(8,128)(2,1)S(1)} custom-call(s32[8]{0:T(128)S(1)} %fusion.2.place_ref, bf16[90,32,256]{2,1,0:T(8,128)(2,1)S(1)} %bitcast.19), custom_call_target="tpu_custom_call" | custom-call | bytes 2949120 | tf_op jit(solution)/shard_map/pallas_call | solution.py:193
  10.7 1.0 %fusion.7 = (bf16[2,360,256]{2,1,0:T(8,128)(2,1)S(1)}, bf16[2,360,256]{2,1,0:T(8,128)(2,1)}, bf16[2,360,256]{2,1,0:T(8,128)(2,1)}, bf16[2,360,256]{2,1,0:T(8,128)(2,1)}) fusion(bf16[8,360,256]{2,1,0:T(8,128)(2,1)S(1)} %shard_map.47), kind=kLoop, calls=%fused_computation.19 | loop fusion | bytes 2949120 | tf_op jit(solution)/shard_map/slice | solution.py:302
  11.8 0.0 copy-start.3
  11.8 1.0 %copy-done.3 = f32[2048,64]{0,1:T(8,128)S(1)} copy-done((f32[2048,64]{0,1:T(8,128)S(1)}, f32[2048,64]{0,1:T(8,128)}, u32[]{:S(2)}) %copy-start.3) | copy-done | bytes 524312
  12.8 0.2 shard_map.49.e_ref
  13.0 0.0 copy-start
  13.0 0.9 %copy-done = bf16[192,2048]{1,0:T(8,128)(2,1)} copy-done((bf16[192,2048]{1,0:T(8,128)(2,1)}, bf16[192,2048]{1,0:T(8,128)(2,1)S(1)}, u32[]{:S(2)}) %copy-start) | copy-done | bytes 786456
  13.9 0.0 collective-permute-done
  13.9 0.1 broadcast_multiply_fusion
  14.0 0.1 dynamic-slice_bitcast_fusion
  14.0 0.1 copy.7
  14.1 0.1 reshape.37.w_ref
  14.2 1.7 %collective-permute-start.2 = (bf16[2,360,256]{2,1,0:T(8,128)(2,1)}, bf16[2,360,256]{2,1,0:T(8,128)(2,1)}, u32[]{:S(2)}, u32[]{:S(2)}) collective-permute-start(bf16[2,360,256]{2,1,0:T(8,128)(2,1)} %get-tuple-element.15), channel_id=1, source_target_pairs={{0,32},{16,48},{32,64},{48,80},{64,96},{80,112},{96,0},{112,16},{1... | collective-permute-start | bytes 1105928 | tf_op jit(solution)/shard_map/ppermute | solution.py:307
  16.0 2.4 %collective-permute-start.4 = (bf16[2,360,256]{2,1,0:T(8,128)(2,1)}, bf16[2,360,256]{2,1,0:T(8,128)(2,1)}, u32[]{:S(2)}, u32[]{:S(2)}) collective-permute-start(bf16[2,360,256]{2,1,0:T(8,128)(2,1)} %get-tuple-element.16), channel_id=1, source_target_pairs={{0,64},{16,80},{32,96},{48,112},{64,0},{80,16},{96,32},{112,48},{1... | collective-permute-start | bytes 1105928 | tf_op jit(solution)/shard_map/ppermute | solution.py:307
  18.4 1.2 %collective-permute-start.6 = (bf16[2,360,256]{2,1,0:T(8,128)(2,1)}, bf16[2,360,256]{2,1,0:T(8,128)(2,1)}, u32[]{:S(2)}, u32[]{:S(2)}) collective-permute-start(bf16[2,360,256]{2,1,0:T(8,128)(2,1)} %get-tuple-element.17), channel_id=1, source_target_pairs={{0,96},{16,112},{32,0},{48,16},{64,32},{80,48},{96,64},{112,80},{1... | collective-permute-start | bytes 1105928 | tf_op jit(solution)/shard_map/ppermute | solution.py:307
  19.5 8.5 %all-to-all-done.t_ref = bf16[8,360,256]{2,1,0:T(8,128)(2,1)S(1)} async-done(((bf16[8,360,256]{2,1,0:T(8,128)(2,1)}), bf16[8,360,256]{2,1,0:T(8,128)(2,1)S(1)}, u32[]{:S(2)}, u32[]{:S(2)}) %all-to-all-start) | async-done | bytes 1474592 | tf_op jit(solution)/shard_map/all_to_all | solution.py:296
  28.1 0.0 copy-start.1
  28.1 1.3 %shard_map.48.z_ref = bf16[360,2048]{1,0:T(8,128)(2,1)S(1)} custom-call(bf16[8,360,256]{2,1,0:T(8,128)(2,1)S(1)} %all-to-all-done.t_ref, f32[1,360]{1,0:T(1,128)S(1)} %reshape.37.w_ref), custom_call_target="tpu_custom_call" | custom-call | flops 11796480 | bytes 2949120 | tf_op jit(solution)/shard_map/pallas_call | solution.py:131
  29.4 0.0 copy-done.1
  29.4 2.1 %shard_map.50 = f32[64,2048]{1,0:T(8,128)} custom-call(bf16[360,2048]{1,0:T(8,128)(2,1)S(1)} %shard_map.48.z_ref, bf16[192,2048]{1,0:T(8,128)(2,1)S(1)} %copy-done.1), custom_call_target="tpu_custom_call" | custom-call | flops 566231040 | bytes 2260992 | tf_op jit(solution)/shard_map/pallas_call | solution.py:139
  31.5 9.5 %all-to-all-start.1 = ((f32[128,8,128]{2,1,0:T(8,128)}), f32[128,8,128]{2,1,0:T(8,128)S(1)}, u32[]{:S(2)}, u32[]{:S(2)}) async-start(f32[128,8,128]{2,1,0:T(8,128)} %bitcast.12), calls=%async_computation.1 | async-start | bytes 1048576 | tf_op jit(solution)/shard_map/all_to_all | solution.py:315
  41.1 1.1 %collective-permute-start.1 = (bf16[1,360,256]{2,1,0:T(8,128)(2,1)S(1)}, bf16[1,360,256]{2,1,0:T(8,128)(2,1)S(1)}, u32[]{:S(2)}, u32[]{:S(2)}) collective-permute-start(bf16[1,360,256]{2,1,0:T(8,128)(2,1)S(1)} %slice.36), channel_id=1, source_target_pairs={{0,16},{16,0},{32,48},{48,32},{64,80},{80,64},{96,112},{112,96},{1... | collective-permute-start | bytes 552968 | tf_op jit(solution)/shard_map/ppermute | solution.py:316
  42.3 0.0 collective-permute-done.2.refs_2_
  42.3 0.9 %slice.37 = bf16[1,360,256]{2,1,0:T(8,128)(2,1)S(1)} slice(bf16[2,360,256]{2,1,0:T(8,128)(2,1)} %collective-permute-done.2.refs_2_), slice={[1:2], [0:360], [0:256]} | slice | bytes 368640 | tf_op jit(solution)/shard_map/slice | solution.py:316
  43.2 0.1 collective-permute-start.3
  43.3 0.7 collective-permute-done.4.refs_4_
  44.0 0.9 %slice.38 = bf16[1,360,256]{2,1,0:T(8,128)(2,1)S(1)} slice(bf16[2,360,256]{2,1,0:T(8,128)(2,1)} %collective-permute-done.4.refs_4_), slice={[1:2], [0:360], [0:256]} | slice | bytes 368640 | tf_op jit(solution)/shard_map/slice | solution.py:316
  44.9 1.0 %collective-permute-start.5 = (bf16[1,360,256]{2,1,0:T(8,128)(2,1)S(1)}, bf16[1,360,256]{2,1,0:T(8,128)(2,1)S(1)}, u32[]{:S(2)}, u32[]{:S(2)}) collective-permute-start(bf16[1,360,256]{2,1,0:T(8,128)(2,1)S(1)} %slice.38), channel_id=1, source_target_pairs={{0,16},{16,0},{32,48},{48,32},{64,80},{80,64},{96,112},{112,96},{1... | collective-permute-start | bytes 552968 | tf_op jit(solution)/shard_map/ppermute | solution.py:316
  45.8 0.0 collective-permute-done.6.refs_6_
  45.8 0.9 %slice.39 = bf16[1,360,256]{2,1,0:T(8,128)(2,1)S(1)} slice(bf16[2,360,256]{2,1,0:T(8,128)(2,1)} %collective-permute-done.6.refs_6_), slice={[1:2], [0:360], [0:256]} | slice | bytes 368640 | tf_op jit(solution)/shard_map/slice | solution.py:316
  46.8 0.1 collective-permute-start.7
  46.9 0.0 collective-permute-done.1.refs_1_
  46.9 0.0 collective-permute-done.3.refs_3_
  46.9 0.0 collective-permute-done.5.refs_5_
  46.9 1.4 %collective-permute-done.7.refs_7_ = bf16[1,360,256]{2,1,0:T(8,128)(2,1)S(1)} collective-permute-done((bf16[1,360,256]{2,1,0:T(8,128)(2,1)S(1)}, bf16[1,360,256]{2,1,0:T(8,128)(2,1)S(1)}, u32[]{:S(2)}, u32[]{:S(2)}) %collective-permute-start.7) | collective-permute-done | bytes 184352 | tf_op jit(solution)/shard_map/ppermute | solution.py:316
  48.3 7.4 %all-to-all-done.1.got_ref = f32[128,8,128]{2,1,0:T(8,128)S(1)} async-done(((f32[128,8,128]{2,1,0:T(8,128)}), f32[128,8,128]{2,1,0:T(8,128)S(1)}, u32[]{:S(2)}, u32[]{:S(2)}) %all-to-all-start.1) | async-done | bytes 524320 | tf_op jit(solution)/shard_map/all_to_all | solution.py:315
  55.7 0.7 shard_map.51
  56.4 4.6 %all-to-all-start.2 = ((f32[64,8,128]{2,1,0:T(8,128)}), f32[64,8,128]{2,1,0:T(8,128)S(1)}, u32[]{:S(2)}, u32[]{:S(2)}) async-start(f32[64,8,128]{2,1,0:T(8,128)} %shard_map.51), calls=%async_computation.2 | async-start | bytes 524288 | tf_op jit(solution)/shard_map/all_to_all | solution.py:321
  61.1 9.3 %all-to-all-done.2 = f32[64,8,128]{2,1,0:T(8,128)S(1)} async-done(((f32[64,8,128]{2,1,0:T(8,128)}), f32[64,8,128]{2,1,0:T(8,128)S(1)}, u32[]{:S(2)}, u32[]{:S(2)}) %all-to-all-start.2) | async-done | bytes 262176 | tf_op jit(solution)/shard_map/all_to_all | solution.py:321
  70.4 2.0 %collective-permute-start.8 = (f32[4,16,8,128]{3,2,1,0:T(8,128)S(1)}, f32[4,16,8,128]{3,2,1,0:T(8,128)S(1)}, u32[]{:S(2)}, u32[]{:S(2)}) collective-permute-start(f32[4,16,8,128]{3,2,1,0:T(8,128)S(1)} %bitcast.20), channel_id=1, source_target_pairs={{0,16},{16,0},{32,48},{48,32},{64,80},{80,64},{96,112},{112,96},{1... | collective-permute-start | bytes 786440 | tf_op jit(solution)/shard_map/ppermute | solution.py:323
  72.5 2.4 %shard_map.52.z_ref = bf16[360,2048]{1,0:T(8,128)(2,1)S(1)} custom-call(s32[8]{0:T(128)S(1)} %fusion.6.place_ref, bf16[2,360,256]{2,1,0:T(8,128)(2,1)S(1)} %get-tuple-element.23.refs_0_, bf16[1,360,256]{2,1,0:T(8,128)(2,1)S(1)} %collective-permute-done.1.refs_1_, bf16[2,360,256]{2,1,0:T(8,128)(2,1)} %collective-permute-done.2.refs_2_, ...), custom_call_target="tpu_custom_call" | custom-call | bytes 11796480 | tf_op jit(solution)/shard_map/pallas_call | solution.py:227
  74.8 0.0 collective-permute-done.8.other_ref
  74.8 1.5 %shard_map.53 = f32[4,64,90]{2,1,0:T(8,128)} custom-call(s32[1]{0:T(128)} %bitcast.core_ref, f32[4,16,8,128]{3,2,1,0:T(8,128)S(1)} %bitcast.21, f32[4,16,8,128]{3,2,1,0:T(8,128)S(1)} %collective-permute-done.8.other_ref, bf16[360,2048]{1,0:T(8,128)(2,1)S(1)} %shard_map.52.z_ref, f32[4,90]{1,0:T(4,128)S(1)} %convert_multiply_fusion.factor_ref), custom_call_target="tpu_custom_call" | custom-call | flops 94371840 | bytes 1998848 | tf_op jit(solution)/shard_map/pallas_call | solution.py:263
  (7 shorter events, 0.1 us)
Async XLA Ops:
  2.5 5.8 %copy-start.4 = (s32[4,90]{1,0:T(4,128)S(1)}, s32[4,90]{1,0:T(4,128)}, u32[]{:S(2)}) copy-start(s32[4,90]{1,0:T(4,128)} %param.7) | copy-start | bytes 4324
  2.5 25.5 %all-to-all-start = ((bf16[8,360,256]{2,1,0:T(8,128)(2,1)}), bf16[8,360,256]{2,1,0:T(8,128)(2,1)S(1)}, u32[]{:S(2)}, u32[]{:S(2)}) async-start(bf16[8,360,256]{2,1,0:T(8,128)(2,1)} %bitcast.23), calls=%async_computation | async-start | bytes 2949120 | tf_op jit(solution)/shard_map/all_to_all | solution.py:296
  8.3 5.5 %collective-permute-start = (s32[4,90]{1,0:T(4,128)S(1)}, s32[4,90]{1,0:T(4,128)S(1)}, u32[]{:S(2)}, u32[]{:S(2)}) collective-permute-start(s32[4,90]{1,0:T(4,128)S(1)} %copy-done.4), channel_id=1, source_target_pairs={{0,16},{16,0},{32,48},{48,32},{64,80},{80,64},{96,112},{112,96},{1... | collective-permute-start | bytes 4328 | tf_op jit(solution)/shard_map/ppermute | solution.py:304
  8.4 1.4 %copy-start.2 = (bf16[32,90,256]{2,0,1:T(8,128)(2,1)S(1)}, bf16[32,90,256]{2,0,1:T(8,128)(2,1)}, u32[]{:S(2)}) copy-start(bf16[32,90,256]{2,0,1:T(8,128)(2,1)} %param.5) | copy-start | bytes 4423684
  11.8 1.0 %copy-start.3 = (f32[2048,64]{0,1:T(8,128)S(1)}, f32[2048,64]{0,1:T(8,128)}, u32[]{:S(2)}) copy-start(f32[2048,64]{0,1:T(8,128)} %param.6) | copy-start | bytes 1572868
  13.0 0.9 %copy-start = (bf16[192,2048]{1,0:T(8,128)(2,1)}, bf16[192,2048]{1,0:T(8,128)(2,1)S(1)}, u32[]{:S(2)}) copy-start(bf16[192,2048]{1,0:T(8,128)(2,1)S(1)} %shard_map.49.e_ref) | copy-start | bytes 2359300
  14.2 28.0 %collective-permute-start.2 = (bf16[2,360,256]{2,1,0:T(8,128)(2,1)}, bf16[2,360,256]{2,1,0:T(8,128)(2,1)}, u32[]{:S(2)}, u32[]{:S(2)}) collective-permute-start(bf16[2,360,256]{2,1,0:T(8,128)(2,1)} %get-tuple-element.15), channel_id=1, source_target_pairs={{0,32},{16,48},{32,64},{48,80},{64,96},{80,112},{96,0},{112,16},{1... | collective-permute-start | bytes 1105928 | tf_op jit(solution)/shard_map/ppermute | solution.py:307
  16.0 28.0 %collective-permute-start.4 = (bf16[2,360,256]{2,1,0:T(8,128)(2,1)}, bf16[2,360,256]{2,1,0:T(8,128)(2,1)}, u32[]{:S(2)}, u32[]{:S(2)}) collective-permute-start(bf16[2,360,256]{2,1,0:T(8,128)(2,1)} %get-tuple-element.16), channel_id=1, source_target_pairs={{0,64},{16,80},{32,96},{48,112},{64,0},{80,16},{96,32},{112,48},{1... | collective-permute-start | bytes 1105928 | tf_op jit(solution)/shard_map/ppermute | solution.py:307
  18.4 27.5 %collective-permute-start.6 = (bf16[2,360,256]{2,1,0:T(8,128)(2,1)}, bf16[2,360,256]{2,1,0:T(8,128)(2,1)}, u32[]{:S(2)}, u32[]{:S(2)}) collective-permute-start(bf16[2,360,256]{2,1,0:T(8,128)(2,1)} %get-tuple-element.17), channel_id=1, source_target_pairs={{0,96},{16,112},{32,0},{48,16},{64,32},{80,48},{96,64},{112,80},{1... | collective-permute-start | bytes 1105928 | tf_op jit(solution)/shard_map/ppermute | solution.py:307
  28.1 1.4 %copy-start.1 = (bf16[192,2048]{1,0:T(8,128)(2,1)S(1)}, bf16[192,2048]{1,0:T(8,128)(2,1)}, u32[]{:S(2)}) copy-start(bf16[192,2048]{1,0:T(8,128)(2,1)} %copy-done) | copy-start | bytes 2359300
  31.5 24.2 %all-to-all-start.1 = ((f32[128,8,128]{2,1,0:T(8,128)}), f32[128,8,128]{2,1,0:T(8,128)S(1)}, u32[]{:S(2)}, u32[]{:S(2)}) async-start(f32[128,8,128]{2,1,0:T(8,128)} %bitcast.12), calls=%async_computation.1 | async-start | bytes 1048576 | tf_op jit(solution)/shard_map/all_to_all | solution.py:315
  41.1 5.8 %collective-permute-start.1 = (bf16[1,360,256]{2,1,0:T(8,128)(2,1)S(1)}, bf16[1,360,256]{2,1,0:T(8,128)(2,1)S(1)}, u32[]{:S(2)}, u32[]{:S(2)}) collective-permute-start(bf16[1,360,256]{2,1,0:T(8,128)(2,1)S(1)} %slice.36), channel_id=1, source_target_pairs={{0,16},{16,0},{32,48},{48,32},{64,80},{80,64},{96,112},{112,96},{1... | collective-permute-start | bytes 552968 | tf_op jit(solution)/shard_map/ppermute | solution.py:316
  43.2 3.7 %collective-permute-start.3 = (bf16[1,360,256]{2,1,0:T(8,128)(2,1)S(1)}, bf16[1,360,256]{2,1,0:T(8,128)(2,1)S(1)}, u32[]{:S(2)}, u32[]{:S(2)}) collective-permute-start(bf16[1,360,256]{2,1,0:T(8,128)(2,1)S(1)} %slice.37), channel_id=1, source_target_pairs={{0,16},{16,0},{32,48},{48,32},{64,80},{80,64},{96,112},{112,96},{1... | collective-permute-start | bytes 552968 | tf_op jit(solution)/shard_map/ppermute | solution.py:316
  44.9 2.0 %collective-permute-start.5 = (bf16[1,360,256]{2,1,0:T(8,128)(2,1)S(1)}, bf16[1,360,256]{2,1,0:T(8,128)(2,1)S(1)}, u32[]{:S(2)}, u32[]{:S(2)}) collective-permute-start(bf16[1,360,256]{2,1,0:T(8,128)(2,1)S(1)} %slice.38), channel_id=1, source_target_pairs={{0,16},{16,0},{32,48},{48,32},{64,80},{80,64},{96,112},{112,96},{1... | collective-permute-start | bytes 552968 | tf_op jit(solution)/shard_map/ppermute | solution.py:316
  46.8 1.5 %collective-permute-start.7 = (bf16[1,360,256]{2,1,0:T(8,128)(2,1)S(1)}, bf16[1,360,256]{2,1,0:T(8,128)(2,1)S(1)}, u32[]{:S(2)}, u32[]{:S(2)}) collective-permute-start(bf16[1,360,256]{2,1,0:T(8,128)(2,1)S(1)} %slice.39), channel_id=1, source_target_pairs={{0,16},{16,0},{32,48},{48,32},{64,80},{80,64},{96,112},{112,96},{1... | collective-permute-start | bytes 552968 | tf_op jit(solution)/shard_map/ppermute | solution.py:316
  56.4 14.0 %all-to-all-start.2 = ((f32[64,8,128]{2,1,0:T(8,128)}), f32[64,8,128]{2,1,0:T(8,128)S(1)}, u32[]{:S(2)}, u32[]{:S(2)}) async-start(f32[64,8,128]{2,1,0:T(8,128)} %shard_map.51), calls=%async_computation.2 | async-start | bytes 524288 | tf_op jit(solution)/shard_map/all_to_all | solution.py:321
  70.4 4.4 %collective-permute-start.8 = (f32[4,16,8,128]{3,2,1,0:T(8,128)S(1)}, f32[4,16,8,128]{3,2,1,0:T(8,128)S(1)}, u32[]{:S(2)}, u32[]{:S(2)}) collective-permute-start(f32[4,16,8,128]{3,2,1,0:T(8,128)S(1)} %bitcast.20), channel_id=1, source_target_pairs={{0,16},{16,0},{32,48},{48,32},{64,80},{80,64},{96,112},{112,96},{1... | collective-permute-start | bytes 786440 | tf_op jit(solution)/shard_map/ppermute | solution.py:323

commit v11 on v10

--- a/solution.py
+++ b/solution.py
@@ -236,40 +236,58 @@
     )(places, *pieces)
 
 
-def final_kernel(core_ref, own_ref, other_ref, z_ref, factor_ref, out_ref, rows_ref):
-    octets, runs, _, _ = own_ref.shape
-    core = core_ref[0]
-    lats, modes, lons = out_ref.shape
-    hours = runs * 128
+def correlations(pcs_ref, z_ref, factor_ref, rows_ref):
+    octets, runs, _, _ = pcs_ref.shape
+    lats, lons = factor_ref.shape
+    modes, hours = 8 * octets, runs * 128
     rows = []
-    for r in range(2 * octets):
-        own = jnp.concatenate([own_ref[r // 2, c] for c in range(runs)], axis=1)
-        other = jnp.concatenate([other_ref[r // 2, c] for c in range(runs)], axis=1)
-        pcs = jnp.where(core == r % 2, own, other)
+    for r in range(octets):
+        pcs = jnp.concatenate([pcs_ref[r, c] for c in range(runs)], axis=1)
         centered = pcs - jnp.sum(pcs, axis=1, keepdims=True) / hours
         variance = jnp.sum(centered * centered, axis=1, keepdims=True) / hours
         rows.append(centered * lax.rsqrt(variance + EPS))
     pcz = jnp.concatenate(rows, axis=0).astype(BF16)
     rows_ref[:, :modes] = lax.dot_general(z_ref[...], pcz, NT, preferred_element_type=F32)
-    for i in range(lats):
-        picked = rows_ref[pl.ds(i, lons, stride=lats), :]
-        out_ref[i] = picked.T[:modes] * factor_ref[i : i + 1, :]
+    return [
+        rows_ref[pl.ds(i, lons, stride=lats), :].T[:modes] * factor_ref[i : i + 1, :]
+        for i in range(lats)
+    ]
+
+
+def own_kernel(pcs_ref, z_ref, factor_ref, out_ref, rows_ref):
+    for i, values in enumerate(correlations(pcs_ref, z_ref, factor_ref, rows_ref)):
+        out_ref[i] = values
+
+
+def both_kernel(core_ref, pcs_ref, z_ref, factor_ref, own_ref, out_ref, rows_ref):
+    core = core_ref[0]
+    for i, other in enumerate(correlations(pcs_ref, z_ref, factor_ref, rows_ref)):
+        own = own_ref[i]
+        for r in range(out_ref.shape[1] // 8):
+            half = slice(8 * (r // 2), 8 * (r // 2) + 8)
+            out_ref[i, 8 * r : 8 * r + 8, :] = jnp.where(core == r % 2, own[half], other[half])
 
 
 def correlate(core, own, other, scores, factor):
     lats, lons = factor.shape
-    modes = 2 * own.shape[0] * own.shape[2]
+    modes = own.shape[0] * own.shape[2]
     vmem = pl.BlockSpec(memory_space=pltpu.VMEM)
-    return pl.pallas_call(
-        final_kernel,
+    settings = dict(
+        scratch_shapes=[pltpu.VMEM((lats * lons, 128), F32)],
+        compiler_params=params(),
+        cost_estimate=pl.CostEstimate(
+            flops=2 * scores.size * modes, bytes_accessed=4 * own.size + 2 * scores.size, transcendentals=0
+        ),
+    )
+    first = pl.pallas_call(
+        own_kernel, out_shape=jax.ShapeDtypeStruct((lats, modes, lons), F32), **settings
+    )(own, scores, factor)
+    return pl.pallas_call(
+        both_kernel,
         in_specs=[pl.BlockSpec(memory_space=pltpu.SMEM), vmem, vmem, vmem, vmem],
-        out_shape=jax.ShapeDtypeStruct((lats, modes, lons), F32),
-        scratch_shapes=[pltpu.VMEM((lats * lons, 128), F32)],
-        compiler_params=params(),
-        cost_estimate=pl.CostEstimate(
-            flops=2 * scores.size * modes, bytes_accessed=8 * own.size + 2 * scores.size, transcendentals=0
-        ),
-    )(core.reshape(1), own, other, scores, factor)
+        out_shape=jax.ShapeDtypeStruct((lats, 2 * modes, lons), F32),
+        **settings,
+    )(core.reshape(1), other, scores, factor, first)
 
 
 def area_root(rows, total_lat):
@@ -314,7 +332,10 @@
     blocks = blocks.transpose(0, 2, 1, 3).reshape(-1, 8, 128)
     got = lax.all_to_all(blocks, BOTH, 0, 0)
     traded = [lax.ppermute(blocks[1:2], "tm", to_core) for blocks in [own, *arrived]]
-    got, *traded = lax.optimization_barrier((got, *traded))
+    pieces = [piece for both in zip([own, *arrived], traded) for piece in both]
+    places = 2 * lax.rem(chip + chips - lax.div(band, 2), chips) + lax.rem(band + core, 2)
+    scores = hum_scores(places, pieces)
+    got, scores = lax.optimization_barrier((got, scores))
     kinds = [
         [t * others + n for t in range(kind, members, 2) for n in range(others)] for kind in range(2)
     ]
@@ -322,9 +343,6 @@
     pcs = pcs.reshape(chips, others, 8, 128)
     pcs_other = lax.ppermute(pcs, "tm", to_core)
 
-    pieces = [piece for both in zip([own, *arrived], traded) for piece in both]
-    places = 2 * lax.rem(chip + chips - lax.div(band, 2), chips) + lax.rem(band + core, 2)
-    scores = hum_scores(places, pieces)
     return correlate(core, pcs, pcs_other, scores, mask_float / hours).transpose(0, 2, 1)
 
 

time: 76.9 us -> 74.5 us (0.969)
  blocking collectives: 0 us -> 13.3 us
  waiting for transfers between devices: 27.3 us -> 16 us
  starting transfers between devices: 29.7 us -> 25.4 us
    all_to_all x0 -> x1, blocking collectives: none -> 13.3 us  [per_device(): lax.all_to_all(sum_for_all(got, chips * others), BOTH, 0, 0, axis_index_g...]
    all_to_all x1 -> x0, waiting for transfers between devices: 9.33 us -> none  [per_device(): lax.all_to_all(sum_for_all(got, chips * others), BOTH, 0, 0, axis_index_g...]
    all_to_all x1 -> x0, starting transfers between devices: 4.61 us -> none  [per_device(): lax.all_to_all(sum_for_all(got, chips * others), BOTH, 0, 0, axis_index_g...]
    all_to_all x1, waiting for transfers between devices: 7.41 us -> 5.05 us  [per_device(): got = lax.all_to_all(blocks, BOTH, 0, 0)]
    pallas_call x1 -> x2, Pallas kernels: 1.53 us -> 2.28 us  [the longest x1 1.48 us: correlate(): pl.pallas_call(both_kernel, in_specs=[pl.BlockSpec(memory_space=pltpu.SME...]
  transfers between devices with their start and end apart: 12 -> 11, of which waited for: 5 -> 5; matrix products, arithmetic and copies ran while one was open for 6% -> 6% of each run, Pallas kernels for 9% -> 10%
where the time goes in v11:
time: 74.5 us; the launch traced here: 74 us
  starting transfers between devices  25.4 us (34%)
  waiting for transfers between devices  16 us (21%)
  blocking collectives  13.3 us (18%)
  Pallas kernels  11.7 us (16%)
  local copies, waits for them, and re-layouts  7.37 us (10%)
    all_to_all x1, blocking collectives, per_device(): lax.all_to_all(sum_for_all(got, chips * others), BOTH, 0, 0, axis_index_g...  13.3 us
    all_to_all x1, starting transfers between devices, per_device(): got = lax.all_to_all(blocks, BOTH, 0, 0)  9.52 us
    all_to_all x1, waiting for transfers between devices, per_device(): temp = lax.all_to_all(temp, 'tm', 0, 0)  8.55 us
    all_to_all x1, starting transfers between devices, per_device(): temp = lax.all_to_all(temp, 'tm', 0, 0)  5.81 us
    ppermute x3, starting transfers between devices, per_device(): lax.ppermute(sent[d - 1], 'tm', to_chip[d])  5.3 us
    all_to_all x1, waiting for transfers between devices, per_device(): got = lax.all_to_all(blocks, BOTH, 0, 0)  5.05 us
    unnamed x10, local copies, waits for them, and re-layouts  3.28 us
    slice x4, local copies, waits for them, and re-layouts, per_device(): blocks[1:2]  2.82 us
  transfers between devices with their start and end apart: 11, of which 5 were waited for; matrix products, arithmetic and copies ran while one was open for 6% of the time, Pallas kernels for 10%

profile of v11, /device:TPU:1, one launch (start us, length us, event | category | flops | bytes accessed | tf_op | source)
XLA Modules:
  0.0 74.0 jit_solution(16311669118250947200)
XLA Ops:
  0.0 2.5 %shard_map.46 = bf16[4,2,45,8,256]{4,3,2,1,0:T(8,128)(2,1)} custom-call(bf16[2,45,4,8,256]{4,3,2,1,0:T(8,128)(2,1)} %bitcast.24), custom_call_target="tpu_custom_call" | custom-call | bytes 2949120 | tf_op jit(solution)/shard_map/pallas_call | solution.py:65
  2.5 0.0 copy-start.4
  2.5 5.8 %all-to-all-start = ((bf16[8,360,256]{2,1,0:T(8,128)(2,1)}), bf16[8,360,256]{2,1,0:T(8,128)(2,1)S(1)}, u32[]{:S(2)}, u32[]{:S(2)}) async-start(bf16[8,360,256]{2,1,0:T(8,128)(2,1)} %bitcast.23), calls=%async_computation | async-start | bytes 2949120 | tf_op jit(solution)/shard_map/all_to_all | solution.py:314
  8.3 0.0 copy-done.4
  8.3 0.1 collective-permute-start
  8.4 0.0 copy-start.2
  8.4 1.4 %copy-done.2 = bf16[32,90,256]{2,0,1:T(8,128)(2,1)S(1)} copy-done((bf16[32,90,256]{2,0,1:T(8,128)(2,1)S(1)}, bf16[32,90,256]{2,0,1:T(8,128)(2,1)}, u32[]{:S(2)}) %copy-start.2) | copy-done | bytes 1474584
  9.8 0.9 %shard_map.47 = bf16[8,360,256]{2,1,0:T(8,128)(2,1)S(1)} custom-call(s32[8]{0:T(128)S(1)} %fusion.2.place_ref, bf16[90,32,256]{2,1,0:T(8,128)(2,1)S(1)} %bitcast.19), custom_call_target="tpu_custom_call" | custom-call | bytes 2949120 | tf_op jit(solution)/shard_map/pallas_call | solution.py:193
  10.7 1.0 %fusion.7 = (bf16[2,360,256]{2,1,0:T(8,128)(2,1)S(1)}, bf16[2,360,256]{2,1,0:T(8,128)(2,1)}, bf16[2,360,256]{2,1,0:T(8,128)(2,1)}, bf16[2,360,256]{2,1,0:T(8,128)(2,1)}) fusion(bf16[8,360,256]{2,1,0:T(8,128)(2,1)S(1)} %shard_map.47), kind=kLoop, calls=%fused_computation.19 | loop fusion | bytes 2949120 | tf_op jit(solution)/shard_map/slice | solution.py:320
  11.7 0.0 copy-start.3
  11.8 1.0 %copy-done.3 = f32[2048,64]{0,1:T(8,128)S(1)} copy-done((f32[2048,64]{0,1:T(8,128)S(1)}, f32[2048,64]{0,1:T(8,128)}, u32[]{:S(2)}) %copy-start.3) | copy-done | bytes 524312
  12.8 0.2 shard_map.49.e_ref
  12.9 0.0 copy-start
  13.0 0.9 %copy-done = bf16[192,2048]{1,0:T(8,128)(2,1)} copy-done((bf16[192,2048]{1,0:T(8,128)(2,1)}, bf16[192,2048]{1,0:T(8,128)(2,1)S(1)}, u32[]{:S(2)}) %copy-start) | copy-done | bytes 786456
  13.8 0.0 collective-permute-done
  13.8 1.7 %collective-permute-start.2 = (bf16[2,360,256]{2,1,0:T(8,128)(2,1)}, bf16[2,360,256]{2,1,0:T(8,128)(2,1)}, u32[]{:S(2)}, u32[]{:S(2)}) collective-permute-start(bf16[2,360,256]{2,1,0:T(8,128)(2,1)} %get-tuple-element.12), channel_id=1, source_target_pairs={{0,32},{16,48},{32,64},{48,80},{64,96},{80,112},{96,0},{112,16},{1... | collective-permute-start | bytes 1105928 | tf_op jit(solution)/shard_map/ppermute | solution.py:325
  15.6 2.4 %collective-permute-start.4 = (bf16[2,360,256]{2,1,0:T(8,128)(2,1)}, bf16[2,360,256]{2,1,0:T(8,128)(2,1)}, u32[]{:S(2)}, u32[]{:S(2)}) collective-permute-start(bf16[2,360,256]{2,1,0:T(8,128)(2,1)} %get-tuple-element.13), channel_id=1, source_target_pairs={{0,64},{16,80},{32,96},{48,112},{64,0},{80,16},{96,32},{112,48},{1... | collective-permute-start | bytes 1105928 | tf_op jit(solution)/shard_map/ppermute | solution.py:325
  18.0 1.2 %collective-permute-start.6 = (bf16[2,360,256]{2,1,0:T(8,128)(2,1)}, bf16[2,360,256]{2,1,0:T(8,128)(2,1)}, u32[]{:S(2)}, u32[]{:S(2)}) collective-permute-start(bf16[2,360,256]{2,1,0:T(8,128)(2,1)} %get-tuple-element.14), channel_id=1, source_target_pairs={{0,96},{16,112},{32,0},{48,16},{64,32},{80,48},{96,64},{112,80},{1... | collective-permute-start | bytes 1105928 | tf_op jit(solution)/shard_map/ppermute | solution.py:325
  19.1 0.1 broadcast_multiply_fusion
  19.2 0.1 dynamic-slice_bitcast_fusion
  19.3 0.1 copy.7
  19.4 0.1 reshape.37.w_ref
  19.5 8.6 %all-to-all-done.t_ref = bf16[8,360,256]{2,1,0:T(8,128)(2,1)S(1)} async-done(((bf16[8,360,256]{2,1,0:T(8,128)(2,1)}), bf16[8,360,256]{2,1,0:T(8,128)(2,1)S(1)}, u32[]{:S(2)}, u32[]{:S(2)}) %all-to-all-start) | async-done | bytes 1474592 | tf_op jit(solution)/shard_map/all_to_all | solution.py:314
  28.0 0.0 copy-start.1
  28.0 1.3 %shard_map.48.z_ref = bf16[360,2048]{1,0:T(8,128)(2,1)S(1)} custom-call(bf16[8,360,256]{2,1,0:T(8,128)(2,1)S(1)} %all-to-all-done.t_ref, f32[1,360]{1,0:T(1,128)S(1)} %reshape.37.w_ref), custom_call_target="tpu_custom_call" | custom-call | flops 11796480 | bytes 2949120 | tf_op jit(solution)/shard_map/pallas_call | solution.py:131
  29.4 0.0 copy-done.1
  29.4 2.2 %shard_map.50 = f32[64,2048]{1,0:T(8,128)} custom-call(bf16[360,2048]{1,0:T(8,128)(2,1)S(1)} %shard_map.48.z_ref, bf16[192,2048]{1,0:T(8,128)(2,1)S(1)} %copy-done.1), custom_call_target="tpu_custom_call" | custom-call | flops 566231040 | bytes 2260992 | tf_op jit(solution)/shard_map/pallas_call | solution.py:139
  31.5 9.5 %all-to-all-start.1 = ((f32[128,8,128]{2,1,0:T(8,128)}), f32[128,8,128]{2,1,0:T(8,128)S(1)}, u32[]{:S(2)}, u32[]{:S(2)}) async-start(f32[128,8,128]{2,1,0:T(8,128)} %bitcast.12), calls=%async_computation.1 | async-start | bytes 1048576 | tf_op jit(solution)/shard_map/all_to_all | solution.py:333
  41.1 1.1 %collective-permute-start.1 = (bf16[1,360,256]{2,1,0:T(8,128)(2,1)S(1)}, bf16[1,360,256]{2,1,0:T(8,128)(2,1)S(1)}, u32[]{:S(2)}, u32[]{:S(2)}) collective-permute-start(bf16[1,360,256]{2,1,0:T(8,128)(2,1)S(1)} %slice.37), channel_id=1, source_target_pairs={{0,16},{16,0},{32,48},{48,32},{64,80},{80,64},{96,112},{112,96},{1... | collective-permute-start | bytes 552968 | tf_op jit(solution)/shard_map/ppermute | solution.py:334
  42.2 0.0 collective-permute-done.2.refs_2_
  42.2 0.9 %slice.38 = bf16[1,360,256]{2,1,0:T(8,128)(2,1)S(1)} slice(bf16[2,360,256]{2,1,0:T(8,128)(2,1)} %collective-permute-done.2.refs_2_), slice={[1:2], [0:360], [0:256]} | slice | bytes 368640 | tf_op jit(solution)/shard_map/slice | solution.py:334
  43.2 0.1 collective-permute-start.3
  43.3 0.6 collective-permute-done.4.refs_4_
  43.9 0.9 %slice.39 = bf16[1,360,256]{2,1,0:T(8,128)(2,1)S(1)} slice(bf16[2,360,256]{2,1,0:T(8,128)(2,1)} %collective-permute-done.4.refs_4_), slice={[1:2], [0:360], [0:256]} | slice | bytes 368640 | tf_op jit(solution)/shard_map/slice | solution.py:334
  44.9 1.0 %collective-permute-start.5 = (bf16[1,360,256]{2,1,0:T(8,128)(2,1)S(1)}, bf16[1,360,256]{2,1,0:T(8,128)(2,1)S(1)}, u32[]{:S(2)}, u32[]{:S(2)}) collective-permute-start(bf16[1,360,256]{2,1,0:T(8,128)(2,1)S(1)} %slice.39), channel_id=1, source_target_pairs={{0,16},{16,0},{32,48},{48,32},{64,80},{80,64},{96,112},{112,96},{1... | collective-permute-start | bytes 552968 | tf_op jit(solution)/shard_map/ppermute | solution.py:334
  45.8 0.0 collective-permute-done.6.refs_6_
  45.8 0.9 %slice.40 = bf16[1,360,256]{2,1,0:T(8,128)(2,1)S(1)} slice(bf16[2,360,256]{2,1,0:T(8,128)(2,1)} %collective-permute-done.6.refs_6_), slice={[1:2], [0:360], [0:256]} | slice | bytes 368640 | tf_op jit(solution)/shard_map/slice | solution.py:334
  46.8 0.1 collective-permute-start.7
  46.9 0.0 collective-permute-done.1.refs_1_
  46.9 0.0 collective-permute-done.3.refs_3_
  46.9 0.0 collective-permute-done.5.refs_5_
  46.9 1.4 %collective-permute-done.7.refs_7_ = bf16[1,360,256]{2,1,0:T(8,128)(2,1)S(1)} collective-permute-done((bf16[1,360,256]{2,1,0:T(8,128)(2,1)S(1)}, bf16[1,360,256]{2,1,0:T(8,128)(2,1)S(1)}, u32[]{:S(2)}, u32[]{:S(2)}) %collective-permute-start.7) | collective-permute-done | bytes 184352 | tf_op jit(solution)/shard_map/ppermute | solution.py:334
  48.3 2.4 %shard_map.51.z_ref = bf16[360,2048]{1,0:T(8,128)(2,1)S(1)} custom-call(s32[8]{0:T(128)S(1)} %fusion.6.place_ref, bf16[2,360,256]{2,1,0:T(8,128)(2,1)S(1)} %get-tuple-element.17.refs_0_, bf16[1,360,256]{2,1,0:T(8,128)(2,1)S(1)} %collective-permute-done.1.refs_1_, bf16[2,360,256]{2,1,0:T(8,128)(2,1)} %collective-permute-done.2.refs_2_, ...), custom_call_target="tpu_custom_call" | custom-call | bytes 11796480 | tf_op jit(solution)/shard_map/pallas_call | solution.py:227
  50.6 5.0 %all-to-all-done.1.got_ref = f32[128,8,128]{2,1,0:T(8,128)S(1)} async-done(((f32[128,8,128]{2,1,0:T(8,128)}), f32[128,8,128]{2,1,0:T(8,128)S(1)}, u32[]{:S(2)}, u32[]{:S(2)}) %all-to-all-start.1) | async-done | bytes 524320 | tf_op jit(solution)/shard_map/all_to_all | solution.py:333
  55.7 13.3 %all_to_all.15 = f32[64,8,128]{2,1,0:T(8,128)S(1)} all-to-all(f32[64,8,128]{2,1,0:T(8,128)S(1)} %shard_map.52), channel_id=1, replica_groups={{0,1,2,3,4,5,6,7,8,9,10,11,12,13,14,15,32,33,34,35,36,37,38,39,40,41,42..., dimensions={0} | all-to-all | bytes 524288 | tf_op jit(solution)/shard_map/all_to_all | solution.py:342
  69.0 2.4 %collective-permute-start.8 = (f32[4,16,8,128]{3,2,1,0:T(8,128)S(1)}, f32[4,16,8,128]{3,2,1,0:T(8,128)S(1)}, u32[]{:S(2)}, u32[]{:S(2)}) collective-permute-start(f32[4,16,8,128]{3,2,1,0:T(8,128)S(1)} %bitcast.20), channel_id=1, source_target_pairs={{0,16},{16,0},{32,48},{48,32},{64,80},{80,64},{96,112},{112,96},{1... | collective-permute-start | bytes 786440 | tf_op jit(solution)/shard_map/ppermute | solution.py:344
  71.4 0.8 %shard_map.53.own_ref = f32[4,32,90]{2,1,0:T(8,128)S(1)} custom-call(f32[4,16,8,128]{3,2,1,0:T(8,128)S(1)} %bitcast.21, bf16[360,2048]{1,0:T(8,128)(2,1)S(1)} %shard_map.51.z_ref, f32[4,90]{1,0:T(4,128)S(1)} %convert_multiply_fusion.factor_ref), custom_call_target="tpu_custom_call" | custom-call | flops 47185920 | bytes 1736704 | tf_op jit(solution)/shard_map/pallas_call | solution.py:282
  72.2 0.4 collective-permute-done.8.pcs_ref
  72.5 1.5 %shard_map.54 = f32[4,64,90]{2,1,0:T(8,128)} custom-call(s32[1]{0:T(128)} %bitcast.core_ref, f32[4,16,8,128]{3,2,1,0:T(8,128)S(1)} %collective-permute-done.8.pcs_ref, bf16[360,2048]{1,0:T(8,128)(2,1)S(1)} %shard_map.51.z_ref, f32[4,90]{1,0:T(4,128)S(1)} %convert_multiply_fusion.factor_ref, f32[4,32,90]{2,1,0:T(8,128)S(1)} %shard_map.53.own_ref), custom_call_target="tpu_custom_call" | custom-call | flops 47185920 | bytes 1736704 | tf_op jit(solution)/shard_map/pallas_call | solution.py:285
  (8 shorter events, 0.1 us)
Async XLA Ops:
  2.5 5.8 %copy-start.4 = (s32[4,90]{1,0:T(4,128)S(1)}, s32[4,90]{1,0:T(4,128)}, u32[]{:S(2)}) copy-start(s32[4,90]{1,0:T(4,128)} %param.7) | copy-start | bytes 4324
  2.5 25.5 %all-to-all-start = ((bf16[8,360,256]{2,1,0:T(8,128)(2,1)}), bf16[8,360,256]{2,1,0:T(8,128)(2,1)S(1)}, u32[]{:S(2)}, u32[]{:S(2)}) async-start(bf16[8,360,256]{2,1,0:T(8,128)(2,1)} %bitcast.23), calls=%async_computation | async-start | bytes 2949120 | tf_op jit(solution)/shard_map/all_to_all | solution.py:314
  8.3 5.5 %collective-permute-start = (s32[4,90]{1,0:T(4,128)S(1)}, s32[4,90]{1,0:T(4,128)S(1)}, u32[]{:S(2)}, u32[]{:S(2)}) collective-permute-start(s32[4,90]{1,0:T(4,128)S(1)} %copy-done.4), channel_id=1, source_target_pairs={{0,16},{16,0},{32,48},{48,32},{64,80},{80,64},{96,112},{112,96},{1... | collective-permute-start | bytes 4328 | tf_op jit(solution)/shard_map/ppermute | solution.py:322
  8.4 1.4 %copy-start.2 = (bf16[32,90,256]{2,0,1:T(8,128)(2,1)S(1)}, bf16[32,90,256]{2,0,1:T(8,128)(2,1)}, u32[]{:S(2)}) copy-start(bf16[32,90,256]{2,0,1:T(8,128)(2,1)} %param.5) | copy-start | bytes 4423684
  11.7 1.0 %copy-start.3 = (f32[2048,64]{0,1:T(8,128)S(1)}, f32[2048,64]{0,1:T(8,128)}, u32[]{:S(2)}) copy-start(f32[2048,64]{0,1:T(8,128)} %param.6) | copy-start | bytes 1572868
  12.9 0.9 %copy-start = (bf16[192,2048]{1,0:T(8,128)(2,1)}, bf16[192,2048]{1,0:T(8,128)(2,1)S(1)}, u32[]{:S(2)}) copy-start(bf16[192,2048]{1,0:T(8,128)(2,1)S(1)} %shard_map.49.e_ref) | copy-start | bytes 2359300
  13.8 28.4 %collective-permute-start.2 = (bf16[2,360,256]{2,1,0:T(8,128)(2,1)}, bf16[2,360,256]{2,1,0:T(8,128)(2,1)}, u32[]{:S(2)}, u32[]{:S(2)}) collective-permute-start(bf16[2,360,256]{2,1,0:T(8,128)(2,1)} %get-tuple-element.12), channel_id=1, source_target_pairs={{0,32},{16,48},{32,64},{48,80},{64,96},{80,112},{96,0},{112,16},{1... | collective-permute-start | bytes 1105928 | tf_op jit(solution)/shard_map/ppermute | solution.py:325
  15.6 28.4 %collective-permute-start.4 = (bf16[2,360,256]{2,1,0:T(8,128)(2,1)}, bf16[2,360,256]{2,1,0:T(8,128)(2,1)}, u32[]{:S(2)}, u32[]{:S(2)}) collective-permute-start(bf16[2,360,256]{2,1,0:T(8,128)(2,1)} %get-tuple-element.13), channel_id=1, source_target_pairs={{0,64},{16,80},{32,96},{48,112},{64,0},{80,16},{96,32},{112,48},{1... | collective-permute-start | bytes 1105928 | tf_op jit(solution)/shard_map/ppermute | solution.py:325
  18.0 27.9 %collective-permute-start.6 = (bf16[2,360,256]{2,1,0:T(8,128)(2,1)}, bf16[2,360,256]{2,1,0:T(8,128)(2,1)}, u32[]{:S(2)}, u32[]{:S(2)}) collective-permute-start(bf16[2,360,256]{2,1,0:T(8,128)(2,1)} %get-tuple-element.14), channel_id=1, source_target_pairs={{0,96},{16,112},{32,0},{48,16},{64,32},{80,48},{96,64},{112,80},{1... | collective-permute-start | bytes 1105928 | tf_op jit(solution)/shard_map/ppermute | solution.py:325
  28.0 1.4 %copy-start.1 = (bf16[192,2048]{1,0:T(8,128)(2,1)S(1)}, bf16[192,2048]{1,0:T(8,128)(2,1)}, u32[]{:S(2)}) copy-start(bf16[192,2048]{1,0:T(8,128)(2,1)} %copy-done) | copy-start | bytes 2359300
  31.5 24.1 %all-to-all-start.1 = ((f32[128,8,128]{2,1,0:T(8,128)}), f32[128,8,128]{2,1,0:T(8,128)S(1)}, u32[]{:S(2)}, u32[]{:S(2)}) async-start(f32[128,8,128]{2,1,0:T(8,128)} %bitcast.12), calls=%async_computation.1 | async-start | bytes 1048576 | tf_op jit(solution)/shard_map/all_to_all | solution.py:333
  41.1 5.8 %collective-permute-start.1 = (bf16[1,360,256]{2,1,0:T(8,128)(2,1)S(1)}, bf16[1,360,256]{2,1,0:T(8,128)(2,1)S(1)}, u32[]{:S(2)}, u32[]{:S(2)}) collective-permute-start(bf16[1,360,256]{2,1,0:T(8,128)(2,1)S(1)} %slice.37), channel_id=1, source_target_pairs={{0,16},{16,0},{32,48},{48,32},{64,80},{80,64},{96,112},{112,96},{1... | collective-permute-start | bytes 552968 | tf_op jit(solution)/shard_map/ppermute | solution.py:334
  43.2 3.7 %collective-permute-start.3 = (bf16[1,360,256]{2,1,0:T(8,128)(2,1)S(1)}, bf16[1,360,256]{2,1,0:T(8,128)(2,1)S(1)}, u32[]{:S(2)}, u32[]{:S(2)}) collective-permute-start(bf16[1,360,256]{2,1,0:T(8,128)(2,1)S(1)} %slice.38), channel_id=1, source_target_pairs={{0,16},{16,0},{32,48},{48,32},{64,80},{80,64},{96,112},{112,96},{1... | collective-permute-start | bytes 552968 | tf_op jit(solution)/shard_map/ppermute | solution.py:334
  44.9 2.0 %collective-permute-start.5 = (bf16[1,360,256]{2,1,0:T(8,128)(2,1)S(1)}, bf16[1,360,256]{2,1,0:T(8,128)(2,1)S(1)}, u32[]{:S(2)}, u32[]{:S(2)}) collective-permute-start(bf16[1,360,256]{2,1,0:T(8,128)(2,1)S(1)} %slice.39), channel_id=1, source_target_pairs={{0,16},{16,0},{32,48},{48,32},{64,80},{80,64},{96,112},{112,96},{1... | collective-permute-start | bytes 552968 | tf_op jit(solution)/shard_map/ppermute | solution.py:334
  46.8 1.5 %collective-permute-start.7 = (bf16[1,360,256]{2,1,0:T(8,128)(2,1)S(1)}, bf16[1,360,256]{2,1,0:T(8,128)(2,1)S(1)}, u32[]{:S(2)}, u32[]{:S(2)}) collective-permute-start(bf16[1,360,256]{2,1,0:T(8,128)(2,1)S(1)} %slice.40), channel_id=1, source_target_pairs={{0,16},{16,0},{32,48},{48,32},{64,80},{80,64},{96,112},{112,96},{1... | collective-permute-start | bytes 552968 | tf_op jit(solution)/shard_map/ppermute | solution.py:334
  69.0 3.5 %collective-permute-start.8 = (f32[4,16,8,128]{3,2,1,0:T(8,128)S(1)}, f32[4,16,8,128]{3,2,1,0:T(8,128)S(1)}, u32[]{:S(2)}, u32[]{:S(2)}) collective-permute-start(f32[4,16,8,128]{3,2,1,0:T(8,128)S(1)} %bitcast.20), channel_id=1, source_target_pairs={{0,16},{16,0},{32,48},{48,32},{64,80},{80,64},{96,112},{112,96},{1... | collective-permute-start | bytes 786440 | tf_op jit(solution)/shard_map/ppermute | solution.py:344

commit v12 on v11

--- a/solution.py
+++ b/solution.py
@@ -113,39 +113,61 @@
             z_ref[rows, b * width : (b + 1) * width] = ((centered * scale) * weight).astype(BF16)
 
 
-def sums_kernel(z_ref, e_ref, out_ref):
-    modes = out_ref.shape[0]
-    turned = lax.dot_general(e_ref[...], z_ref[...], NT, preferred_element_type=F32)
-    turned = turned[:modes] + (turned[modes : 2 * modes] + turned[2 * modes :])
-    stacked = jnp.concatenate(three_terms(turned), axis=0)
-    hours = out_ref.shape[1]
+def column_sums(stacked, z_ref, out_ref):
+    modes, hours = out_ref.shape
     for start, size in row_chunks(hours, 512):
         columns = slice(start, start + size)
         sums = lax.dot_general(stacked, z_ref[:, columns], NN, preferred_element_type=F32)
         out_ref[:, columns] = sums[:modes] + (sums[modes : 2 * modes] + sums[2 * modes :])
 
 
-def temp_sums(temp, split, weight):
+def other_kernel(core_ref, z_ref, e_ref, out_ref, own_ref):
+    modes = 2 * out_ref.shape[0]
+    turned = lax.dot_general(e_ref[...], z_ref[...], NT, preferred_element_type=F32)
+    turned = turned[:modes] + (turned[modes : 2 * modes] + turned[2 * modes :])
+    even = jnp.concatenate([turned[n : n + 8] for n in range(0, modes, 16)], axis=0)
+    odd = jnp.concatenate([turned[n : n + 8] for n in range(8, modes, 16)], axis=0)
+    first = core_ref[0] == 0
+    own_ref[...] = jnp.concatenate(three_terms(jnp.where(first, even, odd)), axis=0)
+    column_sums(jnp.concatenate(three_terms(jnp.where(first, odd, even)), axis=0), z_ref, out_ref)
+
+
+def own_sums_kernel(stacked_ref, z_ref, out_ref):
+    column_sums(stacked_ref[...], z_ref, out_ref)
+
+
+def temp_sums(core, temp, split, weight):
     blocks, cells, width = temp.shape
-    modes = split.shape[0] // 3
+    modes, hours = split.shape[0] // 6, blocks * width
     scores = pl.pallas_call(
         scores_kernel,
-        out_shape=jax.ShapeDtypeStruct((cells, blocks * width), BF16),
+        out_shape=jax.ShapeDtypeStruct((cells, hours), BF16),
         compiler_params=params(),
         cost_estimate=pl.CostEstimate(
             flops=16 * temp.size, bytes_accessed=4 * temp.size, transcendentals=cells
         ),
     )(temp, weight)
-    return pl.pallas_call(
-        sums_kernel,
-        out_shape=jax.ShapeDtypeStruct((modes, blocks * width), F32),
-        compiler_params=params(),
-        cost_estimate=pl.CostEstimate(
-            flops=12 * cells * modes * blocks * width,
-            bytes_accessed=2 * temp.size + 2 * split.size,
-            transcendentals=0,
+    cost = pl.CostEstimate(
+        flops=6 * cells * modes * hours, bytes_accessed=2 * temp.size, transcendentals=0
+    )
+    vmem = pl.BlockSpec(memory_space=pltpu.VMEM)
+    other, stacked = pl.pallas_call(
+        other_kernel,
+        in_specs=[pl.BlockSpec(memory_space=pltpu.SMEM), vmem, vmem],
+        out_shape=(
+            jax.ShapeDtypeStruct((modes, hours), F32),
+            jax.ShapeDtypeStruct((3 * modes, cells), BF16),
         ),
-    )(scores, split)
+        compiler_params=params(),
+        cost_estimate=cost,
+    )(core.reshape(1), scores, split)
+    own = pl.pallas_call(
+        own_sums_kernel,
+        out_shape=jax.ShapeDtypeStruct((modes, hours), F32),
+        compiler_params=params(),
+        cost_estimate=cost,
+    )(stacked, scores)
+    return own, other
 
 
 def sum_kernel(got_ref, out_ref):
@@ -327,18 +349,18 @@
     scaling = root[:, None] * pair.reshape(8, lons).astype(F32)
     weight = lax.dynamic_slice(scaling.T, (core * half, 0), (half, 8)).reshape(1, 8 * half)
 
-    partial_t = temp_sums(temp, split_columns(gram_eigenvector_columns.T), weight)
-    blocks = partial_t.reshape(modes // 8, 8, hours // 128, 128)
-    blocks = blocks.transpose(0, 2, 1, 3).reshape(-1, 8, 128)
-    got = lax.all_to_all(blocks, BOTH, 0, 0)
+    own_sums, other_sums = temp_sums(core, temp, split_columns(gram_eigenvector_columns.T), weight)
+    partial_t = own_sums + lax.ppermute(other_sums, "tm", to_core)
+    blocks = partial_t.reshape(chips, 8, others, 128).transpose(0, 2, 1, 3).reshape(-1, 8, 128)
+    kinds = [
+        [t * others + n for t in range(kind, members, 2) for n in range(others)] for kind in range(2)
+    ]
+    got = lax.all_to_all(blocks, BOTH, 0, 0, axis_index_groups=kinds)
     traded = [lax.ppermute(blocks[1:2], "tm", to_core) for blocks in [own, *arrived]]
     pieces = [piece for both in zip([own, *arrived], traded) for piece in both]
     places = 2 * lax.rem(chip + chips - lax.div(band, 2), chips) + lax.rem(band + core, 2)
     scores = hum_scores(places, pieces)
     got, scores = lax.optimization_barrier((got, scores))
-    kinds = [
-        [t * others + n for t in range(kind, members, 2) for n in range(others)] for kind in range(2)
-    ]
     pcs = lax.all_to_all(sum_for_all(got, chips * others), BOTH, 0, 0, axis_index_groups=kinds)
     pcs = pcs.reshape(chips, others, 8, 128)
     pcs_other = lax.ppermute(pcs, "tm", to_core)

time: 74.5 us -> 75.8 us (1.017)
  blocking collectives: 13.3 us -> 18.5 us
  waiting for transfers between devices: 16 us -> 12.2 us
    all_to_all x1, blocking collectives: 13.3 us -> 18.5 us  [per_device(): lax.all_to_all(sum_for_all(got, chips * others), BOTH, 0, 0, axis_index_g...]
    all_to_all x1, waiting for transfers between devices: 5.05 us -> 1.24 us  [per_device(): got = lax.all_to_all(blocks, BOTH, 0, 0, axis_index_groups=kinds)]
    ppermute x0 -> x1, starting transfers between devices: none -> 1.43 us  [per_device(): partial_t = own_sums + lax.ppermute(other_sums, 'tm', to_core)]
    ppermute x1, starting transfers between devices: 2.37 us -> 1.49 us  [per_device(): pcs_other = lax.ppermute(pcs, 'tm', to_core)]
    ppermute x4, starting transfers between devices: 2.3 us -> 1.5 us  [per_device(): lax.ppermute(blocks[1:2], 'tm', to_core)]
    pallas_call x2 -> x3, Pallas kernels: 3.5 us -> 2.93 us  [the longest x1 1.35 us: temp_sums(): pl.pallas_call(scores_kernel, out_shape=jax.ShapeDtypeStruct((cells, hour...]
  transfers between devices with their start and end apart: 11 -> 12, of which waited for: 5 -> 5; matrix products, arithmetic and copies ran while one was open for 6% -> 7% of each run, Pallas kernels for 10% -> 9%
where the time goes in v12:
time: 75.8 us; the launch traced here: 75.3 us
  starting transfers between devices  24.9 us (33%)
  blocking collectives  18.5 us (24%)
  waiting for transfers between devices  12.2 us (16%)
  Pallas kernels  11.1 us (15%)
  local copies, waits for them, and re-layouts  7.39 us (10%)
  other arithmetic  0.89 us (1%)
    all_to_all x1, blocking collectives, per_device(): lax.all_to_all(sum_for_all(got, chips * others), BOTH, 0, 0, axis_index_g...  18.5 us
    all_to_all x1, starting transfers between devices, per_device(): got = lax.all_to_all(blocks, BOTH, 0, 0, axis_index_groups=kinds)  9.33 us
    all_to_all x1, waiting for transfers between devices, per_device(): temp = lax.all_to_all(temp, 'tm', 0, 0)  8.54 us
    all_to_all x1, starting transfers between devices, per_device(): temp = lax.all_to_all(temp, 'tm', 0, 0)  5.81 us
    ppermute x3, starting transfers between devices, per_device(): lax.ppermute(sent[d - 1], 'tm', to_chip[d])  5.3 us
    unnamed x10, local copies, waits for them, and re-layouts  3.29 us
    slice x4, local copies, waits for them, and re-layouts, per_device(): blocks[1:2]  2.82 us
    pallas_call x1, Pallas kernels, pack_octets(): pl.pallas_call(pack_kernel, in_specs=[pl.BlockSpec(memory_space=pl.ANY)],...  2.51 us
  transfers between devices with their start and end apart: 12, of which 5 were waited for; matrix products, arithmetic and copies ran while one was open for 7% of the time, Pallas kernels for 9%

profile of v12, /device:TPU:1, one launch (start us, length us, event | category | flops | bytes accessed | tf_op | source)
XLA Modules:
  0.0 75.3 jit_solution(2162517062868967361)
XLA Ops:
  0.0 2.5 %shard_map.46 = bf16[4,2,45,8,256]{4,3,2,1,0:T(8,128)(2,1)} custom-call(bf16[2,45,4,8,256]{4,3,2,1,0:T(8,128)(2,1)} %bitcast.24), custom_call_target="tpu_custom_call" | custom-call | bytes 2949120 | tf_op jit(solution)/shard_map/pallas_call | solution.py:65
  2.5 0.0 copy-start.4
  2.5 5.8 %all-to-all-start = ((bf16[8,360,256]{2,1,0:T(8,128)(2,1)}), bf16[8,360,256]{2,1,0:T(8,128)(2,1)S(1)}, u32[]{:S(2)}, u32[]{:S(2)}) async-start(bf16[8,360,256]{2,1,0:T(8,128)(2,1)} %bitcast.23), calls=%async_computation | async-start | bytes 2949120 | tf_op jit(solution)/shard_map/all_to_all | solution.py:336
  8.3 0.0 copy-done.4
  8.3 0.1 collective-permute-start
  8.4 0.0 copy-start.2
  8.5 1.4 %copy-done.2 = bf16[32,90,256]{2,0,1:T(8,128)(2,1)S(1)} copy-done((bf16[32,90,256]{2,0,1:T(8,128)(2,1)S(1)}, bf16[32,90,256]{2,0,1:T(8,128)(2,1)}, u32[]{:S(2)}) %copy-start.2) | copy-done | bytes 1474584
  9.8 0.9 %shard_map.47 = bf16[8,360,256]{2,1,0:T(8,128)(2,1)S(1)} custom-call(s32[8]{0:T(128)S(1)} %fusion.2.place_ref, bf16[90,32,256]{2,1,0:T(8,128)(2,1)S(1)} %bitcast.19), custom_call_target="tpu_custom_call" | custom-call | bytes 2949120 | tf_op jit(solution)/shard_map/pallas_call | solution.py:215
  10.7 1.0 %fusion.7 = (bf16[2,360,256]{2,1,0:T(8,128)(2,1)S(1)}, bf16[2,360,256]{2,1,0:T(8,128)(2,1)}, bf16[2,360,256]{2,1,0:T(8,128)(2,1)}, bf16[2,360,256]{2,1,0:T(8,128)(2,1)}) fusion(bf16[8,360,256]{2,1,0:T(8,128)(2,1)S(1)} %shard_map.47), kind=kLoop, calls=%fused_computation.19 | loop fusion | bytes 2949120 | tf_op jit(solution)/shard_map/slice | solution.py:342
  11.8 0.0 copy-start.3
  11.8 1.0 %copy-done.3 = f32[2048,64]{0,1:T(8,128)S(1)} copy-done((f32[2048,64]{0,1:T(8,128)S(1)}, f32[2048,64]{0,1:T(8,128)}, u32[]{:S(2)}) %copy-start.3) | copy-done | bytes 524312
  12.8 0.2 shard_map.49.e_ref
  13.0 0.0 copy-start
  13.0 0.9 %copy-done = bf16[192,2048]{1,0:T(8,128)(2,1)} copy-done((bf16[192,2048]{1,0:T(8,128)(2,1)}, bf16[192,2048]{1,0:T(8,128)(2,1)S(1)}, u32[]{:S(2)}) %copy-start) | copy-done | bytes 786456
  13.9 0.0 collective-permute-done
  13.9 1.7 %collective-permute-start.3 = (bf16[2,360,256]{2,1,0:T(8,128)(2,1)}, bf16[2,360,256]{2,1,0:T(8,128)(2,1)}, u32[]{:S(2)}, u32[]{:S(2)}) collective-permute-start(bf16[2,360,256]{2,1,0:T(8,128)(2,1)} %get-tuple-element.16), channel_id=1, source_target_pairs={{0,32},{16,48},{32,64},{48,80},{64,96},{80,112},{96,0},{112,16},{1... | collective-permute-start | bytes 1105928 | tf_op jit(solution)/shard_map/ppermute | solution.py:347
  15.6 2.4 %collective-permute-start.5 = (bf16[2,360,256]{2,1,0:T(8,128)(2,1)}, bf16[2,360,256]{2,1,0:T(8,128)(2,1)}, u32[]{:S(2)}, u32[]{:S(2)}) collective-permute-start(bf16[2,360,256]{2,1,0:T(8,128)(2,1)} %get-tuple-element.17), channel_id=1, source_target_pairs={{0,64},{16,80},{32,96},{48,112},{64,0},{80,16},{96,32},{112,48},{1... | collective-permute-start | bytes 1105928 | tf_op jit(solution)/shard_map/ppermute | solution.py:347
  18.0 1.2 %collective-permute-start.7 = (bf16[2,360,256]{2,1,0:T(8,128)(2,1)}, bf16[2,360,256]{2,1,0:T(8,128)(2,1)}, u32[]{:S(2)}, u32[]{:S(2)}) collective-permute-start(bf16[2,360,256]{2,1,0:T(8,128)(2,1)} %get-tuple-element.18), channel_id=1, source_target_pairs={{0,96},{16,112},{32,0},{48,16},{64,32},{80,48},{96,64},{112,80},{1... | collective-permute-start | bytes 1105928 | tf_op jit(solution)/shard_map/ppermute | solution.py:347
  19.2 0.1 broadcast_multiply_fusion
  19.2 0.1 dynamic-slice_bitcast_fusion
  19.3 0.1 copy.7
  19.4 0.1 reshape.38.w_ref
  19.5 8.5 %all-to-all-done.t_ref = bf16[8,360,256]{2,1,0:T(8,128)(2,1)S(1)} async-done(((bf16[8,360,256]{2,1,0:T(8,128)(2,1)}), bf16[8,360,256]{2,1,0:T(8,128)(2,1)S(1)}, u32[]{:S(2)}, u32[]{:S(2)}) %all-to-all-start) | async-done | bytes 1474592 | tf_op jit(solution)/shard_map/all_to_all | solution.py:336
  28.1 0.0 copy-start.1
  28.1 1.3 %shard_map.48.z_ref = bf16[360,2048]{1,0:T(8,128)(2,1)S(1)} custom-call(bf16[8,360,256]{2,1,0:T(8,128)(2,1)S(1)} %all-to-all-done.t_ref, f32[1,360]{1,0:T(1,128)S(1)} %reshape.38.w_ref), custom_call_target="tpu_custom_call" | custom-call | flops 11796480 | bytes 2949120 | tf_op jit(solution)/shard_map/pallas_call | solution.py:142
  29.4 0.0 copy-done.1
  29.4 1.2 %shard_map.50 = (f32[32,2048]{1,0:T(8,128)S(1)}, bf16[96,360]{1,0:T(8,128)(2,1)S(1)}) custom-call(s32[1]{0:T(128)} %bitcast.core_ref, bf16[360,2048]{1,0:T(8,128)(2,1)S(1)} %shard_map.48.z_ref, bf16[192,2048]{1,0:T(8,128)(2,1)S(1)} %copy-done.1), custom_call_target="tpu_custom_call" | custom-call | flops 141557760 | bytes 1474560 | tf_op jit(solution)/shard_map/pallas_call | solution.py:154
  30.6 1.4 %collective-permute-start.1 = (f32[32,2048]{1,0:T(8,128)S(1)}, f32[32,2048]{1,0:T(8,128)S(1)}, u32[]{:S(2)}, u32[]{:S(2)}) collective-permute-start(f32[32,2048]{1,0:T(8,128)S(1)} %get-tuple-element.15), channel_id=1, source_target_pairs={{0,16},{16,0},{32,48},{48,32},{64,80},{80,64},{96,112},{112,96},{1... | collective-permute-start | bytes 786440 | tf_op jit(solution)/shard_map/ppermute | solution.py:353
  32.0 0.4 shard_map.51
  32.4 0.7 collective-permute-done.1
  33.2 0.7 add.57
  33.9 9.3 %all-to-all-start.1 = ((f32[64,8,128]{2,1,0:T(8,128)}), f32[64,8,128]{2,1,0:T(8,128)S(1)}, u32[]{:S(2)}, u32[]{:S(2)}) async-start(f32[64,8,128]{2,1,0:T(8,128)} %bitcast.12), calls=%async_computation.1 | async-start | bytes 524288 | tf_op jit(solution)/shard_map/all_to_all | solution.py:358
  43.3 0.7 collective-permute-start.2
  44.0 0.0 collective-permute-done.3.refs_2_
  44.0 0.9 %slice.38 = bf16[1,360,256]{2,1,0:T(8,128)(2,1)S(1)} slice(bf16[2,360,256]{2,1,0:T(8,128)(2,1)} %collective-permute-done.3.refs_2_), slice={[1:2], [0:360], [0:256]} | slice | bytes 368640 | tf_op jit(solution)/shard_map/slice | solution.py:359
  44.9 0.1 collective-permute-start.4
  45.0 0.0 collective-permute-done.5.refs_4_
  45.0 0.9 %slice.39 = bf16[1,360,256]{2,1,0:T(8,128)(2,1)S(1)} slice(bf16[2,360,256]{2,1,0:T(8,128)(2,1)} %collective-permute-done.5.refs_4_), slice={[1:2], [0:360], [0:256]} | slice | bytes 368640 | tf_op jit(solution)/shard_map/slice | solution.py:359
  46.0 0.6 collective-permute-start.6
  46.6 0.0 collective-permute-done.7.refs_6_
  46.6 0.9 %slice.40 = bf16[1,360,256]{2,1,0:T(8,128)(2,1)S(1)} slice(bf16[2,360,256]{2,1,0:T(8,128)(2,1)} %collective-permute-done.7.refs_6_), slice={[1:2], [0:360], [0:256]} | slice | bytes 368640 | tf_op jit(solution)/shard_map/slice | solution.py:359
  47.5 0.1 collective-permute-start.8
  47.6 0.0 collective-permute-done.2.refs_1_
  47.6 0.0 collective-permute-done.4.refs_3_
  47.6 0.0 collective-permute-done.6.refs_5_
  47.6 1.4 %collective-permute-done.8.refs_7_ = bf16[1,360,256]{2,1,0:T(8,128)(2,1)S(1)} collective-permute-done((bf16[1,360,256]{2,1,0:T(8,128)(2,1)S(1)}, bf16[1,360,256]{2,1,0:T(8,128)(2,1)S(1)}, u32[]{:S(2)}, u32[]{:S(2)}) %collective-permute-start.8) | collective-permute-done | bytes 184352 | tf_op jit(solution)/shard_map/ppermute | solution.py:359
  49.0 2.3 %shard_map.52.z_ref = bf16[360,2048]{1,0:T(8,128)(2,1)S(1)} custom-call(s32[8]{0:T(128)S(1)} %fusion.6.place_ref, bf16[2,360,256]{2,1,0:T(8,128)(2,1)S(1)} %get-tuple-element.21.refs_0_, bf16[1,360,256]{2,1,0:T(8,128)(2,1)S(1)} %collective-permute-done.2.refs_1_, bf16[2,360,256]{2,1,0:T(8,128)(2,1)} %collective-permute-done.3.refs_2_, ...), custom_call_target="tpu_custom_call" | custom-call | bytes 11796480 | tf_op jit(solution)/shard_map/pallas_call | solution.py:249
  51.4 1.2 %all-to-all-done.1.got_ref = f32[64,8,128]{2,1,0:T(8,128)S(1)} async-done(((f32[64,8,128]{2,1,0:T(8,128)}), f32[64,8,128]{2,1,0:T(8,128)S(1)}, u32[]{:S(2)}, u32[]{:S(2)}) %all-to-all-start.1) | async-done | bytes 262176 | tf_op jit(solution)/shard_map/all_to_all | solution.py:358
  52.6 18.5 %all_to_all.15 = f32[64,8,128]{2,1,0:T(8,128)S(1)} all-to-all(f32[64,8,128]{2,1,0:T(8,128)S(1)} %shard_map.53), channel_id=1, replica_groups={{0,1,2,3,4,5,6,7,8,9,10,11,12,13,14,15,32,33,34,35,36,37,38,39,40,41,42..., dimensions={0} | all-to-all | bytes 524288 | tf_op jit(solution)/shard_map/all_to_all | solution.py:364
  71.1 1.5 %collective-permute-start.9 = (f32[4,16,8,128]{3,2,1,0:T(8,128)S(1)}, f32[4,16,8,128]{3,2,1,0:T(8,128)S(1)}, u32[]{:S(2)}, u32[]{:S(2)}) collective-permute-start(f32[4,16,8,128]{3,2,1,0:T(8,128)S(1)} %bitcast.20), channel_id=1, source_target_pairs={{0,16},{16,0},{32,48},{48,32},{64,80},{80,64},{96,112},{112,96},{1... | collective-permute-start | bytes 786440 | tf_op jit(solution)/shard_map/ppermute | solution.py:366
  72.6 0.8 %shard_map.54.own_ref = f32[4,32,90]{2,1,0:T(8,128)S(1)} custom-call(f32[4,16,8,128]{3,2,1,0:T(8,128)S(1)} %bitcast.21, bf16[360,2048]{1,0:T(8,128)(2,1)S(1)} %shard_map.52.z_ref, f32[4,90]{1,0:T(4,128)S(1)} %convert_multiply_fusion.factor_ref), custom_call_target="tpu_custom_call" | custom-call | flops 47185920 | bytes 1736704 | tf_op jit(solution)/shard_map/pallas_call | solution.py:304
  73.5 0.3 collective-permute-done.9.pcs_ref
  73.8 1.5 %shard_map.55 = f32[4,64,90]{2,1,0:T(8,128)} custom-call(s32[1]{0:T(128)} %bitcast.core_ref, f32[4,16,8,128]{3,2,1,0:T(8,128)S(1)} %collective-permute-done.9.pcs_ref, bf16[360,2048]{1,0:T(8,128)(2,1)S(1)} %shard_map.52.z_ref, f32[4,90]{1,0:T(4,128)S(1)} %convert_multiply_fusion.factor_ref, f32[4,32,90]{2,1,0:T(8,128)S(1)} %shard_map.54.own_ref), custom_call_target="tpu_custom_call" | custom-call | flops 47185920 | bytes 1736704 | tf_op jit(solution)/shard_map/pallas_call | solution.py:307
  (8 shorter events, 0.1 us)
Async XLA Ops:
  2.5 5.8 %copy-start.4 = (s32[4,90]{1,0:T(4,128)S(1)}, s32[4,90]{1,0:T(4,128)}, u32[]{:S(2)}) copy-start(s32[4,90]{1,0:T(4,128)} %param.7) | copy-start | bytes 4324
  2.5 25.5 %all-to-all-start = ((bf16[8,360,256]{2,1,0:T(8,128)(2,1)}), bf16[8,360,256]{2,1,0:T(8,128)(2,1)S(1)}, u32[]{:S(2)}, u32[]{:S(2)}) async-start(bf16[8,360,256]{2,1,0:T(8,128)(2,1)} %bitcast.23), calls=%async_computation | async-start | bytes 2949120 | tf_op jit(solution)/shard_map/all_to_all | solution.py:336
  8.3 5.5 %collective-permute-start = (s32[4,90]{1,0:T(4,128)S(1)}, s32[4,90]{1,0:T(4,128)S(1)}, u32[]{:S(2)}, u32[]{:S(2)}) collective-permute-start(s32[4,90]{1,0:T(4,128)S(1)} %copy-done.4), channel_id=1, source_target_pairs={{0,16},{16,0},{32,48},{48,32},{64,80},{80,64},{96,112},{112,96},{1... | collective-permute-start | bytes 4328 | tf_op jit(solution)/shard_map/ppermute | solution.py:344
  8.4 1.4 %copy-start.2 = (bf16[32,90,256]{2,0,1:T(8,128)(2,1)S(1)}, bf16[32,90,256]{2,0,1:T(8,128)(2,1)}, u32[]{:S(2)}) copy-start(bf16[32,90,256]{2,0,1:T(8,128)(2,1)} %param.5) | copy-start | bytes 4423684
  11.8 1.0 %copy-start.3 = (f32[2048,64]{0,1:T(8,128)S(1)}, f32[2048,64]{0,1:T(8,128)}, u32[]{:S(2)}) copy-start(f32[2048,64]{0,1:T(8,128)} %param.6) | copy-start | bytes 1572868
  13.0 0.9 %copy-start = (bf16[192,2048]{1,0:T(8,128)(2,1)}, bf16[192,2048]{1,0:T(8,128)(2,1)S(1)}, u32[]{:S(2)}) copy-start(bf16[192,2048]{1,0:T(8,128)(2,1)S(1)} %shard_map.49.e_ref) | copy-start | bytes 2359300
  13.9 30.1 %collective-permute-start.3 = (bf16[2,360,256]{2,1,0:T(8,128)(2,1)}, bf16[2,360,256]{2,1,0:T(8,128)(2,1)}, u32[]{:S(2)}, u32[]{:S(2)}) collective-permute-start(bf16[2,360,256]{2,1,0:T(8,128)(2,1)} %get-tuple-element.16), channel_id=1, source_target_pairs={{0,32},{16,48},{32,64},{48,80},{64,96},{80,112},{96,0},{112,16},{1... | collective-permute-start | bytes 1105928 | tf_op jit(solution)/shard_map/ppermute | solution.py:347
  15.6 29.5 %collective-permute-start.5 = (bf16[2,360,256]{2,1,0:T(8,128)(2,1)}, bf16[2,360,256]{2,1,0:T(8,128)(2,1)}, u32[]{:S(2)}, u32[]{:S(2)}) collective-permute-start(bf16[2,360,256]{2,1,0:T(8,128)(2,1)} %get-tuple-element.17), channel_id=1, source_target_pairs={{0,64},{16,80},{32,96},{48,112},{64,0},{80,16},{96,32},{112,48},{1... | collective-permute-start | bytes 1105928 | tf_op jit(solution)/shard_map/ppermute | solution.py:347
  18.0 28.6 %collective-permute-start.7 = (bf16[2,360,256]{2,1,0:T(8,128)(2,1)}, bf16[2,360,256]{2,1,0:T(8,128)(2,1)}, u32[]{:S(2)}, u32[]{:S(2)}) collective-permute-start(bf16[2,360,256]{2,1,0:T(8,128)(2,1)} %get-tuple-element.18), channel_id=1, source_target_pairs={{0,96},{16,112},{32,0},{48,16},{64,32},{80,48},{96,64},{112,80},{1... | collective-permute-start | bytes 1105928 | tf_op jit(solution)/shard_map/ppermute | solution.py:347
  28.1 1.4 %copy-start.1 = (bf16[192,2048]{1,0:T(8,128)(2,1)S(1)}, bf16[192,2048]{1,0:T(8,128)(2,1)}, u32[]{:S(2)}) copy-start(bf16[192,2048]{1,0:T(8,128)(2,1)} %copy-done) | copy-start | bytes 2359300
  30.6 2.6 %collective-permute-start.1 = (f32[32,2048]{1,0:T(8,128)S(1)}, f32[32,2048]{1,0:T(8,128)S(1)}, u32[]{:S(2)}, u32[]{:S(2)}) collective-permute-start(f32[32,2048]{1,0:T(8,128)S(1)} %get-tuple-element.15), channel_id=1, source_target_pairs={{0,16},{16,0},{32,48},{48,32},{64,80},{80,64},{96,112},{112,96},{1... | collective-permute-start | bytes 786440 | tf_op jit(solution)/shard_map/ppermute | solution.py:353
  33.9 18.7 %all-to-all-start.1 = ((f32[64,8,128]{2,1,0:T(8,128)}), f32[64,8,128]{2,1,0:T(8,128)S(1)}, u32[]{:S(2)}, u32[]{:S(2)}) async-start(f32[64,8,128]{2,1,0:T(8,128)} %bitcast.12), calls=%async_computation.1 | async-start | bytes 524288 | tf_op jit(solution)/shard_map/all_to_all | solution.py:358
  43.3 4.3 %collective-permute-start.2 = (bf16[1,360,256]{2,1,0:T(8,128)(2,1)S(1)}, bf16[1,360,256]{2,1,0:T(8,128)(2,1)S(1)}, u32[]{:S(2)}, u32[]{:S(2)}) collective-permute-start(bf16[1,360,256]{2,1,0:T(8,128)(2,1)S(1)} %slice.37), channel_id=1, source_target_pairs={{0,16},{16,0},{32,48},{48,32},{64,80},{80,64},{96,112},{112,96},{1... | collective-permute-start | bytes 552968 | tf_op jit(solution)/shard_map/ppermute | solution.py:359
  44.9 2.7 %collective-permute-start.4 = (bf16[1,360,256]{2,1,0:T(8,128)(2,1)S(1)}, bf16[1,360,256]{2,1,0:T(8,128)(2,1)S(1)}, u32[]{:S(2)}, u32[]{:S(2)}) collective-permute-start(bf16[1,360,256]{2,1,0:T(8,128)(2,1)S(1)} %slice.38), channel_id=1, source_target_pairs={{0,16},{16,0},{32,48},{48,32},{64,80},{80,64},{96,112},{112,96},{1... | collective-permute-start | bytes 552968 | tf_op jit(solution)/shard_map/ppermute | solution.py:359
  46.0 1.6 %collective-permute-start.6 = (bf16[1,360,256]{2,1,0:T(8,128)(2,1)S(1)}, bf16[1,360,256]{2,1,0:T(8,128)(2,1)S(1)}, u32[]{:S(2)}, u32[]{:S(2)}) collective-permute-start(bf16[1,360,256]{2,1,0:T(8,128)(2,1)S(1)} %slice.39), channel_id=1, source_target_pairs={{0,16},{16,0},{32,48},{48,32},{64,80},{80,64},{96,112},{112,96},{1... | collective-permute-start | bytes 552968 | tf_op jit(solution)/shard_map/ppermute | solution.py:359
  47.5 1.5 %collective-permute-start.8 = (bf16[1,360,256]{2,1,0:T(8,128)(2,1)S(1)}, bf16[1,360,256]{2,1,0:T(8,128)(2,1)S(1)}, u32[]{:S(2)}, u32[]{:S(2)}) collective-permute-start(bf16[1,360,256]{2,1,0:T(8,128)(2,1)S(1)} %slice.40), channel_id=1, source_target_pairs={{0,16},{16,0},{32,48},{48,32},{64,80},{80,64},{96,112},{112,96},{1... | collective-permute-start | bytes 552968 | tf_op jit(solution)/shard_map/ppermute | solution.py:359
  71.1 2.6 %collective-permute-start.9 = (f32[4,16,8,128]{3,2,1,0:T(8,128)S(1)}, f32[4,16,8,128]{3,2,1,0:T(8,128)S(1)}, u32[]{:S(2)}, u32[]{:S(2)}) collective-permute-start(f32[4,16,8,128]{3,2,1,0:T(8,128)S(1)} %bitcast.20), channel_id=1, source_target_pairs={{0,16},{16,0},{32,48},{48,32},{64,80},{80,64},{96,112},{112,96},{1... | collective-permute-start | bytes 786440 | tf_op jit(solution)/shard_map/ppermute | solution.py:366
